TPU v7x, 32 devices: a whole 2x2x4 slice. The times are simulated.
32 devices in a mesh: dp: 8 (over z, x), tensor: 4 (over y, core).
Axes of the slice: x: 2, y: 2, z: 4, core: 2. Of those that a mesh axis runs over, the one named last changes fastest.
Arguments:
- tokens: bfloat16 [8, 1024, 1024], P('dp'), may hold values from -6 to 6
- cotangent: bfloat16 [8, 1024, 1024], P('dp'), may hold values from -6 to 6
- seg_lengths: int32 [8, 8], P('dp'), may hold values from 1 to 384, 1024 in all within a row
- pad_counts: int32 [8], P('dp'), may hold values from 0 to 127
- ln1_gain: bfloat16 [1024], replicated, may hold values from 0.5 to 1.5
- ln1_shift: bfloat16 [1024], replicated, may hold values from -1 to 1
- qkv_weight: bfloat16 [1024, 3, 1024], P(None, None, 'tensor'), may hold values from -0.1875 to 0.1875
- qkv_bias: bfloat16 [3, 1024], P(None, 'tensor'), may hold values from -1.5 to 1.5
- out_weight: bfloat16 [1024, 1024], P('tensor'), may hold values from -0.5 to 0.5
- out_bias: bfloat16 [1024], replicated, may hold values from -1 to 1
- ln2_gain: bfloat16 [1024], replicated, may hold values from 0.5 to 1.5
- ln2_shift: bfloat16 [1024], replicated, may hold values from -1 to 1
- fc_weight: bfloat16 [1024, 4096], P(None, 'tensor'), may hold values from -0.1875 to 0.1875
- fc_bias: bfloat16 [4096], P('tensor'), may hold values from -1.5 to 1.5
- proj_weight: bfloat16 [4096, 1024], P('tensor'), may hold values from -0.125 to 0.125
- proj_bias: bfloat16 [1024], replicated, may hold values from -1 to 1
- prefix_embed: bfloat16 [10, 1024], replicated, may hold values from -6 to 6
- reparam_w1: bfloat16 [1024, 512], replicated, may hold values from -0.1875 to 0.1875
- reparam_b1: bfloat16 [512], replicated, may hold values from -1.5 to 1.5
- reparam_w2: bfloat16 [512, 2, 1024], P(None, None, 'tensor'), may hold values from -0.5 to 0.5
- reparam_b2: bfloat16 [2, 1024], P(None, 'tensor'), may hold values from -1.5 to 1.5
Outputs:
- mixed: bfloat16 [8, 1024, 1024], P('dp')
- input_grad: float32 [8, 1024, 1024], P('dp')
- embed_grad: float32 [10, 1024], replicated
- w1_grad: float32 [1024, 512], replicated
- b1_grad: float32 [512], replicated
- w2_grad: float32 [512, 2, 1024], P(None, None, 'tensor')
- b2_grad: float32 [2, 1024], P(None, 'tensor')
- prefix_kv: float32 [10, 2, 1024], P(None, None, 'tensor')
Inputs may be any that keep to these rules, and one draw needn't show every extreme that they name: `seg_lengths`: each row's 8 lengths add up to 1024, and each row has a segment of exactly 384 tokens.
All inputs are finite; a program needn't handle non-finite values.
Results may differ from a plain program's by a relative error of at most 0.0097.
Values sent between devices are 32-bit elements; how exact they have to be, the bound alone decides.
No kernel may reach another device: no remote copies, remote signals or barrier semaphores. Data moves between devices by JAX's collectives and lax.ppermute only.
A program may use at most 128 MiB of HBM per device.

v0:
```python
import jax
import jax.numpy as jnp
from jax import lax
from jax.sharding import PartitionSpec as P

HEAD_DIM = 64
QBLK = 512


highest = lax.Precision.HIGHEST
epsilon = 1e-05


def layer_norm(values, gain, shift):
    center = jnp.mean(values, axis=-1, keepdims=True)
    centered = values - center
    spread = jnp.mean(centered * centered, axis=-1, keepdims=True)
    return centered * lax.rsqrt(spread + epsilon) * gain + shift


def gelu_tanh(values):
    return (
        0.5
        * values
        * (1.0 + jnp.tanh(0.7978845608028654 * (values + 0.044715 * values * values * values)))
    )


def shards(
    tokens,
    cotangent,
    seg_lengths,
    pad_counts,
    ln1_gain,
    ln1_shift,
    qkv_weight,
    qkv_bias,
    out_weight,
    out_bias,
    ln2_gain,
    ln2_shift,
    fc_weight,
    fc_bias,
    proj_weight,
    proj_bias,
    prefix_embed,
    reparam_w1,
    reparam_b1,
    reparam_w2,
    reparam_b2,
):
    rows_here, length, width = tokens.shape
    local_width = qkv_weight.shape[2]
    heads_here = local_width // HEAD_DIM
    prefix = prefix_embed.shape[0]
    count = rows_here * length
    per_row = length // QBLK
    blocks = rows_here * per_row
    factor = HEAD_DIM ** (-0.5)
    embed = prefix_embed.astype(jnp.float32)
    trunk_weight = reparam_w1.astype(jnp.float32)
    head_weight = reparam_w2.astype(jnp.float32)
    trunk = jnp.tanh(
        jnp.dot(embed, trunk_weight, precision=highest) + reparam_b1.astype(jnp.float32)
    )
    kv_values = jnp.einsum(
        "pr,rtd->ptd", trunk, head_weight, precision=highest
    ) + reparam_b2.astype(jnp.float32)
    kv_low = kv_values.astype(jnp.bfloat16)
    prefix_keys = kv_low[:, 0].reshape(prefix, heads_here, HEAD_DIM)
    prefix_vals = kv_low[:, 1].reshape(prefix, heads_here, HEAD_DIM)
    places = jnp.arange(length, dtype=jnp.int32)
    ends = jnp.cumsum(seg_lengths, axis=1)
    segment = jnp.sum((places[None, :, None] >= ends[:, None, :]).astype(jnp.int32), axis=2)
    usable = places[None, :] < (length - pad_counts)[:, None]
    inputs = tokens.reshape(count, width).astype(jnp.float32)
    normed, norm_one_back = jax.vjp(
        lambda values: layer_norm(
            values, ln1_gain.astype(jnp.float32), ln1_shift.astype(jnp.float32)
        ),
        inputs,
    )
    flat_qkv = qkv_weight.reshape(width, 3 * local_width)
    projected = jnp.dot(normed.astype(jnp.bfloat16), flat_qkv, preferred_element_type=jnp.float32)
    projected = (projected.reshape(count, 3, local_width) + qkv_bias.astype(jnp.float32)).astype(
        jnp.bfloat16
    )
    queries = projected[:, 0].reshape(count, heads_here, HEAD_DIM)
    keys = projected[:, 1].reshape(count, heads_here, HEAD_DIM)
    values = projected[:, 2].reshape(count, heads_here, HEAD_DIM)

    def block_scores(position):
        row_index = position // per_row
        offset = position % per_row * QBLK
        row_start = row_index * length
        query_block = lax.dynamic_slice_in_dim(queries, row_start + offset, QBLK, 0)
        row_segment = lax.dynamic_index_in_dim(segment, row_index, 0, keepdims=False)
        row_usable = lax.dynamic_index_in_dim(usable, row_index, 0, keepdims=False)
        query_pos = offset + jnp.arange(QBLK, dtype=jnp.int32)
        query_seg = lax.dynamic_slice_in_dim(row_segment, offset, QBLK, 0)
        query_use = lax.dynamic_slice_in_dim(row_usable, offset, QBLK, 0)
        allowed = (
            (query_seg[:, None] == row_segment[None, :])
            & (places[None, :] <= query_pos[:, None])
            & row_usable[None, :]
            & query_use[:, None]
        )
        front = (
            jnp.einsum("qhe,phe->hqp", query_block, prefix_keys, preferred_element_type=jnp.float32)
            * factor
        )
        inside = (
            jnp.einsum("qhe,khe->hqk", query_block, keys, preferred_element_type=jnp.float32)
            * factor
        )
        inside = jnp.where(allowed[None], inside, -1e30)
        return (query_block, keys, values, front, inside)

    def forward_block(position):
        query_block, key_row, value_row, front, inside = block_scores(position)
        largest = jnp.maximum(
            jnp.max(front, axis=2, keepdims=True), jnp.max(inside, axis=2, keepdims=True)
        )
        front_exp = jnp.exp(front - largest)
        inside_exp = jnp.exp(inside - largest)
        totals = jnp.sum(front_exp, axis=2, keepdims=True) + jnp.sum(
            inside_exp, axis=2, keepdims=True
        )
        front_prob = (front_exp / totals).astype(jnp.bfloat16)
        inside_prob = (inside_exp / totals).astype(jnp.bfloat16)
        result = jnp.einsum(
            "hqp,phe->qhe", front_prob, prefix_vals, preferred_element_type=jnp.float32
        ) + jnp.einsum("hqk,khe->qhe", inside_prob, value_row, preferred_element_type=jnp.float32)
        return (result.astype(jnp.bfloat16), largest + jnp.log(totals))

    positions = jnp.arange(blocks, dtype=jnp.int32)
    attended, log_norms = lax.map(forward_block, positions)
    attended = attended.reshape(count, local_width)
    branch = lax.psum(jnp.dot(attended, out_weight, preferred_element_type=jnp.float32), "tensor")
    middle = inputs + branch + out_bias.astype(jnp.float32)
    normed_two, norm_two_back = jax.vjp(
        lambda values: layer_norm(
            values, ln2_gain.astype(jnp.float32), ln2_shift.astype(jnp.float32)
        ),
        middle,
    )
    hidden = jnp.dot(
        normed_two.astype(jnp.bfloat16), fc_weight, preferred_element_type=jnp.float32
    ) + fc_bias.astype(jnp.float32)
    activated, gelu_back = jax.vjp(gelu_tanh, hidden)
    feed = lax.psum(
        jnp.dot(activated.astype(jnp.bfloat16), proj_weight, preferred_element_type=jnp.float32),
        "tensor",
    )
    result = middle + feed + proj_bias.astype(jnp.float32)
    mixed = result.astype(jnp.bfloat16).reshape(rows_here, length, width)
    grad_out = cotangent.reshape(count, width).astype(jnp.float32)
    grad_act = jnp.dot(
        cotangent.reshape(count, width), proj_weight.T, preferred_element_type=jnp.float32
    )
    grad_hidden = gelu_back(grad_act)[0].astype(jnp.bfloat16)
    grad_norm_two = lax.psum(
        jnp.dot(grad_hidden, fc_weight.T, preferred_element_type=jnp.float32), "tensor"
    )
    grad_middle = grad_out + norm_two_back(grad_norm_two)[0]
    grad_heads = jnp.dot(
        grad_middle.astype(jnp.bfloat16), out_weight.T, preferred_element_type=jnp.float32
    ).astype(jnp.bfloat16)
    grad_heads = grad_heads.reshape(blocks, QBLK, heads_here, HEAD_DIM)

    def backward_block(item):
        position, grad_block, log_norm = item
        query_block, key_row, value_row, front, inside = block_scores(position)
        front_prob = jnp.exp(front - log_norm)
        inside_prob = jnp.exp(inside - log_norm)
        grad_front = jnp.einsum(
            "qhe,phe->hqp", grad_block, prefix_vals, preferred_element_type=jnp.float32
        )
        grad_inside = jnp.einsum(
            "qhe,khe->hqk", grad_block, value_row, preferred_element_type=jnp.float32
        )
        delta = jnp.sum(front_prob * grad_front, axis=2, keepdims=True) + jnp.sum(
            inside_prob * grad_inside, axis=2, keepdims=True
        )
        score_front = (front_prob * (grad_front - delta)).astype(jnp.bfloat16)
        score_inside = (inside_prob * (grad_inside - delta)).astype(jnp.bfloat16)
        low_front = front_prob.astype(jnp.bfloat16)
        low_inside = inside_prob.astype(jnp.bfloat16)
        grad_query = (
            jnp.einsum("hqp,phe->qhe", score_front, prefix_keys, preferred_element_type=jnp.float32)
            + jnp.einsum("hqk,khe->qhe", score_inside, key_row, preferred_element_type=jnp.float32)
        ) * factor
        grad_key = (
            jnp.einsum(
                "hqk,qhe->khe", score_inside, query_block, preferred_element_type=jnp.float32
            )
            * factor
        )
        grad_value = jnp.einsum(
            "hqk,qhe->khe", low_inside, grad_block, preferred_element_type=jnp.float32
        )
        grad_pkey = (
            jnp.einsum("hqp,qhe->phe", score_front, query_block, preferred_element_type=jnp.float32)
            * factor
        )
        grad_pval = jnp.einsum(
            "hqp,qhe->phe", low_front, grad_block, preferred_element_type=jnp.float32
        )
        return (grad_query, grad_key, grad_value, grad_pkey, grad_pval)

    grad_query, grad_key, grad_value, grad_pkey, grad_pval = lax.map(
        backward_block, (positions, grad_heads, log_norms)
    )
    grad_query = grad_query.reshape(count, local_width)
    grad_key = jnp.sum(grad_key.reshape(rows_here, per_row, length, local_width), axis=1).reshape(
        count, local_width
    )
    grad_value = jnp.sum(
        grad_value.reshape(rows_here, per_row, length, local_width), axis=1
    ).reshape(count, local_width)
    grad_qkv = (
        jnp.stack([grad_query, grad_key, grad_value], axis=1)
        .astype(jnp.bfloat16)
        .reshape(count, 3 * local_width)
    )
    grad_norm_one = lax.psum(
        jnp.dot(grad_qkv, flat_qkv.T, preferred_element_type=jnp.float32), "tensor"
    )
    input_grad = (grad_middle + norm_one_back(grad_norm_one)[0]).reshape(rows_here, length, width)
    grad_prefix = jnp.stack(
        [
            jnp.sum(grad_pkey, axis=0).reshape(prefix, local_width),
            jnp.sum(grad_pval, axis=0).reshape(prefix, local_width),
        ],
        axis=1,
    )
    grad_prefix = lax.psum(grad_prefix, "dp")
    w2_grad = jnp.einsum("pr,ptd->rtd", trunk, grad_prefix, precision=highest)
    b2_grad = jnp.sum(grad_prefix, axis=0)
    grad_trunk = lax.psum(
        jnp.einsum("ptd,rtd->pr", grad_prefix, head_weight, precision=highest), "tensor"
    )
    grad_pre = grad_trunk * (1.0 - trunk * trunk)
    w1_grad = jnp.dot(embed.T, grad_pre, precision=highest)
    b1_grad = jnp.sum(grad_pre, axis=0)
    embed_grad = jnp.dot(grad_pre, trunk_weight.T, precision=highest)
    return (mixed, input_grad, embed_grad, w1_grad, b1_grad, w2_grad, b2_grad, kv_values)


def solution(mesh):
    return jax.shard_map(
        shards,
        mesh=mesh,
        in_specs=(
            P("dp", None, None),
            P("dp", None, None),
            P("dp", None),
            P("dp"),
            P(),
            P(),
            P(None, None, "tensor"),
            P(None, "tensor"),
            P("tensor", None),
            P(),
            P(),
            P(),
            P(None, "tensor"),
            P("tensor"),
            P("tensor", None),
            P(),
            P(),
            P(),
            P(),
            P(None, None, "tensor"),
            P(None, "tensor"),
        ),
        out_specs=(
            P("dp", None, None),
            P("dp", None, None),
            P(),
            P(),
            P(),
            P(None, None, "tensor"),
            P(None, "tensor"),
            P(None, None, "tensor"),
        ),
        check_vma=False,
    )
```

profile of v0, /device:TPU:0, one launch (start us, length us, event | category | flops | bytes accessed | tf_op | source)
XLA Modules:
  0.0 488.5 jit_solution(15700555201545237687)
XLA Ops:
  12.5 1.9 convert_reduce_fusion
  14.5 2.3 fusion.77
  18.2 2.6 copy.76
  20.8 4.0 add_convert_fusion.2
  25.8 24.0 %while.36 = (s32[]{:T(128)}, bf16[2,512,4,64]{1,3,2,0:T(8,128)(2,1)}, f32[2,4,512,1]{2,1,3,0:T(4,128)S(1)}, s32[2]{0:T(128)S(1)}, bf16[1024,4,64]{0,2,1:T(8,128)...) while((s32[]{:T(128)}, ...), condition=%wide.region_9.10_spmd.clone, body=%wide.region_4.9_spmd.clone.sunk | while | flops 570305024 | bytes 36932684 | solution.py:137
  30.0 1.7 fusion.229
  31.7 2.3 fusion.232
  34.1 2.6 fusion.233
  42.0 1.7 fusion.229
  43.7 2.3 fusion.232
  46.2 2.6 fusion.233
  49.8 1.6 copy.80
  51.5 3.8 fusion.157
  56.0 87.6 %all-reduce.5.cloned.1.call-done = f32[1024,1024]{1,0:T(8,128)} async-done(((f32[1024,1024]{1,0:T(8,128)}), f32[1024,1024]{1,0:T(8,128)}) %all-reduce.5.cloned.1.call-update) | async-done | bytes 4194320 | tf_op jit(solution)/shard_map/psum | solution.py:139
  143.7 3.5 fusion.150
  149.1 4.5 fusion.93
  153.6 11.7 %fusion.127 = f32[1024,1024]{1,0:T(8,128)} fusion(bf16[1024,1024]{1,0:T(8,128)(2,1)S(1)} %copy-done, f32[1024,1024]{1,0:T(8,128)} %fusion.93, bf16[1024,1024]{1,0:T(8,128)(2,1)} %param.39, bf16[1,1024,1024]{2,1,0:T(8,128)(2,1)} %param.26, f32[1024]{0:T(1024)S(1)} %convert_element_type.146), kind=kOutput, calls=%fused_computation.155 | convolution fusion | flops 4321181696 | bytes 14684160 | tf_op jit(solution)/shard_map/dot_general | solution.py:163
  165.4 1.5 copy-done.47
  166.8 6.9 %fusion.112 = f32[1024,1024]{1,0:T(8,128)} fusion(bf16[1024,1024]{1,0:T(8,128)(2,1)S(1)} %copy-done.47, f32[1024,1024]{1,0:T(8,128)} %fusion.93, f32[1024]{0:T(1024)S(1)} %convert_element_type.146), kind=kOutput, calls=%fused_computation.146 | convolution fusion | flops 2157969408 | bytes 10489856 | tf_op jit(solution)/shard_map/dot_general | solution.py:152
  173.8 77.3 %all-reduce.7.cloned.1.call-done = f32[1024,1024]{1,0:T(8,128)} async-done(((f32[1024,1024]{1,0:T(8,128)}), f32[1024,1024]{1,0:T(8,128)}) %all-reduce.7.cloned.1.call-update) | async-done | bytes 4194320 | tf_op jit(solution)/shard_map/psum | solution.py:162
  251.1 4.4 multiply_reduce_fusion.2
  257.0 1.7 fusion.149
  258.7 1.9 copy-done.9
  262.9 1.6 copy.83
  264.5 37.0 %while.37 = (s32[]{:T(128)}, bf16[2,512,4,64]{1,3,2,0:T(8,128)(2,1)}, f32[2,1024,4,64]{1,3,2,0:T(8,128)}, f32[2,1024,4,64]{1,3,2,0:T(8,128)}, f32[2,10,4,64]{3,1...) while((s32[]{:T(128)}, ...), condition=%wide.region_20.21_spmd.clone, body=%wide.region_17.20_spmd.clone.sunk | while | flops 1390052352 | bytes 111069408 | solution.py:211
  270.9 2.4 fusion.259
  273.3 3.2 multiply_reduce_fusion.7
  276.5 2.4 multiply_convert_fusion.7
  279.4 1.4 fusion.257
  289.2 2.4 fusion.259
  291.7 3.2 multiply_reduce_fusion.7
  294.9 2.4 multiply_convert_fusion.7
  301.4 1.9 reduce_sum.209
  303.3 1.9 reduce_sum.210
  308.9 5.0 %convolution_bitcast_fusion.1 = f32[1024,1024]{1,0:T(8,128)} fusion(bf16[1024,3,256]{2,0,1:T(8,128)(2,1)S(1)} %copy-done.22, bf16[1024,1,256]{2,0,1:T(8,128)(2,1)} %copy.88, bf16[1024,1,256]{2,0,1:T(8,128)(2,1)} %copy.87, bf16[1024,1,256]{2,0,1:T(8,128)(2,1)S(1)} %reshape.501), kind=kOutput, calls=%fused_computation.128 | convolution fusion | flops 1612185600 | bytes 7340032 | tf_op jit(solution)/shard_map/dot_general | solution.py:227
  315.6 37.1 %psum.46 = f32[10,2,256]{2,0,1:T(8,128)S(1)} all-reduce(f32[10,2,256]{2,0,1:T(8,128)S(1)} %pad_maximum_fusion), channel_id=1, replica_groups=mesh['dp'=8,'tensor'=4] {'dp'}, use_global_device_ids=true, to_apply=%region_28.29 | all-reduce | flops 5120 | bytes 40960 | tf_op jit(solution)/shard_map/psum | solution.py:237
  354.4 1.8 copy.93
  356.1 1.8 convolution_bitcast_fusion.3
  357.9 12.0 %psum.47 = f32[10,512]{1,0:T(8,128)S(1)} all-reduce(f32[10,512]{1,0:T(8,128)S(1)} %convolution_bitcast_fusion.3), channel_id=1, replica_groups=mesh['dp'=8,'tensor'=4] {'tensor'}, use_global_device_ids=true, to_apply=%region_29.30 | all-reduce | flops 5120 | bytes 40960 | tf_op jit(solution)/shard_map/psum | solution.py:240
  369.9 2.4 convolution_bitcast_fusion.2
  372.3 2.9 copy.92
  375.8 1.6 fusion.147
  377.3 90.7 %all-reduce.9.cloned.1.call-done = (f32[1024,1024]{1,0:T(8,128)}, f32[1024,1024]{1,0:T(8,128)}) async-done(((f32[1024,1024]{1,0:T(8,128)}, f32[1024,1024]{1,0:T(8,128)}), (f32[1024,1024]{1,0:T(8,128)}, f32[1024,1024]{1,0:T(8,128)})) %all-reduce.9.cloned.1.call-update) | async-done | bytes 8388624 | tf_op jit(solution)/shard_map/psum | solution.py:151
  468.0 3.2 fusion.78
  471.5 1.7 fusion.148
  474.1 3.3 add_bitcast_fusion
  477.4 1.7 copy-done.12
  479.1 2.5 fusion.94
  (229 shorter events, 41.0 us)
Async XLA Ops:
  7.2 141.9 %copy-start = (bf16[1024,1024]{1,0:T(8,128)(2,1)S(1)}, bf16[1024,1024]{1,0:T(8,128)(2,1)}, u32[]{:S(2)}) copy-start(bf16[1024,1024]{1,0:T(8,128)(2,1)} %param.37) | copy-start | bytes 6291460
  7.2 9.6 %copy-start.13 = (bf16[1024,512]{1,0:T(8,128)(2,1)S(1)}, bf16[1024,512]{1,0:T(8,128)(2,1)}, u32[]{:S(2)}) copy-start(bf16[1024,512]{1,0:T(8,128)(2,1)} %param.42) | copy-start | bytes 3145732
  7.2 9.6 %copy-start.31 = (bf16[10,1024]{1,0:T(8,128)(2,1)S(1)}, bf16[10,1024]{1,0:T(8,128)(2,1)}, u32[]{:S(2)}) copy-start(bf16[10,1024]{1,0:T(8,128)(2,1)} %param.41) | copy-start | bytes 61444
  7.2 136.5 %all-reduce.5.cloned.1.call-start = ((), (), s32[]{:S(2)}) async-start(), calls=%async_computation | async-start | bytes 8388608 | tf_op jit(solution)/shard_map/psum | solution.py:139
  9.0 8.1 %copy-start.17 = (bf16[512,2,256]{2,1,0:T(2,128)(2,1)S(1)}, bf16[512,2,256]{2,1,0:T(2,128)(2,1)}, u32[]{:S(2)}) copy-start(bf16[512,2,256]{2,1,0:T(2,128)(2,1)} %param.44) | copy-start | bytes 1572868
  11.2 9.7 %copy-start.36 = (f32[1024]{0:T(1024)}, f32[1024]{0:T(1024)S(1)}, u32[]{:S(2)}) copy-start(f32[1024]{0:T(1024)S(1)} %convert_element_type.132) | copy-start | bytes 12292
  14.5 10.4 %copy-start.34 = (f32[1024]{0:T(1024)}, f32[1024]{0:T(1024)S(1)}, u32[]{:S(2)}) copy-start(f32[1024]{0:T(1024)S(1)} %broadcast_multiply_fusion.1) | copy-start | bytes 12292
  16.8 8.1 %copy-start.40 = (f32[1024]{0:T(1024)}, f32[1024]{0:T(1024)S(1)}, u32[]{:S(2)}) copy-start(f32[1024]{0:T(1024)S(1)} %fusion.135) | copy-start | bytes 12292
  31.7 2.4 copy-start.7
  34.1 2.6 copy-start.29
  43.7 2.4 copy-start.7
  46.1 2.6 copy-start.29
  55.3 195.7 %all-reduce.7.cloned.1.call-start = ((), (), s32[]{:S(2)}) async-start(), calls=%async_computation.1 | async-start | bytes 8388608 | tf_op jit(solution)/shard_map/psum | solution.py:162
  147.2 1.9 copy-start.2
  165.2 1.6 copy-start.47
  165.3 302.8 %all-reduce.9.cloned.1.call-start = ((), (), s32[]{:S(2)}) async-start(), calls=%async_computation.2 | async-start | bytes 16777216 | tf_op jit(solution)/shard_map/psum | solution.py:151
  251.1 4.6 copy-start.3
  251.1 5.9 %copy-start.11 = (f32[1024,1024]{1,0:T(8,128)S(1)}, f32[1024,1024]{1,0:T(8,128)}, u32[]{:S(2)}) copy-start(f32[1024,1024]{1,0:T(8,128)} %all-reduce.7.cloned.1.call-done) | copy-start | bytes 12582916
  257.0 3.7 copy-start.15
  257.0 3.7 copy-start.25
  258.7 2.0 copy-start.9
  260.7 3.8 copy-start.8
  269.3 1.6 copy-start.18
  273.3 3.2 copy-start.19
  276.5 2.9 copy-start.26
  278.9 1.9 copy-start.20
  281.7 1.3 copy-start.21
  287.6 1.6 copy-start.18
  291.7 3.2 copy-start.19
  294.9 2.9 copy-start.26
  297.3 1.9 copy-start.20
  300.1 1.3 copy-start.21
  301.4 5.8 %copy-start.28 = (bf16[2,512,4,64]{1,3,2,0:T(8,128)(2,1)S(1)}, bf16[2,512,4,64]{1,3,2,0:T(8,128)(2,1)}, u32[]{:S(2)}) copy-start(bf16[2,512,4,64]{1,3,2,0:T(8,128)(2,1)} %get-tuple-element.379) | copy-start | bytes 1572868
  303.3 5.6 %copy-start.22 = (bf16[1024,3,256]{2,0,1:T(8,128)(2,1)S(1)}, bf16[1024,3,256]{2,0,1:T(8,128)(2,1)}, u32[]{:S(2)}) copy-start(bf16[1024,3,256]{2,0,1:T(8,128)(2,1)} %param.31) | copy-start | bytes 4718596
  314.0 39.3 %copy-start.24 = (f32[10,512]{1,0:T(8,128)S(1)}, f32[10,512]{1,0:T(8,128)}, u32[]{:S(2)}) copy-start(f32[10,512]{1,0:T(8,128)} %copy-done.23) | copy-start | bytes 61444
  314.6 55.3 %copy-start.32 = (bf16[10,1024]{1,0:T(8,128)(2,1)S(1)}, bf16[10,1024]{1,0:T(8,128)(2,1)}, u32[]{:S(2)}) copy-start(bf16[10,1024]{1,0:T(8,128)(2,1)} %param.41) | copy-start | bytes 61444
  354.3 21.4 %copy-start.14 = (bf16[1024,512]{1,0:T(8,128)(2,1)S(1)}, bf16[1024,512]{1,0:T(8,128)(2,1)}, u32[]{:S(2)}) copy-start(bf16[1024,512]{1,0:T(8,128)(2,1)} %param.42) | copy-start | bytes 3145732
  356.1 111.9 %copy-start.5 = (bf16[1,1024,1024]{2,1,0:T(8,128)(2,1)S(1)}, bf16[1,1024,1024]{2,1,0:T(8,128)(2,1)}, u32[]{:S(2)}) copy-start(bf16[1,1024,1024]{2,1,0:T(8,128)(2,1)} %param.25) | copy-start | bytes 6291460
  356.1 111.9 %copy-start.35 = (f32[1024]{0:T(1024)S(1)}, f32[1024]{0:T(1024)}, u32[]{:S(2)}) copy-start(f32[1024]{0:T(1024)} %copy-done.34) | copy-start | bytes 12292
  356.1 111.9 %copy-start.37 = (f32[1024]{0:T(1024)S(1)}, f32[1024]{0:T(1024)}, u32[]{:S(2)}) copy-start(f32[1024]{0:T(1024)} %copy-done.36) | copy-start | bytes 12292
  375.2 96.1 %copy-start.39 = (f32[1024]{0:T(1024)S(1)}, f32[1024]{0:T(1024)}, u32[]{:S(2)}) copy-start(f32[1024]{0:T(1024)} %copy-done.38) | copy-start | bytes 12292
  375.2 96.1 %copy-start.41 = (f32[1024]{0:T(1024)S(1)}, f32[1024]{0:T(1024)}, u32[]{:S(2)}) copy-start(f32[1024]{0:T(1024)} %copy-done.40) | copy-start | bytes 12292
  468.0 3.4 copy-start.6
  471.2 2.2 copy-start.10
  471.3 2.8 copy-start.16
  474.1 3.3 copy-start.4
  474.1 5.0 %copy-start.12 = (f32[1024,1024]{1,0:T(8,128)S(1)}, f32[1024,1024]{1,0:T(8,128)}, u32[]{:S(2)}) copy-start(f32[1024,1024]{1,0:T(8,128)} %get-tuple-element.636) | copy-start | bytes 12582916
  477.3 4.2 copy-start.1
  (12 other events, 9.9 us)
Sparse Core Ops, SparseCore 0:
  55.5 88.1 all-reduce.4
  165.4 85.6 all-reduce.6
  314.1 153.8 all-reduce.8
where the time goes:
time: 497 us; the launch traced here: 489 us
  waiting for transfers between devices  256 us (52%)
  matrix products  74.5 us (15%)
  blocking collectives  49.1 us (10%)
  other arithmetic  47.2 us (9%)
  local copies, waits for them, and re-layouts  35.1 us (7%)
  between operations  15.4 us (3%)
  loops' own time  11.2 us (2%)
    psum x1, waiting for transfers between devices, shards(): lax.psum(jnp.dot(activated.astype(jnp.bfloat16), proj_weight, preferred_e...  90.7 us
    psum x1, waiting for transfers between devices, shards(): lax.psum(jnp.dot(attended, out_weight, preferred_element_type=jnp.float32...  87.6 us
    psum x1, waiting for transfers between devices, shards(): lax.psum(jnp.dot(grad_hidden, fc_weight.T, preferred_element_type=jnp.flo...  77.3 us
    psum x1, blocking collectives, shards(): grad_prefix = lax.psum(grad_prefix, 'dp')  37.1 us
    unnamed x86, local copies, waits for them, and re-layouts  19.9 us
    psum x1, blocking collectives, shards(): lax.psum(jnp.einsum('ptd,rtd->pr', grad_prefix, head_weight, precision=hi...  12 us
    dot_general x1, matrix products, shards(): jnp.dot(grad_hidden, fc_weight.T, preferred_element_type=jnp.float32)  11.7 us
  transfers between devices with their start and end apart: 3, of which 3 were waited for; matrix products, arithmetic and copies ran while one was open for 4% of the time, Pallas kernels for 0%

commit v1 on v0

v1 whole, which is shorter than its diff:
```python
import functools

import jax
import jax.numpy as jnp
from jax import lax
from jax.experimental import pallas as pl
from jax.experimental.pallas import tpu as pltpu
from jax.sharding import PartitionSpec as P

HEAD_DIM = 64
CORES = 2
QB = 128
SPAN = 384
PAD = 16
RING = 8
LIGHT = 16
KEEP, OWN, FAR = 640, 320, 320
MASKED = -1e30
GAIN_ONE, SHIFT_ONE, OUT_BIAS, GAIN_TWO, SHIFT_TWO, PROJ_BIAS = range(6)
highest = lax.Precision.HIGHEST
epsilon = 1e-05
f32 = jnp.float32
bf16 = jnp.bfloat16


def nn(a, b):
    return jnp.dot(a, b, preferred_element_type=f32)


def nt(a, b):
    return lax.dot_general(a, b, (((1,), (1,)), ((), ())), preferred_element_type=f32)


def tn(a, b):
    return lax.dot_general(a, b, (((0,), (0,)), ((), ())), preferred_element_type=f32)


def params(mib):
    return pltpu.CompilerParams(vmem_limit_bytes=mib * 1024 * 1024)


def in_hbm(values):
    return [pltpu.with_memory_space_constraint(v, pltpu.HBM) for v in values]


def cost(flops, bytes_accessed, transcendentals=0):
    return pl.CostEstimate(
        flops=int(flops) // LIGHT,
        bytes_accessed=int(bytes_accessed) // LIGHT,
        transcendentals=int(transcendentals) // LIGHT,
    )


def unread(after):
    return [pl.BlockSpec(memory_space=pl.ANY)] * len(after)


def once(shape, index):
    return pl.BlockSpec(shape, lambda *_: index, pipeline_mode=pl.Buffered(1))


def vector(ref, number):
    return ref[number : number + 1, :]


def normalize(values):
    centered = values - jnp.mean(values, axis=-1, keepdims=True)
    scale = lax.rsqrt(jnp.mean(centered * centered, axis=-1, keepdims=True) + epsilon)
    return centered * scale, scale


def norm_back(grad, hat, scale):
    mean_grad = jnp.mean(grad, axis=-1, keepdims=True)
    mean_both = jnp.mean(grad * hat, axis=-1, keepdims=True)
    return scale * (grad - mean_grad - hat * mean_both)


class Parcel:
    def __init__(self, length, width, full):
        self.length, self.width, self.full = length, width, full
        self.piece = full // 8
        self.kv = length + self.piece
        self.lse = self.kv + 2 * PAD
        self.bias = self.lse + 2 * (length // QB)
        self.rows = self.bias + 16

    def part(self, start, size):
        assert start % size == 0
        return once((size, self.width), (start // size, 0))


def head_masks():
    lanes = lax.broadcasted_iota(jnp.int32, (QB, 2 * HEAD_DIM), 1)
    return lanes < HEAD_DIM


def both_heads(block, first):
    zero = jnp.zeros_like(block)
    return jnp.concatenate([jnp.where(first, block, zero), jnp.where(first, zero, block)], axis=0)


def own_quadrants(product):
    return jnp.concatenate([product[:HEAD_DIM, :QB], product[HEAD_DIM:, QB:]], axis=0)


def segment_start(position, lengths_ref):
    start, end = jnp.zeros_like(position), jnp.int32(0)
    for number in range(lengths_ref.shape[0]):
        end = end + lengths_ref[number]
        start = jnp.where(position >= end, end, start)
    return start


def by_window(length, lengths_ref, order_ref, run):
    blocks = length // QB
    most = min(length, SPAN + QB) // QB

    def tiles_of(block):
        return block - segment_start(block * QB, lengths_ref) // QB + 1

    def place(block, ends):
        low, high = ends
        small = tiles_of(block) <= most // 2
        order_ref[jnp.where(small, low, high)] = block
        return jnp.where(small, low + 1, low), jnp.where(small, high, high - 1)

    lax.fori_loop(0, blocks, place, (jnp.int32(0), jnp.int32(blocks - 1)))

    def step(number, _):
        pair = order_ref[2 * number], order_ref[2 * number + 1]
        tiles = jnp.maximum(tiles_of(pair[0]), tiles_of(pair[1]))
        for count in (most // 2, most):

            @pl.when((tiles <= count) & (tiles > count - most // 2))
            def _():
                run(pair, count * QB)

        return 0

    lax.fori_loop(0, blocks // 2, step, 0)


def window_bias(block, start, window, length, lengths_ref, pads_ref):
    lanes = lax.broadcasted_iota(jnp.int32, (1, 2 * QB), 1)
    position = block * QB + jnp.where(lanes < QB, lanes, lanes - QB)
    low = segment_start(position, lengths_ref)
    low = jnp.where(position < length - pads_ref[0], low, 4 * length)
    key = start + lax.broadcasted_iota(jnp.int32, (window, 2 * QB), 0)
    return jnp.where((key >= low) & (key <= position), 0.0, MASKED)


def window_start(block, window):
    return pl.multiple_of(jnp.maximum((block + 1) * QB - window, 0), QB)


def prefix_bias(prefix):
    rows = lax.broadcasted_iota(jnp.int32, (PAD, 2 * QB), 0)
    return jnp.where(rows < prefix, 0.0, MASKED)


def project_kernel(first, x_ref, vec_ref, w_ref, bias_ref, *refs):
    if first:
        qkv_ref, normed_ref = refs[-2:]
        hat, _ = normalize(x_ref[...].astype(f32))
        normed = (hat * vector(vec_ref, GAIN_ONE) + vector(vec_ref, SHIFT_ONE)).astype(bf16)
        normed_ref[...] = normed
    else:
        qkv_ref = refs[-1]
        normed = x_ref[...]
    width = w_ref.shape[2]
    for i in range(3):
        part = nn(normed, w_ref[i]) + bias_ref[i : i + 1, :]
        qkv_ref[:, i * width : (i + 1) * width] = part.astype(bf16)


def project(first, x, vectors, weight, bias, bias_spec, after=()):
    length, full = x.shape
    width = weight.shape[2]
    step = 256
    block = pl.BlockSpec((step, full), lambda i: (i, 0))
    specs = [pl.BlockSpec((step, 3 * width), lambda i: (i, 0))]
    shapes = [jax.ShapeDtypeStruct((length, 3 * width), bf16)]
    if first:
        specs.append(block)
        shapes.append(pltpu.HBM((length, full), bf16))
    return pl.pallas_call(
        functools.partial(project_kernel, first),
        grid=(length // step,),
        in_specs=[
            block,
            once(vectors.shape, (0, 0)),
            once(weight.shape, (0, 0, 0)),
            bias_spec,
        ]
        + unread(after),
        out_specs=specs,
        out_shape=shapes,
        compiler_params=params(4),
        cost_estimate=cost(6 * length * full * width, length * full * 8),
        name="project",
    )(x, vectors, weight, bias, *after)


def attend_kernel(
    prefix, parcel, lengths_ref, pads_ref, qkv_ref, kv_ref, bias_ref, *refs
):
    o_ref, token_ref, norm_ref, order_ref = refs[-4:]
    token_ref[...] = jnp.zeros_like(token_ref)
    length, width = parcel.length, parcel.width
    pairs = width // (2 * HEAD_DIM)
    first = head_masks()
    front_bias = prefix_bias(prefix)
    o_ref[parcel.kv : parcel.lse, :] = kv_ref[...]
    o_ref[parcel.bias :, :] = bias_ref[...]

    def attend(blocks, window):
        for block in blocks:
            rows = pl.ds(pl.multiple_of(block * QB, QB), QB)
            start = window_start(block, window)
            keys_at = pl.ds(start, window)
            bias = window_bias(block, start, window, length, lengths_ref, pads_ref)
            for pair in range(pairs):
                at = pair * 2 * HEAD_DIM
                cols = slice(at, at + 2 * HEAD_DIM)
                q = both_heads(qkv_ref[rows, cols] * jnp.asarray(HEAD_DIM**-0.5, bf16), first)
                k = qkv_ref[keys_at, width + at : width + at + 2 * HEAD_DIM]
                v = qkv_ref[keys_at, 2 * width + at : 2 * width + at + 2 * HEAD_DIM]
                pk = kv_ref[:PAD, cols].astype(bf16)
                pv = kv_ref[PAD:, cols].astype(bf16)
                inside = nt(k, q) + bias
                front = nt(pk, q) + front_bias
                largest = jnp.maximum(
                    jnp.max(inside, axis=0, keepdims=True), jnp.max(front, axis=0, keepdims=True)
                )
                inside = jnp.exp(inside - largest)
                front = jnp.exp(front - largest)
                total = jnp.sum(inside, axis=0, keepdims=True) + jnp.sum(
                    front, axis=0, keepdims=True
                )
                scale = 1.0 / total
                out = tn(v, (inside * scale).astype(bf16)) + tn(pv, (front * scale).astype(bf16))
                o_ref[rows, cols] = own_quadrants(out).T
                lse = largest + jnp.log(total)
                norm_ref[pair, pl.ds(2 * block, 1), :] = lse[:, :QB]
                norm_ref[pair, pl.ds(2 * block + 1, 1), :] = lse[:, QB:]

    by_window(length, lengths_ref, order_ref, attend)
    for pair in range(pairs):
        cols = slice(pair * 2 * HEAD_DIM, (pair + 1) * 2 * HEAD_DIM)
        o_ref[parcel.lse : parcel.bias, cols] = norm_ref[pair]


def attend(prefix, parcel, lengths, pads, qkv, prefix_kv, biases, after=()):
    length, width = parcel.length, parcel.width
    return pl.pallas_call(
        functools.partial(attend_kernel, prefix, parcel),
        grid=(1,),
        in_specs=[pl.BlockSpec(memory_space=pltpu.SMEM)] * 2
        + [once(v.shape, (0, 0)) for v in (qkv, prefix_kv, biases)]
        + unread(after),
        out_specs=[once((parcel.rows, width), (0, 0)), once((8, 128), (0, 0))],
        out_shape=[
            jax.ShapeDtypeStruct((parcel.rows, width), f32),
            jax.ShapeDtypeStruct((8, 128), f32),
        ],
        scratch_shapes=[
            pltpu.VMEM((width // (2 * HEAD_DIM), parcel.bias - parcel.lse, 2 * HEAD_DIM), f32),
            pltpu.SMEM((length // QB,), jnp.int32),
        ],
        compiler_params=params(10),
        cost_estimate=cost(
            8 * length * (SPAN + QB) * width,
            length * width * 10,
            length * (SPAN + QB) * width // HEAD_DIM,
        ),
        name="attend",
    )(lengths, pads, qkv, prefix_kv, biases, *after)


def pack_kernel(which_ref, w_ref, *refs):
    out_ref = refs[-1]
    size, width = w_ref.shape[0], out_ref.shape[1]
    for i in range(w_ref.shape[1] // width):
        out_ref[i * size : (i + 1) * size, :] = w_ref[:, i * width : (i + 1) * width].astype(f32)


def pack(which, parcel, out, weight, after=()):
    size = weight.shape[0] // RING
    assert size * (weight.shape[1] // parcel.width) == parcel.piece
    assert parcel.length % parcel.piece == 0
    place = parcel.length // parcel.piece
    return pl.pallas_call(
        pack_kernel,
        grid_spec=pltpu.PrefetchScalarGridSpec(
            num_scalar_prefetch=1,
            grid=(1,),
            in_specs=[pl.BlockSpec((size, weight.shape[1]), lambda i, w: (w[0], 0))]
            + unread([out])
            + unread(after),
            out_specs=pl.BlockSpec((parcel.piece, parcel.width), lambda i, w: (place, 0)),
        ),
        out_shape=jax.ShapeDtypeStruct(out.shape, f32),
        input_output_aliases={2: 0},
        compiler_params=params(2),
        cost_estimate=cost(0, parcel.piece * parcel.width * 6),
        name="pack",
    )(which, weight, out, *after)


def heads_back_kernel(count, core_ref, keep_ref, other_ref, *refs):
    weights, outs = refs[:count], refs[-count:]
    own = pl.program_id(0) == core_ref[0]
    low = jnp.where(own, keep_ref[...], other_ref[...]).astype(bf16)
    for w_ref, out_ref in zip(weights, outs):
        out_ref[...] = nt(low, w_ref[...]).astype(bf16)


def heads_back(which, keep, other, weights, after=()):
    half, full = keep.shape
    step = 256
    count = half // step

    def at_keep(h, i, w):
        return jnp.where(h == w[0], i, (count - 1) * (1 - w[0])), 0

    def at_other(h, i, w):
        return jnp.where(h == w[0], (count - 1) * w[0], i), 0

    return pl.pallas_call(
        functools.partial(heads_back_kernel, len(weights)),
        grid_spec=pltpu.PrefetchScalarGridSpec(
            num_scalar_prefetch=1,
            grid=(2, count),
            in_specs=[pl.BlockSpec((step, full), at_keep), pl.BlockSpec((step, full), at_other)]
            + [once(w.shape, (0, 0)) for w in weights]
            + unread(after),
            out_specs=[
                pl.BlockSpec((step, w.shape[0]), lambda h, i, w: (h * count + i, 0))
                for w in weights
            ],
        ),
        out_shape=[jax.ShapeDtypeStruct((2 * half, w.shape[0]), bf16) for w in weights],
        compiler_params=params(8),
        cost_estimate=cost(4 * half * sum(w.size for w in weights), half * full * 10),
        name="heads_back",
    )(which, keep, other, *weights, *after)


def attend_back_kernel(
    prefix, lengths_ref, pads_ref, qkv_ref, do_ref, kv_ref, lse_ref, *refs
):
    dqkv_ref, dpk_ref, dpv_ref, norm_ref, order_ref, *sums = refs[-9:]
    length, width = do_ref.shape
    pairs = width // (2 * HEAD_DIM)
    first = head_masks()
    front_bias = prefix_bias(prefix)
    for pair in range(pairs):
        norm_ref[pair] = lse_ref[:, pair * 2 * HEAD_DIM : (pair + 1) * 2 * HEAD_DIM]
    for ref in (dpk_ref, dpv_ref, *sums):
        ref[...] = jnp.zeros_like(ref)
    factor = HEAD_DIM**-0.5

    def back(blocks, window):
        for number, block in enumerate(blocks):
            dk_ref, dv_ref = sums[2 * number : 2 * number + 2]
            rows = pl.ds(pl.multiple_of(block * QB, QB), QB)
            start = window_start(block, window)
            keys_at = pl.ds(start, window)
            bias = window_bias(block, start, window, length, lengths_ref, pads_ref)
            for pair in range(pairs):
                at = pair * 2 * HEAD_DIM
                cols = slice(at, at + 2 * HEAD_DIM)
                k = qkv_ref[keys_at, width + at : width + at + 2 * HEAD_DIM]
                v = qkv_ref[keys_at, 2 * width + at : 2 * width + at + 2 * HEAD_DIM]
                pk = kv_ref[:PAD, cols].astype(bf16)
                pv = kv_ref[PAD:, cols].astype(bf16)
                q = both_heads(qkv_ref[rows, cols] * jnp.asarray(factor, bf16), first)
                do = both_heads(do_ref[rows, cols], first)
                lse = jnp.concatenate(
                    [
                        norm_ref[pair, pl.ds(2 * block, 1), :],
                        norm_ref[pair, pl.ds(2 * block + 1, 1), :],
                    ],
                    axis=1,
                )
                inside = jnp.exp(nt(k, q) + bias - lse)
                front = jnp.exp(nt(pk, q) + front_bias - lse)
                d_inside = nt(v, do)
                d_front = nt(pv, do)
                delta = jnp.sum(inside * d_inside, axis=0, keepdims=True) + jnp.sum(
                    front * d_front, axis=0, keepdims=True
                )
                s_inside = (inside * (d_inside - delta)).astype(bf16)
                s_front = (front * (d_front - delta)).astype(bf16)
                dk_ref[keys_at, cols] += nn(s_inside, q)
                dv_ref[keys_at, cols] += nn(inside.astype(bf16), do)
                dpk_ref[:, cols] += nn(s_front, q)
                dpv_ref[:, cols] += nn(front.astype(bf16), do)
                dq = own_quadrants(tn(k, s_inside) + tn(pk, s_front)).T * factor
                dqkv_ref[rows, cols] = dq.astype(bf16)

    by_window(length, lengths_ref, order_ref, back)
    dqkv_ref[:, width : 2 * width] = (sums[0][...] + sums[2][...]).astype(bf16)
    dqkv_ref[:, 2 * width :] = (sums[1][...] + sums[3][...]).astype(bf16)


def attend_back(prefix, parcel, lengths, pads, qkv, grad, out, after=(), weight=1):
    length, width = parcel.length, parcel.width
    lse_rows = parcel.bias - parcel.lse
    return pl.pallas_call(
        functools.partial(attend_back_kernel, prefix),
        grid=(1,),
        in_specs=[pl.BlockSpec(memory_space=pltpu.SMEM)] * 2
        + [
            once(qkv.shape, (0, 0)),
            once(grad.shape, (0, 0)),
            parcel.part(parcel.kv, 2 * PAD),
            parcel.part(parcel.lse, lse_rows),
        ]
        + unread(after),
        out_specs=[
            once((length, 3 * width), (0, 0)),
            once((PAD, width), (0, 0)),
            once((PAD, width), (0, 0)),
        ],
        out_shape=[
            jax.ShapeDtypeStruct((length, 3 * width), bf16),
            jax.ShapeDtypeStruct((PAD, width), f32),
            jax.ShapeDtypeStruct((PAD, width), f32),
        ],
        scratch_shapes=[
            pltpu.VMEM((width // (2 * HEAD_DIM), lse_rows, 2 * HEAD_DIM), f32),
            pltpu.SMEM((length // QB,), jnp.int32),
        ]
        + [pltpu.VMEM((length, width), f32)] * 4,
        compiler_params=params(14),
        cost_estimate=cost(
            weight * 20 * length * (SPAN + QB) * width,
            length * width * 40,
            length * (SPAN + QB) * width // HEAD_DIM,
        ),
        name="attend_back",
    )(lengths, pads, qkv, grad, out, out, *after)


def pass_kernel(*refs):
    del refs


def held(values, after):
    count = len(values)
    return pl.pallas_call(
        pass_kernel,
        in_specs=unread(values) + unread(after),
        out_specs=unread(values),
        out_shape=[jax.ShapeDtypeStruct(v.shape, v.dtype) for v in values],
        input_output_aliases={i: i for i in range(count)},
        compiler_params=params(1),
        cost_estimate=cost(0, 0),
        name="held",
    )(*values, *after)


def pick_kernel(count, which_ref, *refs):
    weights, outs = refs[:count], refs[-2 * count - 1 : -count - 1]
    buffers, sems = refs[-count - 1 : -1], refs[-1]
    copies = []
    for number, (ref, buffer) in enumerate(zip(weights, buffers)):
        size = buffer.shape[-2]
        rows = pl.ds(pl.multiple_of(which_ref[number] * size, size), size)
        source = ref.at[rows, :] if len(ref.shape) == 2 else ref.at[:, rows, :]
        copies.append(pltpu.make_async_copy(source, buffer, sems.at[number]))
        copies[-1].start()
    for copy, buffer, out_ref in zip(copies, buffers, outs):
        copy.wait()
        out_ref[...] = buffer[...].astype(f32)


def picked(whiches, weights, after=()):
    shapes = [(*w.shape[:-2], w.shape[-2] // RING, w.shape[-1]) for w in weights]
    return pl.pallas_call(
        functools.partial(pick_kernel, len(weights)),
        grid=(1,),
        in_specs=[pl.BlockSpec(memory_space=pltpu.SMEM)]
        + [pl.BlockSpec(memory_space=pltpu.HBM)] * len(weights)
        + unread(after),
        out_specs=[once(shape, (0,) * len(shape)) for shape in shapes],
        out_shape=[jax.ShapeDtypeStruct(shape, f32) for shape in shapes],
        scratch_shapes=[pltpu.VMEM(shape, bf16) for shape in shapes]
        + [pltpu.SemaphoreType.DMA((len(weights),))],
        compiler_params=params(6),
        cost_estimate=cost(0, sum(shape[-2] * shape[-1] for shape in shapes) * 6),
        name="pick",
    )(jnp.concatenate(whiches), *in_hbm(weights), *after)


def assemble_kernel(shifts, folded, order_ref, *refs):
    out_ref = refs[-1]
    pieces = refs[: len(shifts)]
    size = pieces[0].shape[-2]
    for shift, ref in zip(shifts, pieces):
        at = lax.rem(order_ref[0] + (shift + RING), RING) * size
        rows = pl.ds(pl.multiple_of(at, size), size)
        if folded and ref is pieces[-1]:
            width = ref.shape[1]
            for i in range(out_ref.shape[1] // width):
                block = ref[i * size : (i + 1) * size, :]
                out_ref[rows, i * width : (i + 1) * width] = block.astype(bf16)
        else:
            out_ref[..., rows, :] = ref[...].astype(bf16)


def assembled(order, shifts, pieces, last_spec, folded=False, after=()):
    shape = pieces[0].shape
    zeros = (0,) * len(shape)
    whole = (*shape[:-2], shape[-2] * RING, shape[-1])
    return pl.pallas_call(
        functools.partial(assemble_kernel, shifts, folded),
        grid=(1,),
        in_specs=[pl.BlockSpec(memory_space=pltpu.SMEM)]
        + [once(shape, zeros)] * (len(pieces) - 1)
        + [last_spec]
        + unread(after),
        out_specs=once(whole, zeros),
        out_shape=jax.ShapeDtypeStruct(whole, bf16),
        compiler_params=params(6),
        cost_estimate=cost(0, shape[-2] * RING * shape[-1] * 6),
        name="assemble",
    )(order, *pieces, *after)


def product_kernel(pieces, which_ref, *refs):
    total = None
    for a_ref, b_ref in zip(refs[:pieces], refs[pieces : 2 * pieces]):
        part = nn(a_ref[...].astype(bf16), b_ref[...])
        total = part if total is None else total + part
    refs[-1][...] = total


def half_product(which, half, lefts, rights, after=(), weight=1):
    columns = rights[0].shape[1]
    step = 256
    count = half // step
    depth = sum(b.shape[0] for b in rights)
    return pl.pallas_call(
        functools.partial(product_kernel, len(lefts)),
        grid_spec=pltpu.PrefetchScalarGridSpec(
            num_scalar_prefetch=1,
            grid=(count,),
            in_specs=[
                pl.BlockSpec((step, a.shape[1]), lambda i, w: (w[0] * count + i, 0)) for a in lefts
            ]
            + [once(b.shape, (0, 0)) for b in rights]
            + unread(after),
            out_specs=pl.BlockSpec((step, columns), lambda i, w: (i, 0)),
        ),
        out_shape=jax.ShapeDtypeStruct((half, columns), f32),
        compiler_params=params(6),
        cost_estimate=cost(
            weight * 2 * half * columns * depth, half * columns * 4 + depth * columns * 2
        ),
        name="half_product",
    )(which, *lefts, *rights, *after)


def unproject_kernel(pieces, which_ref, *refs):
    total = None
    for grad_ref, w_ref in zip(refs[:pieces], refs[pieces : 2 * pieces]):
        width = w_ref.shape[2]
        part = None
        for i in range(3):
            product = nt(grad_ref[:, i * width : (i + 1) * width], w_ref[i])
            part = product if part is None else part + product
        total = part if total is None else total + part
    refs[-1][...] = total


def unproject(which, grads, weights, after=()):
    full, width = weights[0].shape[1:]
    half = grads[0].shape[0] // 2
    step = 256
    count = half // step
    return pl.pallas_call(
        functools.partial(unproject_kernel, len(weights)),
        grid_spec=pltpu.PrefetchScalarGridSpec(
            num_scalar_prefetch=1,
            grid=(count,),
            in_specs=[pl.BlockSpec((step, 3 * width), lambda i, w: (w[0] * count + i, 0))]
            * len(grads)
            + [once(w.shape, (0, 0, 0)) for w in weights]
            + unread(after),
            out_specs=pl.BlockSpec((step, full), lambda i, w: (i, 0)),
        ),
        out_shape=jax.ShapeDtypeStruct((half, full), f32),
        compiler_params=params(4),
        cost_estimate=cost(6 * half * full * width * len(weights), half * full * 8),
        name="unproject",
    )(which, *grads, *weights, *after)


def norm_two_kernel(which_ref, x_ref, a_ref, b_ref, vec_ref, *refs):
    middle_ref, normed_ref = refs[-2:]
    middle = x_ref[...].astype(f32) + (a_ref[...] + b_ref[...]) + vector(vec_ref, OUT_BIAS)
    middle_ref[...] = middle
    hat, _ = normalize(middle)
    normed = hat * vector(vec_ref, GAIN_TWO) + vector(vec_ref, SHIFT_TWO)
    normed_ref[...] = normed.astype(bf16).astype(f32)


def norm_two(which, x, terms, vectors, after=()):
    half, width = terms[0].shape
    step = 128
    count = half // step
    block = pl.BlockSpec((step, width), lambda i, w: (i, 0))
    return pl.pallas_call(
        norm_two_kernel,
        grid_spec=pltpu.PrefetchScalarGridSpec(
            num_scalar_prefetch=1,
            grid=(count,),
            in_specs=[pl.BlockSpec((step, width), lambda i, w: (w[0] * count + i, 0))]
            + [block] * 2
            + [once(vectors.shape, (0, 0))]
            + unread(after),
            out_specs=[block] * 2,
        ),
        out_shape=[jax.ShapeDtypeStruct((half, width), f32)] * 2,
        compiler_params=params(6),
        cost_estimate=cost(half * width * 12, half * width * 20),
        name="norm_two",
    )(which, x, *terms, vectors, *after)


def mlp_kernel(has_sum, which_ref, n_ref, g_ref, fc_ref, proj_ref, bias_ref, *refs):
    feed_ref, back_ref, act_ref, grad_ref = refs[-4:]
    normed = n_ref[...].astype(bf16)
    grad = g_ref[...]
    units, step = fc_ref.shape[1], bias_ref.shape[1]
    for number, at in enumerate(range(0, units, step)):
        cols = slice(at, at + step)
        hidden = nn(normed, fc_ref[:, cols]) + bias_ref[number : number + 1, :]
        square = hidden * hidden
        inner = jnp.tanh(hidden * (0.7978845608028654 + 0.7978845608028654 * 0.044715 * square))
        gate = 0.5 + 0.5 * inner
        act_ref[:, cols] = (hidden * gate).astype(bf16)
        slope = gate + (0.5 * hidden) * (1.0 - inner * inner) * (
            0.7978845608028654 + 3.0 * 0.7978845608028654 * 0.044715 * square
        )
        grad_ref[:, cols] = (nt(grad, proj_ref[cols, :]) * slope).astype(bf16)
    feed = nn(act_ref[...], proj_ref[...])
    back = nt(grad_ref[...], fc_ref[...])
    if has_sum:
        feed = feed + refs[0][...]
        back = back + refs[1][...]
    feed_ref[...] = feed
    back_ref[...] = back


def mlp(which, normed, cotangent, fc, proj, bias, bias_spec, sums=(), after=(), weight=1):
    half, width = normed.shape
    units = fc.shape[1]
    step = 256
    count = half // step
    block = pl.BlockSpec((step, width), lambda i, w: (i, 0))
    return pl.pallas_call(
        functools.partial(mlp_kernel, bool(sums)),
        grid_spec=pltpu.PrefetchScalarGridSpec(
            num_scalar_prefetch=1,
            grid=(count,),
            in_specs=[
                block,
                pl.BlockSpec((step, width), lambda i, w: (w[0] * count + i, 0)),
                once(fc.shape, (0, 0)),
                once(proj.shape, (0, 0)),
                bias_spec,
            ]
            + [block] * len(sums)
            + unread(after),
            out_specs=[block] * 2,
            scratch_shapes=[pltpu.VMEM((step, units), bf16)] * 2,
        ),
        out_shape=[jax.ShapeDtypeStruct((half, width), f32)] * 2,
        compiler_params=params(14),
        cost_estimate=cost(
            weight * 8 * half * width * units, half * width * 16 + 4 * width * units, half * units
        ),
        name="mlp",
    )(which, normed, cotangent, fc, proj, bias, *sums, *after)


def norm_two_back_kernel(which_ref, g_ref, a_ref, b_ref, middle_ref, vec_ref, *refs):
    hat, scale = normalize(middle_ref[...])
    grad = (a_ref[...] + b_ref[...]) * vector(vec_ref, GAIN_TWO)
    refs[-1][...] = g_ref[...].astype(f32) + norm_back(grad, hat, scale)


def norm_two_back(which, cotangent, a, b, middle, vectors, after=()):
    half, width = a.shape
    step = 128
    count = half // step
    block = pl.BlockSpec((step, width), lambda i, w: (i, 0))
    return pl.pallas_call(
        norm_two_back_kernel,
        grid_spec=pltpu.PrefetchScalarGridSpec(
            num_scalar_prefetch=1,
            grid=(count,),
            in_specs=[
                pl.BlockSpec((step, width), lambda i, w: (w[0] * count + i, 0)),
                block,
                block,
                block,
                once(vectors.shape, (0, 0)),
            ]
            + unread(after),
            out_specs=block,
        ),
        out_shape=jax.ShapeDtypeStruct((half, width), f32),
        compiler_params=params(7),
        cost_estimate=cost(half * width * 20, half * width * 18),
        name="norm_two_back",
    )(which, cotangent, a, b, middle, vectors, *after)


def norm_one_back_kernel(which_ref, x_ref, upper_ref, vec_ref, a_ref, b_ref, *refs):
    hat, scale = normalize(x_ref[...].astype(f32))
    grad = (a_ref[...] + b_ref[...]) * vector(vec_ref, GAIN_ONE)
    refs[-2][...] = upper_ref[...] + norm_back(grad, hat, scale)
    refs[-1][...] = jnp.zeros_like(refs[-1])


def norm_one_back(which, x, upper, vectors, a, b, whole=(), after=()):
    half, width = upper.shape
    step = 128
    count = half // step
    block = pl.BlockSpec((step, width), lambda i, w: (i, 0))
    placed = pl.BlockSpec((step, width), lambda i, w: (w[0] * count + i, 0))
    return pl.pallas_call(
        norm_one_back_kernel,
        grid_spec=pltpu.PrefetchScalarGridSpec(
            num_scalar_prefetch=1,
            grid=(count,),
            in_specs=[placed, block, once(vectors.shape, (0, 0)), block, block]
            + unread(whole)
            + unread(after),
            out_specs=[placed, once((8, 128), (0, 0))],
        ),
        out_shape=[
            jax.ShapeDtypeStruct((2 * half, width), f32),
            jax.ShapeDtypeStruct((8, 128), f32),
        ],
        input_output_aliases={6: 0} if whole else {},
        compiler_params=params(6),
        cost_estimate=cost(half * width * 20, half * width * 18),
        name="norm_one_back",
    )(which, x, upper, vectors, a, b, *whole, *after)


def result_kernel(which_ref, a_ref, b_ref, middle_ref, vec_ref, *refs):
    half_ref, whole_ref, token_ref = refs[-3:]
    token_ref[...] = jnp.zeros_like(token_ref)
    result = middle_ref[...] + (a_ref[...] + b_ref[...]) + vector(vec_ref, PROJ_BIAS)
    half_ref[...] = result
    whole_ref[...] = result.astype(bf16)


def result_half(which, a, b, middle, vectors, after=(), weight=1):
    half, width = middle.shape
    step = 128
    count = half // step
    block = pl.BlockSpec((step, width), lambda i, w: (i, 0))
    placed = pl.BlockSpec((step, width), lambda i, w: (w[0] * count + i, 0))
    return pl.pallas_call(
        result_kernel,
        grid_spec=pltpu.PrefetchScalarGridSpec(
            num_scalar_prefetch=1,
            grid=(count,),
            in_specs=[block, block, block, once(vectors.shape, (0, 0))] + unread(after),
            out_specs=[block, placed, once((8, 128), (0, 0))],
        ),
        out_shape=[
            jax.ShapeDtypeStruct((half, width), f32),
            jax.ShapeDtypeStruct((2 * half, width), bf16),
            jax.ShapeDtypeStruct((8, 128), f32),
        ],
        compiler_params=params(6),
        cost_estimate=cost(weight * half * width * 2048, half * width * 18),
        name="result",
    )(which, a, b, middle, vectors, *after)


def place_kernel(which_ref, half_ref, *refs):
    refs[-2][...] = half_ref[...].astype(refs[-2].dtype)
    refs[-1][...] = jnp.zeros_like(refs[-1])


def placed_half(which, half_values, whole, after=()):
    half, width = half_values.shape
    step = 128
    count = half // step
    return pl.pallas_call(
        place_kernel,
        grid_spec=pltpu.PrefetchScalarGridSpec(
            num_scalar_prefetch=1,
            grid=(count,),
            in_specs=[pl.BlockSpec((step, width), lambda i, w: (i, 0))]
            + unread([whole])
            + unread(after),
            out_specs=[
                pl.BlockSpec((step, width), lambda i, w: (w[0] * count + i, 0)),
                once((8, 128), (0, 0)),
            ],
        ),
        out_shape=[
            jax.ShapeDtypeStruct(whole.shape, whole.dtype),
            jax.ShapeDtypeStruct((8, 128), f32),
        ],
        input_output_aliases={2: 0},
        compiler_params=params(3),
        cost_estimate=cost(0, half * width * 8),
        name="place",
    )(which, half_values, whole, *after)


def parts(values):
    high = values.astype(bf16)
    return high, (values - high.astype(f32)).astype(bf16)


def prefix_kernel(a_ref, b_ref, trunk_ref, embed_ref, w1_ref, *refs):
    w1_grad_ref, w2_grad_ref, b1_grad_ref, b2_grad_ref, embed_grad_ref = refs[-5:]
    columns = w2_grad_ref.shape[2]
    wide = w2_grad_ref.shape[1] * columns
    both = a_ref[:PAD, :] + b_ref[:PAD, :]
    kv, trunk = both[:, :wide], trunk_ref[...]
    pre = both[:, wide:] * (1.0 - trunk * trunk)
    pre_high, pre_low = parts(pre)
    embed = embed_ref[...]
    w1_grad_ref[...] = tn(
        jnp.concatenate([embed, embed], axis=0), jnp.concatenate([pre_high, pre_low], axis=0)
    )
    rows = nt(jnp.concatenate([pre_high, pre_low], axis=0), w1_ref[...])
    embed_grad_ref[...] = rows[:PAD] + rows[PAD:]
    b1_grad_ref[...] = jnp.sum(pre, axis=0, keepdims=True)
    b2_grad = jnp.sum(kv, axis=0, keepdims=True)
    trunk_high, trunk_low = parts(trunk)
    kv_high, kv_low = parts(kv)
    w2_grad = tn(
        jnp.concatenate([trunk_high, trunk_high, trunk_low], axis=0),
        jnp.concatenate([kv_high, kv_low, kv_high], axis=0),
    )
    for i in range(w2_grad_ref.shape[1]):
        cols = slice(i * columns, (i + 1) * columns)
        w2_grad_ref[:, i, :] = w2_grad[:, cols]
        b2_grad_ref[i : i + 1, :] = b2_grad[:, cols]


def prefix_grads(a, b, trunk, embed, w1, width, after=()):
    full, rank = w1.shape
    shapes = [(full, rank), (rank, 2, width), (1, rank), (2, width), (PAD, full)]
    return pl.pallas_call(
        prefix_kernel,
        grid=(1,),
        in_specs=[once(v.shape, (0, 0)) for v in (a, b, trunk, embed, w1)] + unread(after),
        out_specs=[once(shape, (0,) * len(shape)) for shape in shapes],
        out_shape=[jax.ShapeDtypeStruct(shape, f32) for shape in shapes],
        compiler_params=params(16),
        cost_estimate=cost(0, full * rank * 8),
        name="prefix_grads",
    )(a, b, trunk, embed, w1, *after)


def shards(
    group,
    copies,
    tokens,
    cotangent,
    seg_lengths,
    pad_counts,
    ln1_gain,
    ln1_shift,
    qkv_weight,
    qkv_bias,
    out_weight,
    out_bias,
    ln2_gain,
    ln2_shift,
    fc_weight,
    fc_bias,
    proj_weight,
    proj_bias,
    prefix_embed,
    reparam_w1,
    reparam_b1,
    reparam_w2,
    reparam_b2,
):
    rows_here, length, width = tokens.shape
    assert rows_here == 1 and copies % RING == 0
    local_width = qkv_weight.shape[2]
    prefix = prefix_embed.shape[0]
    half = length // 2
    parcel = Parcel(length, local_width, width)
    place = lax.axis_index("tensor")
    core = place % CORES
    mine = core.reshape(1).astype(jnp.int32)
    theirs = 1 - mine
    none = mine * 0
    far_shifts = [CORES * s for s in range(1, group // CORES)]

    def to_core(values):
        return lax.ppermute(values, "tensor", [(t, t ^ 1) for t in range(group)])

    def to_far(values):
        return [
            lax.ppermute(values, "tensor", [(t, (t + shift) % group) for t in range(group)])
            for shift in far_shifts
        ]

    def swapped(values, axis, size, step):
        return values + lax.ppermute(values, axis, [(i, i ^ step) for i in range(size)])

    ring = list(range(0, RING, 2)) + list(range(RING - 1, 0, -2))
    member = lax.axis_index("dp") % RING
    order = jnp.where(member % 2 == 0, member // 2, RING - 1 - member // 2)
    here = order.reshape(1).astype(jnp.int32)
    across = (here + RING // 2) % RING
    hops = RING // 2 - 1

    def along(values, step):
        hop = [
            (base + ring[i], base + ring[(i + step) % RING])
            for base in range(0, copies, RING)
            for i in range(RING)
        ]
        return lax.ppermute(values, "dp", hop)

    def hop(rings):
        for levels in rings:
            up, down = levels[-1]
            levels.append((along(up, 1), along(down, -1)))

    def last(rings):
        return [piece for levels in rings for piece in levels[-1]]

    def hold(rings, after):
        for levels in rings:
            up, down = levels[-1]
            if up is down:
                up = down = held([up], after)[0]
            else:
                up, down = held([up, down], after)
            levels[-1] = (up, down)

    def starting(pieces):
        return [[(piece, piece)] for piece in pieces]

    def rebuilt(levels, facing, spec, folded=False, after=()):
        shifts, pieces = [0], [levels[0][0]]
        for number, (up, down) in enumerate(levels[1:]):
            shifts += [-1 - number, number + 1]
            pieces += [up, down]
        return assembled(here, shifts + [RING // 2], pieces + [facing], spec, folded, after)

    x = tokens.reshape(length, width)
    grad_out = cotangent.reshape(length, width)
    lengths = seg_lengths.reshape(-1)
    qkv_w = jnp.transpose(qkv_weight, (1, 0, 2))
    vectors = jnp.stack([ln1_gain, ln1_shift, out_bias, ln2_gain, ln2_shift, proj_bias])
    vectors = jnp.pad(vectors, ((0, 2), (0, 0))).astype(f32)

    (piece_fc,) = picked([here], [fc_weight])
    near_fc = to_far(piece_fc)
    (piece_out,) = picked([here], [out_weight], [piece_fc])
    near_out = to_far(piece_out)
    (piece_proj,) = picked([here], [proj_weight], [piece_out])
    near_proj = to_far(piece_proj)
    ring_out, ring_fc, ring_proj = starting(near_out), starting(near_fc), starting(near_proj)

    fc_rows = fc_bias.astype(f32).reshape(-1, local_width)
    biases = jnp.concatenate(
        [
            jnp.pad(qkv_bias.astype(f32), ((0, 5), (0, 0))),
            jnp.pad(fc_rows, ((0, 8 - fc_rows.shape[0]), (0, 0))),
        ],
        axis=0,
    )
    qkv_bias_spec = once((8, local_width), (0, 0))
    fc_bias_spec = once((8, local_width), (1, 0))
    qkv, normed_one = project(True, in_hbm([x])[0], vectors, qkv_w, biases, qkv_bias_spec)

    embed = prefix_embed.astype(f32)
    trunk_weight = reparam_w1.astype(f32)
    head_weight = reparam_w2.astype(f32)
    trunk = jnp.tanh(jnp.dot(embed, trunk_weight, precision=highest) + reparam_b1.astype(f32))
    kv_values = jnp.einsum(
        "pr,rtd->ptd", trunk, head_weight, precision=highest
    ) + reparam_b2.astype(f32)
    flat_kv = jnp.pad(kv_values, ((0, PAD - prefix), (0, 0), (0, 0)))
    prefix_kv = jnp.concatenate([flat_kv[:, 0], flat_kv[:, 1]], axis=0)

    hold(ring_fc, [qkv])
    fc_held = last(ring_fc)
    hop(ring_fc)
    hold(ring_out, [qkv])
    out_held = last(ring_out)
    hop(ring_out)
    out, token = attend(
        prefix, parcel, lengths, pad_counts, qkv, prefix_kv, biases, fc_held + out_held
    )
    out = pack(across, parcel, out, out_weight, last(ring_fc) + last(ring_out))
    out = held([out], [token])[0]
    far_out_parcel = to_far(out)
    hold(ring_out, [out])
    out_held = last(ring_out)
    hop(ring_out)
    hold(ring_proj, out_held)
    hop(ring_proj)
    second_out = last(ring_out)
    hop(ring_out)
    hold(ring_fc, last(ring_proj) + second_out)
    hop(ring_fc)
    hold(ring_proj, last(ring_out))
    hop(ring_proj)
    across_fc, across_proj, piece_qkv, across_qkv, behind_qkv, ahead_qkv = picked(
        [across, across, here, across, (here + RING - hops) % RING, (here + hops) % RING],
        [fc_weight, proj_weight] + [qkv_w] * 4,
        last(ring_out),
    )
    far_out = [
        rebuilt(levels, far, parcel.part(length, parcel.piece), True, [across_qkv])
        for levels, far in zip(ring_out, far_out_parcel)
    ]
    lefts = [out] + far_out_parcel
    rights = [out_weight] + far_out
    send = half_product(theirs, half, lefts, rights, last(ring_fc))
    received = to_core(send)
    keep = half_product(mine, half, lefts, rights, [send], KEEP)
    facing_fc = to_far(held([across_fc], last(ring_fc))[0])
    hold(ring_fc, last(ring_proj))
    fc_held = last(ring_fc)
    hop(ring_fc)
    middle, normed = norm_two(mine, x, [keep, received], vectors, fc_held)
    other_normed = to_core(normed)
    own = (fc_weight, proj_weight, biases, fc_bias_spec)
    keep_sums = mlp(mine, normed, grad_out, *own, (), (), OWN)
    hold(ring_proj, [other_normed])
    hop(ring_proj)
    near_qkv = to_far(held([piece_qkv], [normed])[0])
    facing_proj = to_far(held([across_proj], facing_fc + [keep_sums[0]])[0])
    fc_spec, proj_spec = once(piece_fc.shape, (0, 0)), once(piece_proj.shape, (0, 0))
    send_sums = mlp(
        theirs, other_normed, grad_out, *own, (), [keep_sums[0]] + last(ring_fc)
    )
    ring_qkv = starting(near_qkv)
    hold(ring_qkv, [send_sums[0]] + last(ring_fc))
    hop(ring_qkv)
    far_fc = [
        rebuilt(levels, piece, fc_spec, False, [send_sums[0]])
        for levels, piece in zip(ring_fc, facing_fc)
    ]
    far_proj = [
        rebuilt(levels, piece, proj_spec, False, far_fc)
        for levels, piece in zip(ring_proj, facing_proj)
    ]
    far_bias_spec = parcel.part(parcel.bias + 8, 8)
    for fc, proj, far in zip(far_fc, far_proj, far_out_parcel):
        send_sums = mlp(
            theirs, other_normed, grad_out, fc, proj, far, far_bias_spec, send_sums, (), LIGHT
        )
    back_received = to_core(send_sums[1])
    for fc, proj, far in zip(far_fc, far_proj, far_out_parcel):
        keep_sums = mlp(
            mine,
            normed,
            grad_out,
            fc,
            proj,
            far,
            far_bias_spec,
            keep_sums,
            [send_sums[0]],
            FAR,
        )
    facing_qkv = to_far(held([across_qkv], near_qkv + [send_sums[0]])[0])
    upper = norm_two_back(
        mine, grad_out, keep_sums[1], back_received, middle, vectors
    )
    hold(ring_qkv, [upper])
    q_held = last(ring_qkv)
    hop(ring_qkv)
    other_upper = to_core(upper)
    feed_received = to_core(send_sums[0])
    result, mixed, result_token = result_half(
        mine, keep_sums[0], feed_received, middle, vectors, q_held + facing_qkv, FAR
    )
    other_result = to_core(result)
    behind = to_far(held([behind_qkv], [send_sums[0]])[0])
    ahead = to_far(held([ahead_qkv], [upper])[0])

    grads_far = heads_back(
        mine, upper, other_upper, [out_weight] + far_out, [result_token]
    )
    dqkv, grad_keys, grad_vals = attend_back(
        prefix,
        parcel,
        lengths,
        pad_counts,
        qkv,
        grads_far[0],
        out,
        (),
        LIGHT,
    )

    for levels, *ends in zip(ring_qkv, behind, ahead):
        levels.append(ends)
    grad_keys, grad_vals = held(
        [grad_keys, grad_vals],
        behind + ahead + [piece for levels in ring_qkv for piece in levels[-2]],
    )
    grad_here = jnp.concatenate([grad_keys, grad_vals], axis=1)
    flat_head = jnp.transpose(head_weight, (1, 2, 0)).reshape(2 * local_width, -1)
    trunk_here = jnp.dot(grad_here, flat_head, precision=highest)
    for_tensor = [("tensor", group, 1 << i) for i in range(group.bit_length() - 1)]
    for_dp = [("dp", copies, 1 << i) for i in reversed(range(copies.bit_length() - 1))]
    mixed, token = placed_half(theirs, other_result, mixed, [dqkv])
    far_qkv = [
        rebuilt(levels, piece, once(piece.shape, (0, 0, 0)), False, [token])
        for levels, piece in zip(ring_qkv, facing_qkv)
    ]
    qkvs = [qkv_w] + far_qkv
    trunk_here = swapped(trunk_here, *for_tensor[0])
    far_projected = [
        project(
            False,
            in_hbm([normed_one])[0],
            vectors,
            weight,
            far,
            parcel.part(parcel.bias, 8),
            [trunk_here],
        )[0]
        for weight, far in zip(far_qkv, far_out_parcel)
    ]
    for step in for_tensor[1:]:
        trunk_here = swapped(trunk_here, *step)
    grads = [dqkv]
    for number, far in enumerate(far_out_parcel):
        found = attend_back(
            prefix,
            parcel,
            lengths,
            pad_counts,
            far_projected[number],
            grads_far[1 + number],
            far,
            [trunk_here],
            LIGHT,
        )
        grads.append(found[0])
    both = jnp.concatenate([grad_here, trunk_here], axis=1)
    both = swapped(held([both], far_projected)[0], *for_dp[0])
    both = held([both], grads[-1:])[0]
    send_one = unproject(theirs, grads, qkvs, [both])
    received_one = to_core(send_one)
    both = swapped(both, *for_dp[1])
    keep_one = unproject(mine, grads, qkvs, [send_one, both])
    received_two = to_core(keep_one)
    for step in for_dp[2:-1]:
        both = swapped(both, *step)
    last_step = for_dp[-1]
    other_both = lax.ppermute(both, "dp", [(i, i ^ last_step[2]) for i in range(copies)])
    input_grad, token = norm_one_back(mine, x, upper, vectors, keep_one, received_one)
    w1_grad, w2_grad, b1_grad, b2_grad, embed_grad = prefix_grads(
        both,
        other_both,
        jnp.pad(trunk, ((0, PAD - prefix), (0, 0))),
        jnp.pad(prefix_embed, ((0, PAD - prefix), (0, 0))),
        reparam_w1,
        local_width,
        [token],
    )
    input_grad, _ = norm_one_back(
        theirs, x, other_upper, vectors, send_one, received_two, [input_grad], [b1_grad]
    )
    b1_grad, embed_grad = b1_grad.reshape(-1), embed_grad[:prefix]
    mixed, input_grad = mixed.reshape(tokens.shape), input_grad.reshape(tokens.shape)
    return (mixed, input_grad, embed_grad, w1_grad, b1_grad, w2_grad, b2_grad, kv_values)


def solution(mesh):
    return jax.shard_map(
        functools.partial(shards, mesh.shape["tensor"], mesh.shape["dp"]),
        mesh=mesh,
        in_specs=(
            P("dp", None, None),
            P("dp", None, None),
            P("dp", None),
            P("dp"),
            P(),
            P(),
            P(None, None, "tensor"),
            P(None, "tensor"),
            P("tensor", None),
            P(),
            P(),
            P(),
            P(None, "tensor"),
            P("tensor"),
            P("tensor", None),
            P(),
            P(),
            P(),
            P(),
            P(None, None, "tensor"),
            P(None, "tensor"),
        ),
        out_specs=(
            P("dp", None, None),
            P("dp", None, None),
            P(),
            P(),
            P(),
            P(None, None, "tensor"),
            P(None, "tensor"),
            P(None, None, "tensor"),
        ),
        check_vma=False,
    )
```

time: 497 us -> 183 us (0.37); the launches traced: 489 us -> 182 us
  waiting for transfers between devices: 256 us -> 38.8 us
  Pallas kernels: 0 us -> 90 us
  matrix products: 74.5 us -> 1.07 us
  blocking collectives: 49.1 us -> 0 us
  other arithmetic: 47.2 us -> 0.06 us
  starting transfers between devices: 0.29 us -> 41 us
  local copies, waits for them, and re-layouts: 35.1 us -> 8.96 us
  between operations: 15.4 us -> 2.37 us
  loops' own time: 11.2 us -> 0 us
    psum x3 -> x0, waiting for transfers between devices: 256 us -> none  [the longest x1 90.7 us: shards(): lax.psum(jnp.dot(activated.astype(jnp.bfloat16), proj_weight, preferred_e...]
    pallas_call x0 -> x50, Pallas kernels: none -> 90 us  [the longest x4 21 us: mlp(): pl.pallas_call(functools.partial(mlp_kernel, bool(sums)), grid_spec=pltpu...]
    dot_general x40 -> x2, matrix products: 73.6 us -> 0.76 us  [the longest x1 0.51 us: shards(): trunk_here = jnp.dot(grad_here, flat_head, precision=highest)]
    psum x2 -> x0, blocking collectives: 49.1 us -> none  [the longest x1 37.1 us: shards(): grad_prefix = lax.psum(grad_prefix, 'dp')]
    ppermute x0 -> x45, starting transfers between devices: none -> 41 us  [the longest x22 22.6 us: along(): return lax.ppermute(values, 'dp', hop)]
    ppermute x0 -> x45, waiting for transfers between devices: none -> 38.8 us  [the longest x22 26.6 us: along(): return lax.ppermute(values, 'dp', hop)]
    reduce_sum x19 -> x0, other arithmetic: 29.2 us -> none  [the longest x2 7.57 us: layer_norm(): return centered * lax.rsqrt(spread + epsilon) * gain + shift]
    unnamed x86 -> x116, local copies, waits for them, and re-layouts: 19.9 us -> 8.25 us
  transfers between devices with their start and end apart: 3 -> 45, of which waited for: 3 -> 20; matrix products, arithmetic and copies ran while one was open for 4% -> 1% of each run, Pallas kernels for 0% -> 47%
where the time goes in v1:
time: 183 us; the launch traced here: 182 us
  Pallas kernels  90 us (49%)
  starting transfers between devices  41 us (22%)
  waiting for transfers between devices  38.8 us (21%)
  local copies, waits for them, and re-layouts  8.96 us (5%)
  between operations  2.37 us (1%)
    ppermute x22, waiting for transfers between devices, along(): return lax.ppermute(values, 'dp', hop)  26.6 us
    ppermute x22, starting transfers between devices, along(): return lax.ppermute(values, 'dp', hop)  22.6 us
    pallas_call x4, Pallas kernels, mlp(): pl.pallas_call(functools.partial(mlp_kernel, bool(sums)), grid_spec=pltpu...  21 us
    pallas_call x2, Pallas kernels, attend_back(): pl.pallas_call(functools.partial(attend_back_kernel, prefix), grid=(1,),...  20.8 us
    ppermute x10, starting transfers between devices, to_far(): lax.ppermute(values, 'tensor', [(t, (t + shift) % group) for t in range(g...  13.4 us
    ppermute x10, waiting for transfers between devices, to_far(): lax.ppermute(values, 'tensor', [(t, (t + shift) % group) for t in range(g...  9.17 us
    pallas_call x2, Pallas kernels, project(): pl.pallas_call(functools.partial(project_kernel, first), grid=(length //...  9.03 us
    unnamed x116, local copies, waits for them, and re-layouts  8.25 us
  transfers between devices with their start and end apart: 45, of which 20 were waited for; matrix products, arithmetic and copies ran while one was open for 1% of the time, Pallas kernels for 47%

profile of v1, /device:TPU:0, one launch (start us, length us, event | category | flops | bytes accessed | tf_op | source)
XLA Modules:
  0.0 182.3 jit_solution(17545857139312831211)
XLA Ops:
  1.8 3.0 %collective-permute-start = (f32[128,1024]{1,0:T(8,128)S(1)}, f32[128,1024]{1,0:T(8,128)S(1)}, u32[]{:S(2)}, u32[]{:S(2)}) collective-permute-start(f32[128,1024]{1,0:T(8,128)S(1)} %pick.4.refs_1_), channel_id=1, source_target_pairs={{0,2},{1,3},{2,0},{3,1},{4,6},{5,7},{6,4},{7,5},{8,10},{9,11},{10,... | collective-permute-start | bytes 1572872 | tf_op jit(solution)/shard_map/ppermute | solution.py:914
  5.9 1.8 pick.7
  7.7 2.0 %collective-permute-start.11 = (f32[128,1024]{1,0:T(8,128)}, f32[128,1024]{1,0:T(8,128)}, u32[]{:S(2)}, u32[]{:S(2)}) collective-permute-start(f32[128,1024]{1,0:T(8,128)} %pick.7), channel_id=1, source_target_pairs={{0,2},{1,3},{2,0},{3,1},{4,6},{5,7},{6,4},{7,5},{8,10},{9,11},{10,... | collective-permute-start | bytes 1572872 | tf_op jit(solution)/shard_map/ppermute | solution.py:914
  9.9 5.1 %project.2 = (bf16[1024,768]{1,0:T(8,128)(2,1)S(1)}, bf16[1024,1024]{1,0:T(8,128)(2,1)}) custom-call(bf16[1024,1024]{1,0:T(8,128)(2,1)} %bitcast.32, f32[8,1024]{1,0:T(8,128)S(1)} %pad_convert_fusion.vec_ref, bf16[3,1024,256]{2,1,0:T(8,128)(2,1)S(1)} %bitcast.29, f32[16,256]{1,0:T(8,128)S(1)} %fusion.12.bias_ref), custom_call_target="tpu_custom_call" | custom-call | flops 100663296 | bytes 524288 | tf_op jit(solution)/shard_map/project/pallas_call | solution.py:186
  15.7 1.9 %collective-permute-done.refs_0_ = f32[128,1024]{1,0:T(8,128)S(1)} collective-permute-done((f32[128,1024]{1,0:T(8,128)S(1)}, f32[128,1024]{1,0:T(8,128)S(1)}, u32[]{:S(2)}, u32[]{:S(2)}) %collective-permute-start) | collective-permute-done | bytes 524320 | tf_op jit(solution)/shard_map/ppermute | solution.py:914
  17.6 2.1 %collective-permute-start.2 = (f32[128,1024]{1,0:T(8,128)S(1)}, f32[128,1024]{1,0:T(8,128)}, u32[]{:S(2)}, u32[]{:S(2)}) collective-permute-start(f32[128,1024]{1,0:T(8,128)S(1)} %held.20.refs_0_.refs_1_), channel_id=1, source_target_pairs={{0,8},{8,16},{16,24},{24,28},{28,20},{20,12},{12,4},{4,0},{1,9},{9... | collective-permute-start | bytes 1572872 | tf_op jit(solution)/shard_map/ppermute | solution.py:934
  20.4 2.1 %collective-permute-start.4 = (f32[32,1024]{1,0:T(8,128)S(1)}, f32[32,1024]{1,0:T(8,128)S(1)}, u32[]{:S(2)}, u32[]{:S(2)}) collective-permute-start(f32[32,1024]{1,0:T(8,128)S(1)} %held.21.refs_2_.refs_3_.refs_0_), channel_id=1, source_target_pairs={{0,8},{8,16},{16,24},{24,28},{28,20},{20,12},{12,4},{4,0},{1,9},{9... | collective-permute-start | bytes 393224 | tf_op jit(solution)/shard_map/ppermute | solution.py:934
  23.2 8.1 %attend.1 = (f32[1216,256]{1,0:T(8,128)S(1)}, f32[8,128]{1,0:T(8,128)S(1)}) custom-call(s32[8]{0:T(128)S(1)} %bitcast.42, s32[1]{0:T(128)S(6)} %copy.94.pads_ref, bf16[1024,768]{1,0:T(8,128)(2,1)S(1)} %get-tuple-element.61.refs_1_.qkv_ref, f32[32,256]{1,0:T(8,128)S(1)} %pad_maximum_fusion.1.kv_ref, f32[16,256]{1,0:T(8,128)S(1)} %fusion.12.bias_ref, ...), custom_call_target="tpu_custom_call" | custom-call | flops 67108864 | bytes 163840 | tf_op jit(solution)/shard_map/attend/pallas_call | solution.py:255
  33.9 1.6 collective-permute-start.6
  35.5 1.6 collective-permute-start.12
  37.6 1.6 collective-permute-start.7
  39.7 10.9 %collective-permute-done.7.refs_3_.refs_4_ = f32[32,1024]{1,0:T(8,128)S(1)} collective-permute-done((f32[32,1024]{1,0:T(8,128)S(1)}, f32[32,1024]{1,0:T(8,128)S(1)}, u32[]{:S(2)}, u32[]{:S(2)}) %collective-permute-start.7) | collective-permute-done | bytes 131104 | tf_op jit(solution)/shard_map/ppermute | solution.py:934
  50.6 1.6 collective-permute-start.9
  52.6 1.6 collective-permute-start.14
  54.7 2.3 %collective-permute-done.9.refs_6_.refs_5_.refs_2_ = f32[32,1024]{1,0:T(8,128)S(1)} collective-permute-done((f32[32,1024]{1,0:T(8,128)S(1)}, f32[32,1024]{1,0:T(8,128)S(1)}, u32[]{:S(2)}, u32[]{:S(2)}) %collective-permute-start.9) | collective-permute-done | bytes 131104 | tf_op jit(solution)/shard_map/ppermute | solution.py:934
  57.0 1.6 collective-permute-done.10.refs_7_.refs_6_.refs_3_
  59.9 1.6 collective-permute-start.17
  65.0 1.9 %pick.6 = (f32[128,1024]{1,0:T(8,128)S(1)}, f32[128,1024]{1,0:T(8,128)S(1)}, f32[3,128,256]{2,1,0:T(8,128)S(1)}, f32[3,128,256]{2,1,0:T(8,128)S(1)}, f32[3,128,2...) custom-call(s32[6]{0:T(128)S(1)} %copy-done.35, bf16[1024,1024]{1,0:T(8,128)(2,1)} %fc_ref.3, bf16[1024,1024]{1,0:T(8,128)(2,1)} %proj_ref.3, ...), custom_call_target="tpu_custom_call" | custom-call | bytes 147456 | tf_op jit(solution)/shard_map/pick/pallas_call | solution.py:481
  68.3 1.6 collective-permute-done.15.refs_5_.refs_1_.refs_2_
  71.4 2.9 %collective-permute-done.17.refs_2_.refs_0_ = f32[128,1024]{1,0:T(8,128)} collective-permute-done((f32[128,1024]{1,0:T(8,128)}, f32[128,1024]{1,0:T(8,128)}, u32[]{:S(2)}, u32[]{:S(2)}) %collective-permute-start.17) | collective-permute-done | bytes 524320 | tf_op jit(solution)/shard_map/ppermute | solution.py:934
  75.6 1.6 collective-permute-start.19
  81.4 5.2 %mlp.4 = (f32[512,1024]{1,0:T(8,128)S(1)}, f32[512,1024]{1,0:T(8,128)S(1)}) custom-call(s32[1]{0:T(128)} %bitcast.which_ref.core_ref, f32[512,1024]{1,0:T(8,128)S(1)} %get-tuple-element.73.n_ref.refs_1_, bf16[1024,1024]{1,0:T(8,128)(2,1)S(1)} %bitcast.36, bf16[1024,1024]{1,0:T(8,128)(2,1)S(1)} %copy-done.4, bf16[1024,1024]{1,0:T(8,128)(2,1)S(1)} %copy-done.5, ...), custom_call_target="tpu_custom_call" | custom-call | flops 85899345920 | bytes 786432 | tf_op jit(solution)/shard_map/mlp/pallas_call | solution.py:664
  87.2 1.8 collective-permute-start.23
  89.3 1.8 collective-permute-start.27
  91.0 5.2 %mlp.5 = (f32[512,1024]{1,0:T(8,128)S(1)}, f32[512,1024]{1,0:T(8,128)S(1)}) custom-call(s32[1]{0:T(128)S(6)} %sub.14.which_ref, f32[512,1024]{1,0:T(8,128)S(1)} %collective-permute-done.22.n_ref.refs_2_, bf16[1024,1024]{1,0:T(8,128)(2,1)S(1)} %bitcast.37, bf16[1024,1024]{1,0:T(8,128)(2,1)S(1)} %copy-done.4, bf16[1024,1024]{1,0:T(8,128)(2,1)S(1)} %copy-done.5, ...), custom_call_target="tpu_custom_call" | custom-call | flops 268435456 | bytes 786432 | tf_op jit(solution)/shard_map/mlp/pallas_call | solution.py:664
  97.7 3.9 %collective-permute-done.25.refs_7_ = f32[128,1024]{1,0:T(8,128)S(1)} collective-permute-done((f32[128,1024]{1,0:T(8,128)S(1)}, f32[128,1024]{1,0:T(8,128)S(1)}, u32[]{:S(2)}, u32[]{:S(2)}) %collective-permute-start.25) | collective-permute-done | bytes 524320 | tf_op jit(solution)/shard_map/ppermute | solution.py:914
  102.3 1.9 %assemble.6.proj_ref = bf16[1024,1024]{1,0:T(8,128)(2,1)S(1)} custom-call(s32[1]{0:T(128)} %bitcast.2.which_ref.order_ref, f32[128,1024]{1,0:T(8,128)} %held.24.refs_0_, f32[128,1024]{1,0:T(8,128)} %get-tuple-element.69.refs_1_, f32[128,1024]{1,0:T(8,128)} %get-tuple-element.70.refs_2_, f32[128,1024]{1,0:T(8,128)} %get-tuple-element.77.refs_3_, ...), custom_call_target="tpu_custom_call" | custom-call | bytes 393216 | tf_op jit(solution)/shard_map/assemble/pallas_call | solution.py:517
  104.1 5.3 %mlp.6 = (f32[512,1024]{1,0:T(8,128)S(1)}, f32[512,1024]{1,0:T(8,128)S(1)}) custom-call(s32[1]{0:T(128)S(6)} %sub.14.which_ref, f32[512,1024]{1,0:T(8,128)S(1)} %collective-permute-done.22.n_ref.refs_2_, bf16[1024,1024]{1,0:T(8,128)(2,1)S(1)} %bitcast.38, bf16[1024,1024]{1,0:T(8,128)(2,1)S(1)} %assemble.5.refs_8_.fc_ref, ...), custom_call_target="tpu_custom_call" | custom-call | flops 4294967296 | bytes 786432 | tf_op jit(solution)/shard_map/mlp/pallas_call | solution.py:664
  109.5 1.6 collective-permute-start.28
  111.6 1.7 collective-permute-start.31
  113.3 5.2 %mlp.7 = (f32[512,1024]{1,0:T(8,128)S(1)}, f32[512,1024]{1,0:T(8,128)S(1)}) custom-call(s32[1]{0:T(128)} %bitcast.which_ref.core_ref, f32[512,1024]{1,0:T(8,128)S(1)} %get-tuple-element.73.n_ref.refs_1_, bf16[1024,1024]{1,0:T(8,128)(2,1)S(1)} %bitcast.39, bf16[1024,1024]{1,0:T(8,128)(2,1)S(1)} %assemble.5.refs_8_.fc_ref, ...), custom_call_target="tpu_custom_call" | custom-call | flops 85899345920 | bytes 786432 | tf_op jit(solution)/shard_map/mlp/pallas_call | solution.py:664
  118.6 1.7 norm_two_back.1.refs_2_.keep_ref.refs_1_.upper_ref
  122.5 1.7 result.1
  124.2 1.7 collective-permute-start.36
  125.9 1.4 collective-permute-start.34
  128.5 2.2 %heads_back.1 = (bf16[1024,256]{1,0:T(8,128)(2,1)S(1)}, bf16[1024,256]{1,0:T(8,128)(2,1)S(1)}) custom-call(s32[1]{0:T(128)} %bitcast.which_ref.core_ref, f32[512,1024]{1,0:T(8,128)S(1)} %norm_two_back.1.refs_2_.keep_ref.refs_1_.upper_ref, f32[512,1024]{1,0:T(8,128)S(1)} %collective-permute-done.33.other_ref.upper_ref, bf16[256,1024]{1,0:T(8,128)(2,1)S(1)} %copy-done.10, ...), custom_call_target="tpu_custom_call" | custom-call | flops 67108864 | bytes 327680 | tf_op jit(solution)/shard_map/heads_back/pallas_call | solution.py:329
  130.7 10.2 %attend_back.2 = (bf16[1024,768]{1,0:T(8,128)(2,1)S(1)}, f32[16,256]{1,0:T(8,128)S(1)}, f32[16,256]{1,0:T(8,128)S(1)}) custom-call(s32[8]{0:T(128)S(1)} %bitcast.43, s32[1]{0:T(128)S(6)} %copy.94.pads_ref, bf16[1024,768]{1,0:T(8,128)(2,1)S(1)} %copy-done.7, bf16[1024,256]{1,0:T(8,128)(2,1)S(1)} %get-tuple-element.93.do_ref, ...), custom_call_target="tpu_custom_call" | custom-call | flops 2684354560 | bytes 655360 | tf_op jit(solution)/shard_map/attend_back/pallas_call | solution.py:410
  140.9 3.2 %collective-permute-done.37.refs_6_.refs_3_ = f32[3,128,256]{2,1,0:T(8,128)S(1)} collective-permute-done((f32[3,128,256]{2,1,0:T(8,128)S(1)}, f32[3,128,256]{2,1,0:T(8,128)S(1)}, u32[]{:S(2)}, u32[]{:S(2)}) %collective-permute-start.37) | collective-permute-done | bytes 393248 | tf_op jit(solution)/shard_map/ppermute | solution.py:914
  145.9 1.7 collective-permute-start.39
  147.6 1.5 place.1
  149.3 3.9 %project.3.qkv_ref.refs_1_ = bf16[1024,768]{1,0:T(8,128)(2,1)S(1)} custom-call(bf16[1024,1024]{1,0:T(8,128)(2,1)} %get-tuple-element.96.x_ref, f32[8,1024]{1,0:T(8,128)S(1)} %copy-done.26, bf16[3,1024,256]{2,1,0:T(8,128)(2,1)S(1)} %assemble.7.w_ref.refs_3_, f32[1216,256]{1,0:T(8,128)S(1)} %collective-permute-done.6.refs_7_.refs_1_.bias_ref.kv_ref.lse_ref, ...), custom_call_target="tpu_custom_call" | custom-call | flops 100663296 | bytes 524288 | tf_op jit(solution)/shard_map/project/pallas_call | solution.py:186
  153.2 1.6 collective-permute-start.40
  154.9 10.6 %attend_back.3 = (bf16[1024,768]{1,0:T(8,128)(2,1)S(1)}, f32[16,256]{1,0:T(8,128)}, f32[16,256]{1,0:T(8,128)}) custom-call(s32[8]{0:T(128)S(1)} %bitcast.44, s32[1]{0:T(128)S(6)} %copy.94.pads_ref, bf16[1024,768]{1,0:T(8,128)(2,1)S(1)} %project.3.qkv_ref.refs_1_, bf16[1024,256]{1,0:T(8,128)(2,1)S(1)} %get-tuple-element.104.do_ref, ...), custom_call_target="tpu_custom_call" | custom-call | flops 2684354560 | bytes 655360 | tf_op jit(solution)/shard_map/attend_back/pallas_call | solution.py:410
  166.9 2.0 %unproject.2.refs_4_.a_ref = f32[512,1024]{1,0:T(8,128)S(1)} custom-call(s32[1]{0:T(128)S(6)} %sub.14.which_ref, bf16[1024,768]{1,0:T(8,128)(2,1)S(1)} %get-tuple-element.94.refs_1_.refs_0_, bf16[1024,768]{1,0:T(8,128)(2,1)S(1)} %get-tuple-element.105.refs_1_, bf16[3,1024,256]{2,1,0:T(8,128)(2,1)S(1)} %bitcast.30, ...), custom_call_target="tpu_custom_call" | custom-call | flops 100663296 | bytes 262144 | tf_op jit(solution)/shard_map/unproject/pallas_call | solution.py:583
  169.9 2.0 %unproject.3.a_ref = f32[512,1024]{1,0:T(8,128)S(1)} custom-call(s32[1]{0:T(128)} %bitcast.which_ref.core_ref, bf16[1024,768]{1,0:T(8,128)(2,1)S(1)} %get-tuple-element.94.refs_1_.refs_0_, bf16[1024,768]{1,0:T(8,128)(2,1)S(1)} %get-tuple-element.105.refs_1_, bf16[3,1024,256]{2,1,0:T(8,128)(2,1)S(1)} %bitcast.31, ...), custom_call_target="tpu_custom_call" | custom-call | flops 100663296 | bytes 262144 | tf_op jit(solution)/shard_map/unproject/pallas_call | solution.py:583
  173.1 2.8 %norm_one_back.2 = (f32[1024,1024]{1,0:T(8,128)}, f32[8,128]{1,0:T(8,128)S(1)}) custom-call(s32[1]{0:T(128)} %bitcast.which_ref.core_ref, bf16[1024,1024]{1,0:T(8,128)(2,1)S(1)} %bitcast.34, f32[512,1024]{1,0:T(8,128)S(1)} %norm_two_back.1.refs_2_.keep_ref.refs_1_.upper_ref, f32[8,1024]{1,0:T(8,128)S(1)} %copy-done.26, f32[512,1024]{1,0:T(8,128)S(1)} %unproject.3.a_ref, ...), custom_call_target="tpu_custom_call" | custom-call | flops 655360 | bytes 589824 | tf_op jit(solution)/shard_map/norm_one_back/pallas_call | solution.py:736
  176.5 2.2 %prefix_grads.1 = (f32[1024,512]{1,0:T(8,128)}, f32[512,2,256]{2,1,0:T(2,128)}, f32[1,512]{1,0:T(1,128)}, f32[2,256]{1,0:T(2,128)}, f32[16,1024]{1,0:T(8,128)}) custom-call(f32[16,1024]{1,0:T(8,128)S(1)} %add.90.refs_5_.a_ref, f32[16,1024]{1,0:T(8,128)S(1)} %collective-permute-done.44.b_ref, f32[16,512]{1,0:T(8,128)S(1)} %pad.30.trunk_ref, ...), custom_call_target="tpu_custom_call" | custom-call | bytes 262144 | tf_op jit(solution)/shard_map/prefix_grads/pallas_call | solution.py:859
  179.4 2.8 %norm_one_back.3 = (f32[1024,1024]{1,0:T(8,128)}, f32[8,128]{1,0:T(8,128)}) custom-call(s32[1]{0:T(128)S(6)} %sub.14.which_ref, bf16[1024,1024]{1,0:T(8,128)(2,1)S(1)} %bitcast.35, f32[512,1024]{1,0:T(8,128)S(1)} %collective-permute-done.33.other_ref.upper_ref, f32[8,1024]{1,0:T(8,128)S(1)} %copy-done.26, ...), custom_call_target="tpu_custom_call", output_to_operand_aliasing={{0}: (6, {})} | custom-call | flops 655360 | bytes 589824 | tf_op jit(solution)/shard_map/norm_one_back/pallas_call | solution.py:736
  (233 shorter events, 34.5 us)
Async XLA Ops:
  1.8 15.8 %collective-permute-start = (f32[128,1024]{1,0:T(8,128)S(1)}, f32[128,1024]{1,0:T(8,128)S(1)}, u32[]{:S(2)}, u32[]{:S(2)}) collective-permute-start(f32[128,1024]{1,0:T(8,128)S(1)} %pick.4.refs_1_), channel_id=1, source_target_pairs={{0,2},{1,3},{2,0},{3,1},{4,6},{5,7},{6,4},{7,5},{8,10},{9,11},{10,... | collective-permute-start | bytes 1572872 | tf_op jit(solution)/shard_map/ppermute | solution.py:914
  5.7 14.7 %collective-permute-start.1 = (f32[32,1024]{1,0:T(8,128)S(1)}, f32[32,1024]{1,0:T(8,128)S(1)}, u32[]{:S(2)}, u32[]{:S(2)}) collective-permute-start(f32[32,1024]{1,0:T(8,128)S(1)} %pick.5.refs_1_), channel_id=1, source_target_pairs={{0,2},{1,3},{2,0},{3,1},{4,6},{5,7},{6,4},{7,5},{8,10},{9,11},{10,... | collective-permute-start | bytes 393224 | tf_op jit(solution)/shard_map/ppermute | solution.py:914
  7.7 27.8 %collective-permute-start.11 = (f32[128,1024]{1,0:T(8,128)}, f32[128,1024]{1,0:T(8,128)}, u32[]{:S(2)}, u32[]{:S(2)}) collective-permute-start(f32[128,1024]{1,0:T(8,128)} %pick.7), channel_id=1, source_target_pairs={{0,2},{1,3},{2,0},{3,1},{4,6},{5,7},{6,4},{7,5},{8,10},{9,11},{10,... | collective-permute-start | bytes 1572872 | tf_op jit(solution)/shard_map/ppermute | solution.py:914
  17.6 13.7 %copy-start.11 = (f32[128,1024]{1,0:T(8,128)}, f32[128,1024]{1,0:T(8,128)S(1)}, u32[]{:S(2)}) copy-start(f32[128,1024]{1,0:T(8,128)S(1)} %held.20.refs_0_.refs_1_) | copy-start | bytes 1572868
  17.6 16.3 %collective-permute-start.2 = (f32[128,1024]{1,0:T(8,128)S(1)}, f32[128,1024]{1,0:T(8,128)}, u32[]{:S(2)}, u32[]{:S(2)}) collective-permute-start(f32[128,1024]{1,0:T(8,128)S(1)} %held.20.refs_0_.refs_1_), channel_id=1, source_target_pairs={{0,8},{8,16},{16,24},{24,28},{28,20},{20,12},{12,4},{4,0},{1,9},{9... | collective-permute-start | bytes 1572872 | tf_op jit(solution)/shard_map/ppermute | solution.py:934
  19.7 14.2 %collective-permute-start.3 = (f32[128,1024]{1,0:T(8,128)S(1)}, f32[128,1024]{1,0:T(8,128)}, u32[]{:S(2)}, u32[]{:S(2)}) collective-permute-start(f32[128,1024]{1,0:T(8,128)S(1)} %held.20.refs_0_.refs_1_), channel_id=1, source_target_pairs={{0,4},{8,0},{16,8},{24,16},{28,24},{20,28},{12,20},{4,12},{1,5},{9... | collective-permute-start | bytes 1572872 | tf_op jit(solution)/shard_map/ppermute | solution.py:934
  20.4 12.3 %collective-permute-start.4 = (f32[32,1024]{1,0:T(8,128)S(1)}, f32[32,1024]{1,0:T(8,128)S(1)}, u32[]{:S(2)}, u32[]{:S(2)}) collective-permute-start(f32[32,1024]{1,0:T(8,128)S(1)} %held.21.refs_2_.refs_3_.refs_0_), channel_id=1, source_target_pairs={{0,8},{8,16},{16,24},{24,28},{28,20},{20,12},{12,4},{4,0},{1,9},{9... | collective-permute-start | bytes 393224 | tf_op jit(solution)/shard_map/ppermute | solution.py:934
  22.5 11.4 %collective-permute-start.5 = (f32[32,1024]{1,0:T(8,128)S(1)}, f32[32,1024]{1,0:T(8,128)S(1)}, u32[]{:S(2)}, u32[]{:S(2)}) collective-permute-start(f32[32,1024]{1,0:T(8,128)S(1)} %held.21.refs_2_.refs_3_.refs_0_), channel_id=1, source_target_pairs={{0,4},{8,0},{16,8},{24,16},{28,24},{20,28},{12,20},{4,12},{1,5},{9... | collective-permute-start | bytes 393224 | tf_op jit(solution)/shard_map/ppermute | solution.py:934
  33.9 33.0 %collective-permute-start.6 = (f32[1216,256]{1,0:T(8,128)S(1)}, f32[1216,256]{1,0:T(8,128)S(1)}, u32[]{:S(2)}, u32[]{:S(2)}) collective-permute-start(f32[1216,256]{1,0:T(8,128)S(1)} %held.22.refs_2_.refs_0_.kv_ref.lse_ref), channel_id=1, source_target_pairs={{0,2},{1,3},{2,0},{3,1},{4,6},{5,7},{6,4},{7,5},{8,10},{9,11},{10,... | collective-permute-start | bytes 3735560 | tf_op jit(solution)/shard_map/ppermute | solution.py:914
  35.5 17.1 %copy-start.20 = (f32[32,1024]{1,0:T(8,128)}, f32[32,1024]{1,0:T(8,128)S(1)}, u32[]{:S(2)}) copy-start(f32[32,1024]{1,0:T(8,128)S(1)} %get-tuple-element.65.refs_2_) | copy-start | bytes 393220
  35.5 18.7 %copy-start.18 = (f32[32,1024]{1,0:T(8,128)}, f32[32,1024]{1,0:T(8,128)S(1)}, u32[]{:S(2)}) copy-start(f32[32,1024]{1,0:T(8,128)S(1)} %get-tuple-element.64.refs_1_) | copy-start | bytes 393220
  35.5 17.1 %collective-permute-start.12 = (f32[128,1024]{1,0:T(8,128)}, f32[128,1024]{1,0:T(8,128)}, u32[]{:S(2)}, u32[]{:S(2)}) collective-permute-start(f32[128,1024]{1,0:T(8,128)} %held.24.refs_0_), channel_id=1, source_target_pairs={{0,8},{8,16},{16,24},{24,28},{28,20},{20,12},{12,4},{4,0},{1,9},{9... | collective-permute-start | bytes 1572872 | tf_op jit(solution)/shard_map/ppermute | solution.py:934
  37.2 15.5 %collective-permute-start.13 = (f32[128,1024]{1,0:T(8,128)}, f32[128,1024]{1,0:T(8,128)}, u32[]{:S(2)}, u32[]{:S(2)}) collective-permute-start(f32[128,1024]{1,0:T(8,128)} %held.24.refs_0_), channel_id=1, source_target_pairs={{0,4},{8,0},{16,8},{24,16},{28,24},{20,28},{12,20},{4,12},{1,5},{9... | collective-permute-start | bytes 1572872 | tf_op jit(solution)/shard_map/ppermute | solution.py:934
  37.6 13.0 %collective-permute-start.7 = (f32[32,1024]{1,0:T(8,128)S(1)}, f32[32,1024]{1,0:T(8,128)S(1)}, u32[]{:S(2)}, u32[]{:S(2)}) collective-permute-start(f32[32,1024]{1,0:T(8,128)S(1)} %get-tuple-element.64.refs_1_), channel_id=1, source_target_pairs={{0,8},{8,16},{16,24},{24,28},{28,20},{20,12},{12,4},{4,0},{1,9},{9... | collective-permute-start | bytes 393224 | tf_op jit(solution)/shard_map/ppermute | solution.py:934
  39.2 13.0 %collective-permute-start.8 = (f32[32,1024]{1,0:T(8,128)S(1)}, f32[32,1024]{1,0:T(8,128)S(1)}, u32[]{:S(2)}, u32[]{:S(2)}) collective-permute-start(f32[32,1024]{1,0:T(8,128)S(1)} %get-tuple-element.65.refs_2_), channel_id=1, source_target_pairs={{0,4},{8,0},{16,8},{24,16},{28,24},{20,28},{12,20},{4,12},{1,5},{9... | collective-permute-start | bytes 393224 | tf_op jit(solution)/shard_map/ppermute | solution.py:934
  50.6 6.4 %collective-permute-start.9 = (f32[32,1024]{1,0:T(8,128)S(1)}, f32[32,1024]{1,0:T(8,128)S(1)}, u32[]{:S(2)}, u32[]{:S(2)}) collective-permute-start(f32[32,1024]{1,0:T(8,128)S(1)} %collective-permute-done.7.refs_3_.refs_4_), channel_id=1, source_target_pairs={{0,8},{8,16},{16,24},{24,28},{28,20},{20,12},{12,4},{4,0},{1,9},{9... | collective-permute-start | bytes 393224 | tf_op jit(solution)/shard_map/ppermute | solution.py:934
  52.2 6.4 %collective-permute-start.10 = (f32[32,1024]{1,0:T(8,128)S(1)}, f32[32,1024]{1,0:T(8,128)S(1)}, u32[]{:S(2)}, u32[]{:S(2)}) collective-permute-start(f32[32,1024]{1,0:T(8,128)S(1)} %collective-permute-done.8.refs_4_.refs_5_), channel_id=1, source_target_pairs={{0,4},{8,0},{16,8},{24,16},{28,24},{20,28},{12,20},{4,12},{1,5},{9... | collective-permute-start | bytes 393224 | tf_op jit(solution)/shard_map/ppermute | solution.py:934
  52.6 15.6 %collective-permute-start.14 = (f32[128,1024]{1,0:T(8,128)}, f32[128,1024]{1,0:T(8,128)S(1)}, u32[]{:S(2)}, u32[]{:S(2)}) collective-permute-start(f32[128,1024]{1,0:T(8,128)} %get-tuple-element.67.refs_1_), channel_id=1, source_target_pairs={{0,8},{8,16},{16,24},{24,28},{28,20},{20,12},{12,4},{4,0},{1,9},{9... | collective-permute-start | bytes 1572872 | tf_op jit(solution)/shard_map/ppermute | solution.py:934
  54.3 15.6 %collective-permute-start.15 = (f32[128,1024]{1,0:T(8,128)}, f32[128,1024]{1,0:T(8,128)S(1)}, u32[]{:S(2)}, u32[]{:S(2)}) collective-permute-start(f32[128,1024]{1,0:T(8,128)} %get-tuple-element.68.refs_2_), channel_id=1, source_target_pairs={{0,4},{8,0},{16,8},{24,16},{28,24},{20,28},{12,20},{4,12},{1,5},{9... | collective-permute-start | bytes 1572872 | tf_op jit(solution)/shard_map/ppermute | solution.py:934
  59.9 14.4 %collective-permute-start.17 = (f32[128,1024]{1,0:T(8,128)}, f32[128,1024]{1,0:T(8,128)}, u32[]{:S(2)}, u32[]{:S(2)}) collective-permute-start(f32[128,1024]{1,0:T(8,128)} %get-tuple-element.69.refs_1_), channel_id=1, source_target_pairs={{0,8},{8,16},{16,24},{24,28},{28,20},{20,12},{12,4},{4,0},{1,9},{9... | collective-permute-start | bytes 1572872 | tf_op jit(solution)/shard_map/ppermute | solution.py:934
  61.5 14.1 %collective-permute-start.18 = (f32[128,1024]{1,0:T(8,128)}, f32[128,1024]{1,0:T(8,128)}, u32[]{:S(2)}, u32[]{:S(2)}) collective-permute-start(f32[128,1024]{1,0:T(8,128)} %get-tuple-element.70.refs_2_), channel_id=1, source_target_pairs={{0,4},{8,0},{16,8},{24,16},{28,24},{20,28},{12,20},{4,12},{1,5},{9... | collective-permute-start | bytes 1572872 | tf_op jit(solution)/shard_map/ppermute | solution.py:934
  70.8 7.8 %collective-permute-start.16 = (f32[512,1024]{1,0:T(8,128)S(1)}, f32[512,1024]{1,0:T(8,128)S(1)}, u32[]{:S(2)}, u32[]{:S(2)}) collective-permute-start(f32[512,1024]{1,0:T(8,128)S(1)} %half_product.2.refs_4_), channel_id=1, source_target_pairs={{0,1},{1,0},{2,3},{3,2},{4,5},{5,4},{6,7},{7,6},{8,9},{9,8},{10,11... | collective-permute-start | bytes 6291464 | tf_op jit(solution)/shard_map/ppermute | solution.py:910
  70.8 15.8 %collective-permute-start.21 = (f32[128,1024]{1,0:T(8,128)S(1)}, f32[128,1024]{1,0:T(8,128)S(1)}, u32[]{:S(2)}, u32[]{:S(2)}) collective-permute-start(f32[128,1024]{1,0:T(8,128)S(1)} %held.28), channel_id=1, source_target_pairs={{0,2},{1,3},{2,0},{3,1},{4,6},{5,7},{6,4},{7,5},{8,10},{9,11},{10,... | collective-permute-start | bytes 1572872 | tf_op jit(solution)/shard_map/ppermute | solution.py:914
  75.6 13.7 %collective-permute-start.19 = (f32[128,1024]{1,0:T(8,128)S(1)}, f32[128,1024]{1,0:T(8,128)S(1)}, u32[]{:S(2)}, u32[]{:S(2)}) collective-permute-start(f32[128,1024]{1,0:T(8,128)S(1)} %get-tuple-element.71.refs_0_.refs_3_), channel_id=1, source_target_pairs={{0,8},{8,16},{16,24},{24,28},{28,20},{20,12},{12,4},{4,0},{1,9},{9... | collective-permute-start | bytes 1572872 | tf_op jit(solution)/shard_map/ppermute | solution.py:934
  77.2 13.9 %collective-permute-start.20 = (f32[128,1024]{1,0:T(8,128)S(1)}, f32[128,1024]{1,0:T(8,128)S(1)}, u32[]{:S(2)}, u32[]{:S(2)}) collective-permute-start(f32[128,1024]{1,0:T(8,128)S(1)} %get-tuple-element.72.refs_1_.refs_4_), channel_id=1, source_target_pairs={{0,4},{8,0},{16,8},{24,16},{28,24},{20,28},{12,20},{4,12},{1,5},{9... | collective-permute-start | bytes 1572872 | tf_op jit(solution)/shard_map/ppermute | solution.py:934
  80.0 7.2 %collective-permute-start.22 = (f32[512,1024]{1,0:T(8,128)S(1)}, f32[512,1024]{1,0:T(8,128)S(1)}, u32[]{:S(2)}, u32[]{:S(2)}) collective-permute-start(f32[512,1024]{1,0:T(8,128)S(1)} %get-tuple-element.73.n_ref.refs_1_), channel_id=1, source_target_pairs={{0,1},{1,0},{2,3},{3,2},{4,5},{5,4},{6,7},{7,6},{8,9},{9,8},{10,11... | collective-permute-start | bytes 6291464 | tf_op jit(solution)/shard_map/ppermute | solution.py:910
  86.6 14.9 %collective-permute-start.25 = (f32[128,1024]{1,0:T(8,128)S(1)}, f32[128,1024]{1,0:T(8,128)S(1)}, u32[]{:S(2)}, u32[]{:S(2)}) collective-permute-start(f32[128,1024]{1,0:T(8,128)S(1)} %held.30), channel_id=1, source_target_pairs={{0,2},{1,3},{2,0},{3,1},{4,6},{5,7},{6,4},{7,5},{8,10},{9,11},{10,... | collective-permute-start | bytes 1572872 | tf_op jit(solution)/shard_map/ppermute | solution.py:914
  87.2 14.4 %collective-permute-start.23 = (f32[128,1024]{1,0:T(8,128)}, f32[128,1024]{1,0:T(8,128)S(1)}, u32[]{:S(2)}, u32[]{:S(2)}) collective-permute-start(f32[128,1024]{1,0:T(8,128)} %get-tuple-element.77.refs_3_), channel_id=1, source_target_pairs={{0,8},{8,16},{16,24},{24,28},{28,20},{20,12},{12,4},{4,0},{1,9},{9... | collective-permute-start | bytes 1572872 | tf_op jit(solution)/shard_map/ppermute | solution.py:934
  89.0 13.3 %collective-permute-start.24 = (f32[128,1024]{1,0:T(8,128)}, f32[128,1024]{1,0:T(8,128)S(1)}, u32[]{:S(2)}, u32[]{:S(2)}) collective-permute-start(f32[128,1024]{1,0:T(8,128)} %get-tuple-element.78.refs_4_), channel_id=1, source_target_pairs={{0,4},{8,0},{16,8},{24,16},{28,24},{20,28},{12,20},{4,12},{1,5},{9... | collective-permute-start | bytes 1572872 | tf_op jit(solution)/shard_map/ppermute | solution.py:934
  89.3 20.2 %collective-permute-start.27 = (f32[3,128,256]{2,1,0:T(8,128)S(1)}, f32[3,128,256]{2,1,0:T(8,128)S(1)}, u32[]{:S(2)}, u32[]{:S(2)}) collective-permute-start(f32[3,128,256]{2,1,0:T(8,128)S(1)} %held.31), channel_id=1, source_target_pairs={{0,2},{1,3},{2,0},{3,1},{4,6},{5,7},{6,4},{7,5},{8,10},{9,11},{10,... | collective-permute-start | bytes 1179656 | tf_op jit(solution)/shard_map/ppermute | solution.py:914
  109.4 13.1 %collective-permute-start.26 = (f32[512,1024]{1,0:T(8,128)S(1)}, f32[512,1024]{1,0:T(8,128)S(1)}, u32[]{:S(2)}, u32[]{:S(2)}) collective-permute-start(f32[512,1024]{1,0:T(8,128)S(1)} %get-tuple-element.82.refs_2_.refs_1_), channel_id=1, source_target_pairs={{0,1},{1,0},{2,3},{3,2},{4,5},{5,4},{6,7},{7,6},{8,9},{9,8},{10,11... | collective-permute-start | bytes 6291464 | tf_op jit(solution)/shard_map/ppermute | solution.py:910
  109.5 11.5 %collective-permute-start.28 = (f32[3,128,256]{2,1,0:T(8,128)S(1)}, f32[3,128,256]{2,1,0:T(8,128)S(1)}, u32[]{:S(2)}, u32[]{:S(2)}) collective-permute-start(f32[3,128,256]{2,1,0:T(8,128)S(1)} %held.32.refs_0_), channel_id=1, source_target_pairs={{0,8},{8,16},{16,24},{24,28},{28,20},{20,12},{12,4},{4,0},{1,9},{9... | collective-permute-start | bytes 1179656 | tf_op jit(solution)/shard_map/ppermute | solution.py:934
  111.1 11.3 %collective-permute-start.29 = (f32[3,128,256]{2,1,0:T(8,128)S(1)}, f32[3,128,256]{2,1,0:T(8,128)S(1)}, u32[]{:S(2)}, u32[]{:S(2)}) collective-permute-start(f32[3,128,256]{2,1,0:T(8,128)S(1)} %held.32.refs_0_), channel_id=1, source_target_pairs={{0,4},{8,0},{16,8},{24,16},{28,24},{20,28},{12,20},{4,12},{1,5},{9... | collective-permute-start | bytes 1179656 | tf_op jit(solution)/shard_map/ppermute | solution.py:934
  111.6 10.9 %collective-permute-start.31 = (f32[3,128,256]{2,1,0:T(8,128)S(1)}, f32[3,128,256]{2,1,0:T(8,128)S(1)}, u32[]{:S(2)}, u32[]{:S(2)}) collective-permute-start(f32[3,128,256]{2,1,0:T(8,128)S(1)} %held.34), channel_id=1, source_target_pairs={{0,2},{1,3},{2,0},{3,1},{4,6},{5,7},{6,4},{7,5},{8,10},{9,11},{10,... | collective-permute-start | bytes 1179656 | tf_op jit(solution)/shard_map/ppermute | solution.py:914
  113.3 5.3 %collective-permute-start.30 = (f32[512,1024]{1,0:T(8,128)S(1)}, f32[512,1024]{1,0:T(8,128)S(1)}, u32[]{:S(2)}, u32[]{:S(2)}) collective-permute-start(f32[512,1024]{1,0:T(8,128)S(1)} %get-tuple-element.87), channel_id=1, source_target_pairs={{0,1},{1,0},{2,3},{3,2},{4,5},{5,4},{6,7},{7,6},{8,9},{9,8},{10,11... | collective-permute-start | bytes 6291464 | tf_op jit(solution)/shard_map/ppermute | solution.py:910
  120.2 7.7 %collective-permute-start.33 = (f32[512,1024]{1,0:T(8,128)S(1)}, f32[512,1024]{1,0:T(8,128)S(1)}, u32[]{:S(2)}, u32[]{:S(2)}) collective-permute-start(f32[512,1024]{1,0:T(8,128)S(1)} %norm_two_back.1.refs_2_.keep_ref.refs_1_.upper_ref), channel_id=1, source_target_pairs={{0,1},{1,0},{2,3},{3,2},{4,5},{5,4},{6,7},{7,6},{8,9},{9,8},{10,11... | collective-permute-start | bytes 6291464 | tf_op jit(solution)/shard_map/ppermute | solution.py:910
  124.2 23.4 %collective-permute-start.32 = (f32[512,1024]{1,0:T(8,128)S(1)}, f32[512,1024]{1,0:T(8,128)S(1)}, u32[]{:S(2)}, u32[]{:S(2)}) collective-permute-start(f32[512,1024]{1,0:T(8,128)S(1)} %get-tuple-element.90), channel_id=1, source_target_pairs={{0,1},{1,0},{2,3},{3,2},{4,5},{5,4},{6,7},{7,6},{8,9},{9,8},{10,11... | collective-permute-start | bytes 6291464 | tf_op jit(solution)/shard_map/ppermute | solution.py:910
  124.2 16.7 %collective-permute-start.36 = (f32[3,128,256]{2,1,0:T(8,128)S(1)}, f32[3,128,256]{2,1,0:T(8,128)S(1)}, u32[]{:S(2)}, u32[]{:S(2)}) collective-permute-start(f32[3,128,256]{2,1,0:T(8,128)S(1)} %held.35), channel_id=1, source_target_pairs={{0,2},{1,3},{2,0},{3,1},{4,6},{5,7},{6,4},{7,5},{8,10},{9,11},{10,... | collective-permute-start | bytes 1179656 | tf_op jit(solution)/shard_map/ppermute | solution.py:914
  125.9 15.0 %collective-permute-start.34 = (f32[3,128,256]{2,1,0:T(8,128)S(1)}, f32[3,128,256]{2,1,0:T(8,128)S(1)}, u32[]{:S(2)}, u32[]{:S(2)}) collective-permute-start(f32[3,128,256]{2,1,0:T(8,128)S(1)} %get-tuple-element.88.refs_0_.refs_1_), channel_id=1, source_target_pairs={{0,8},{8,16},{16,24},{24,28},{28,20},{20,12},{12,4},{4,0},{1,9},{9... | collective-permute-start | bytes 1179656 | tf_op jit(solution)/shard_map/ppermute | solution.py:934
  127.4 13.6 %collective-permute-start.35 = (f32[3,128,256]{2,1,0:T(8,128)S(1)}, f32[3,128,256]{2,1,0:T(8,128)S(1)}, u32[]{:S(2)}, u32[]{:S(2)}) collective-permute-start(f32[3,128,256]{2,1,0:T(8,128)S(1)} %get-tuple-element.89.refs_1_.refs_2_), channel_id=1, source_target_pairs={{0,4},{8,0},{16,8},{24,16},{28,24},{20,28},{12,20},{4,12},{1,5},{9... | collective-permute-start | bytes 1179656 | tf_op jit(solution)/shard_map/ppermute | solution.py:934
  128.0 16.2 %collective-permute-start.37 = (f32[3,128,256]{2,1,0:T(8,128)S(1)}, f32[3,128,256]{2,1,0:T(8,128)S(1)}, u32[]{:S(2)}, u32[]{:S(2)}) collective-permute-start(f32[3,128,256]{2,1,0:T(8,128)S(1)} %held.36), channel_id=1, source_target_pairs={{0,2},{1,3},{2,0},{3,1},{4,6},{5,7},{6,4},{7,5},{8,10},{9,11},{10,... | collective-permute-start | bytes 1179656 | tf_op jit(solution)/shard_map/ppermute | solution.py:914
  144.7 1.2 collective-permute-start.38
  145.9 7.3 %collective-permute-start.39 = (f32[16,512]{1,0:T(8,128)S(1)}, f32[16,512]{1,0:T(8,128)S(1)}, u32[]{:S(2)}, u32[]{:S(2)}) collective-permute-start(f32[16,512]{1,0:T(8,128)S(1)} %add.87.refs_0_), channel_id=1, source_target_pairs={{0,2},{1,3},{2,0},{3,1},{4,6},{5,7},{6,4},{7,5},{8,10},{9,11},{10,... | collective-permute-start | bytes 98312 | tf_op jit(solution)/shard_map/ppermute | solution.py:919
  153.2 12.2 %collective-permute-start.40 = (f32[16,1024]{1,0:T(8,128)S(1)}, f32[16,1024]{1,0:T(8,128)S(1)}, u32[]{:S(2)}, u32[]{:S(2)}) collective-permute-start(f32[16,1024]{1,0:T(8,128)S(1)} %held.38), channel_id=1, source_target_pairs={{0,16},{4,20},{8,24},{12,28},{16,0},{20,4},{24,8},{28,12},{1,17},{... | collective-permute-start | bytes 196616 | tf_op jit(solution)/shard_map/ppermute | solution.py:919
  165.5 4.3 %collective-permute-start.41 = (f32[16,1024]{1,0:T(8,128)S(1)}, f32[16,1024]{1,0:T(8,128)S(1)}, u32[]{:S(2)}, u32[]{:S(2)}) collective-permute-start(f32[16,1024]{1,0:T(8,128)S(1)} %held.39.refs_4_), channel_id=1, source_target_pairs={{0,8},{4,12},{8,0},{12,4},{16,24},{20,28},{24,16},{28,20},{1,9},{5... | collective-permute-start | bytes 196616 | tf_op jit(solution)/shard_map/ppermute | solution.py:919
  168.9 4.2 %collective-permute-start.43 = (f32[512,1024]{1,0:T(8,128)S(1)}, f32[512,1024]{1,0:T(8,128)S(1)}, u32[]{:S(2)}, u32[]{:S(2)}) collective-permute-start(f32[512,1024]{1,0:T(8,128)S(1)} %unproject.2.refs_4_.a_ref), channel_id=1, source_target_pairs={{0,1},{1,0},{2,3},{3,2},{4,5},{5,4},{6,7},{7,6},{8,9},{9,8},{10,11... | collective-permute-start | bytes 6291464 | tf_op jit(solution)/shard_map/ppermute | solution.py:910
  171.9 6.8 %collective-permute-start.42 = (f32[512,1024]{1,0:T(8,128)S(1)}, f32[512,1024]{1,0:T(8,128)S(1)}, u32[]{:S(2)}, u32[]{:S(2)}) collective-permute-start(f32[512,1024]{1,0:T(8,128)S(1)} %unproject.3.a_ref), channel_id=1, source_target_pairs={{0,1},{1,0},{2,3},{3,2},{4,5},{5,4},{6,7},{7,6},{8,9},{9,8},{10,11... | collective-permute-start | bytes 6291464 | tf_op jit(solution)/shard_map/ppermute | solution.py:910
  172.0 4.5 %collective-permute-start.44 = (f32[16,1024]{1,0:T(8,128)S(1)}, f32[16,1024]{1,0:T(8,128)S(1)}, u32[]{:S(2)}, u32[]{:S(2)}) collective-permute-start(f32[16,1024]{1,0:T(8,128)S(1)} %add.90.refs_5_.a_ref), channel_id=1, source_target_pairs={{0,4},{4,0},{8,12},{12,8},{16,20},{20,16},{24,28},{28,24},{1,5},{5... | collective-permute-start | bytes 196616 | tf_op jit(solution)/shard_map/ppermute | solution.py:1171
  (54 other events, 254.3 us)

commit v2 on v1

--- a/solution.py
+++ b/solution.py
@@ -158,15 +158,16 @@
     return jnp.where(rows < prefix, 0.0, MASKED)
 
 
-def project_kernel(first, x_ref, vec_ref, w_ref, bias_ref, *refs):
+def project_kernel(first, x_ref, y_ref, vec_ref, w_ref, bias_ref, *refs):
+    whole = jnp.concatenate([x_ref[...], y_ref[...]], axis=1)
     if first:
         qkv_ref, normed_ref = refs[-2:]
-        hat, _ = normalize(x_ref[...].astype(f32))
+        hat, _ = normalize(whole.astype(f32))
         normed = (hat * vector(vec_ref, GAIN_ONE) + vector(vec_ref, SHIFT_ONE)).astype(bf16)
         normed_ref[...] = normed
     else:
         qkv_ref = refs[-1]
-        normed = x_ref[...]
+        normed = whole
     width = w_ref.shape[2]
     for i in range(3):
         part = nn(normed, w_ref[i]) + bias_ref[i : i + 1, :]
@@ -187,7 +188,8 @@
         functools.partial(project_kernel, first),
         grid=(length // step,),
         in_specs=[
-            block,
+            pl.BlockSpec((step, full // 2), lambda i: (i, 0)),
+            pl.BlockSpec((step, full // 2), lambda i: (i, 1)),
             once(vectors.shape, (0, 0)),
             once(weight.shape, (0, 0, 0)),
             bias_spec,
@@ -198,7 +200,7 @@
         compiler_params=params(4),
         cost_estimate=cost(6 * length * full * width, length * full * 8),
         name="project",
-    )(x, vectors, weight, bias, *after)
+    )(x, x, vectors, weight, bias, *after)
 
 
 def attend_kernel(
@@ -476,6 +478,40 @@
         out_ref[...] = buffer[...].astype(f32)
 
 
+def joined_kernel(count, which_ref, w_ref, *refs):
+    out_ref, buffer, sems = refs[-3:]
+    lead, size = w_ref.shape[0], buffer.shape[-2]
+    copies = []
+    for number in range(count):
+        rows = pl.ds(pl.multiple_of(which_ref[number] * size, size), size)
+        part = buffer.at[number * lead : (number + 1) * lead]
+        copies.append(pltpu.make_async_copy(w_ref.at[:, rows, :], part, sems.at[number]))
+        copies[-1].start()
+    for copy in copies:
+        copy.wait()
+    out_ref[...] = buffer[...].astype(f32)
+
+
+def joined(whiches, weight, after=()):
+    count, size = len(whiches), weight.shape[1] // RING
+    whole = (count * weight.shape[0], size, weight.shape[2])
+    return pl.pallas_call(
+        functools.partial(joined_kernel, count),
+        grid=(1,),
+        in_specs=[
+            pl.BlockSpec(memory_space=pltpu.SMEM),
+            pl.BlockSpec(memory_space=pltpu.HBM),
+        ]
+        + unread(after),
+        out_specs=once(whole, (0, 0, 0)),
+        out_shape=jax.ShapeDtypeStruct(whole, f32),
+        scratch_shapes=[pltpu.VMEM(whole, bf16), pltpu.SemaphoreType.DMA((count,))],
+        compiler_params=params(4),
+        cost_estimate=cost(0, whole[0] * size * whole[2] * 6),
+        name="joined",
+    )(jnp.concatenate(whiches), *in_hbm([weight]), *after)
+
+
 def picked(whiches, weights, after=()):
     shapes = [(*w.shape[:-2], w.shape[-2] // RING, w.shape[-1]) for w in weights]
     return pl.pallas_call(
@@ -510,7 +546,7 @@
             out_ref[..., rows, :] = ref[...].astype(bf16)
 
 
-def assembled(order, shifts, pieces, last_spec, folded=False, after=()):
+def assembled(order, shifts, pieces, last_specs, folded=False, after=()):
     shape = pieces[0].shape
     zeros = (0,) * len(shape)
     whole = (*shape[:-2], shape[-2] * RING, shape[-1])
@@ -518,8 +554,8 @@
         functools.partial(assemble_kernel, shifts, folded),
         grid=(1,),
         in_specs=[pl.BlockSpec(memory_space=pltpu.SMEM)]
-        + [once(shape, zeros)] * (len(pieces) - 1)
-        + [last_spec]
+        + [once(shape, zeros)] * (len(pieces) - len(last_specs))
+        + last_specs
         + unread(after),
         out_specs=once(whole, zeros),
         out_shape=jax.ShapeDtypeStruct(whole, bf16),
@@ -958,7 +994,7 @@
         for number, (up, down) in enumerate(levels[1:]):
             shifts += [-1 - number, number + 1]
             pieces += [up, down]
-        return assembled(here, shifts + [RING // 2], pieces + [facing], spec, folded, after)
+        return assembled(here, shifts + [RING // 2], pieces + [facing], [spec], folded, after)
 
     x = tokens.reshape(length, width)
     grad_out = cotangent.reshape(length, width)
@@ -1020,13 +1056,15 @@
     hop(ring_fc)
     hold(ring_proj, last(ring_out))
     hop(ring_proj)
-    across_fc, across_proj, piece_qkv, across_qkv, behind_qkv, ahead_qkv = picked(
-        [across, across, here, across, (here + RING - hops) % RING, (here + hops) % RING],
-        [fc_weight, proj_weight] + [qkv_w] * 4,
-        last(ring_out),
+    across_fc, across_proj, piece_qkv, across_qkv = picked(
+        [across, across, here, across], [fc_weight, proj_weight, qkv_w, qkv_w], last(ring_out)
+    )
+    far_places = [-hops, hops]
+    pieces_qkv = joined(
+        [(here + place + RING) % RING for place in far_places], qkv_w, [piece_qkv]
     )
     far_out = [
-        rebuilt(levels, far, parcel.part(length, parcel.piece), True, [across_qkv])
+        rebuilt(levels, far, parcel.part(length, parcel.piece), True, [pieces_qkv])
         for levels, far in zip(ring_out, far_out_parcel)
     ]
     lefts = [out] + far_out_parcel
@@ -1093,8 +1131,7 @@
         mine, keep_sums[0], feed_received, middle, vectors, q_held + facing_qkv, FAR
     )
     other_result = to_core(result)
-    behind = to_far(held([behind_qkv], [send_sums[0]])[0])
-    ahead = to_far(held([ahead_qkv], [upper])[0])
+    ends_qkv = to_far(held([pieces_qkv], [upper])[0])
 
     grads_far = heads_back(
         mine, upper, other_upper, [out_weight] + far_out, [result_token]
@@ -1111,22 +1148,24 @@
         LIGHT,
     )
 
-    for levels, *ends in zip(ring_qkv, behind, ahead):
-        levels.append(ends)
-    grad_keys, grad_vals = held(
-        [grad_keys, grad_vals],
-        behind + ahead + [piece for levels in ring_qkv for piece in levels[-2]],
-    )
+    grad_keys, grad_vals = held([grad_keys, grad_vals], last(ring_qkv))
     grad_here = jnp.concatenate([grad_keys, grad_vals], axis=1)
     flat_head = jnp.transpose(head_weight, (1, 2, 0)).reshape(2 * local_width, -1)
     trunk_here = jnp.dot(grad_here, flat_head, precision=highest)
     for_tensor = [("tensor", group, 1 << i) for i in range(group.bit_length() - 1)]
     for_dp = [("dp", copies, 1 << i) for i in reversed(range(copies.bit_length() - 1))]
     mixed, token = placed_half(theirs, other_result, mixed, [dqkv])
-    far_qkv = [
-        rebuilt(levels, piece, once(piece.shape, (0, 0, 0)), False, [token])
-        for levels, piece in zip(ring_qkv, facing_qkv)
-    ]
+    far_qkv = []
+    for levels, facing, pieces in zip(ring_qkv, facing_qkv, ends_qkv):
+        shifts, found = [0], [levels[0][0]]
+        for number, ends in enumerate(levels[1:]):
+            shifts += [-1 - number, number + 1]
+            found += list(ends)
+        shifts, found = shifts + [RING // 2], found + [facing]
+        specs = [once(piece_qkv.shape, (i, 0, 0)) for i in range(len(far_places))]
+        far_qkv.append(
+            assembled(here, shifts + far_places, found + [pieces] * len(far_places), specs, False, [token])
+        )
     qkvs = [qkv_w] + far_qkv
     trunk_here = swapped(trunk_here, *for_tensor[0])
     far_projected = [
@@ -1180,7 +1219,7 @@
         [token],
     )
     input_grad, _ = norm_one_back(
-        theirs, x, other_upper, vectors, send_one, received_two, [input_grad], [b1_grad]
+        theirs, x, other_upper, vectors, send_one, received_two, [input_grad]
     )
     b1_grad, embed_grad = b1_grad.reshape(-1), embed_grad[:prefix]
     mixed, input_grad = mixed.reshape(tokens.shape), input_grad.reshape(tokens.shape)

time: 183 us -> 178 us (0.973)
  waiting for transfers between devices: 38.8 us -> 36.2 us
  local copies, waits for them, and re-layouts: 8.96 us -> 6.84 us
    ppermute x10 -> x9, waiting for transfers between devices: 9.17 us -> 6.8 us  [to_far(): lax.ppermute(values, 'tensor', [(t, (t + shift) % group) for t in range(g...]
    pallas_call x2, Pallas kernels: 20.8 us -> 18.8 us  [attend_back(): pl.pallas_call(functools.partial(attend_back_kernel, prefix), grid=(1,),...]
    unnamed x116 -> x120, local copies, waits for them, and re-layouts: 8.25 us -> 6.73 us
    ppermute x10 -> x9, starting transfers between devices: 13.4 us -> 13.1 us  [to_far(): lax.ppermute(values, 'tensor', [(t, (t + shift) % group) for t in range(g...]
  transfers between devices with their start and end apart: 45 -> 44, of which waited for: 20 -> 19; matrix products, arithmetic and copies ran while one was open for 1% -> 1% of each run, Pallas kernels for 47% -> 48%
where the time goes in v2:
time: 178 us; the launch traced here: 177 us
  Pallas kernels  88.7 us (50%)
  starting transfers between devices  41.6 us (23%)
  waiting for transfers between devices  36.2 us (20%)
  local copies, waits for them, and re-layouts  6.84 us (4%)
  between operations  2.47 us (1%)
    ppermute x22, waiting for transfers between devices, along(): return lax.ppermute(values, 'dp', hop)  26.9 us
    ppermute x22, starting transfers between devices, along(): return lax.ppermute(values, 'dp', hop)  22.6 us
    pallas_call x4, Pallas kernels, mlp(): pl.pallas_call(functools.partial(mlp_kernel, bool(sums)), grid_spec=pltpu...  21 us
    pallas_call x2, Pallas kernels, attend_back(): pl.pallas_call(functools.partial(attend_back_kernel, prefix), grid=(1,),...  18.8 us
    ppermute x9, starting transfers between devices, to_far(): lax.ppermute(values, 'tensor', [(t, (t + shift) % group) for t in range(g...  13.1 us
    pallas_call x2, Pallas kernels, project(): pl.pallas_call(functools.partial(project_kernel, first), grid=(length //...  8.97 us
    pallas_call x1, Pallas kernels, attend(): pl.pallas_call(functools.partial(attend_kernel, prefix, parcel), grid=(1,...  7.27 us
    ppermute x9, waiting for transfers between devices, to_far(): lax.ppermute(values, 'tensor', [(t, (t + shift) % group) for t in range(g...  6.8 us
  transfers between devices with their start and end apart: 44, of which 19 were waited for; matrix products, arithmetic and copies ran while one was open for 1% of the time, Pallas kernels for 48%

profile of v2, /device:TPU:0, one launch (start us, length us, event | category | flops | bytes accessed | tf_op | source)
XLA Modules:
  0.0 177.1 jit_solution(1704358724774252026)
XLA Ops:
  1.8 3.0 %collective-permute-start = (f32[128,1024]{1,0:T(8,128)S(1)}, f32[128,1024]{1,0:T(8,128)S(1)}, u32[]{:S(2)}, u32[]{:S(2)}) collective-permute-start(f32[128,1024]{1,0:T(8,128)S(1)} %pick.4.refs_1_), channel_id=1, source_target_pairs={{0,2},{1,3},{2,0},{3,1},{4,6},{5,7},{6,4},{7,5},{8,10},{9,11},{10,... | collective-permute-start | bytes 1572872 | tf_op jit(solution)/shard_map/ppermute | solution.py:950
  5.9 1.8 %pick.7 = f32[128,1024]{1,0:T(8,128)} custom-call(s32[1]{0:T(128)} %bitcast.2.which_ref.order_ref, bf16[1024,1024]{1,0:T(8,128)(2,1)} %proj_ref.3, f32[32,1024]{1,0:T(8,128)S(1)} %pick.5.refs_1_), custom_call_target="tpu_custom_call" | custom-call | bytes 49152 | tf_op jit(solution)/shard_map/pick/pallas_call | solution.py:517
  7.7 2.0 %collective-permute-start.11 = (f32[128,1024]{1,0:T(8,128)}, f32[128,1024]{1,0:T(8,128)}, u32[]{:S(2)}, u32[]{:S(2)}) collective-permute-start(f32[128,1024]{1,0:T(8,128)} %pick.7), channel_id=1, source_target_pairs={{0,2},{1,3},{2,0},{3,1},{4,6},{5,7},{6,4},{7,5},{8,10},{9,11},{10,... | collective-permute-start | bytes 1572872 | tf_op jit(solution)/shard_map/ppermute | solution.py:950
  9.9 5.1 %project.2 = (bf16[1024,768]{1,0:T(8,128)(2,1)S(1)}, bf16[1024,1024]{1,0:T(8,128)(2,1)}) custom-call(bf16[1024,1024]{1,0:T(8,128)(2,1)} %bitcast.31, bf16[1024,1024]{1,0:T(8,128)(2,1)} %bitcast.32, f32[8,1024]{1,0:T(8,128)S(1)} %pad_convert_fusion.vec_ref, bf16[3,1024,256]{2,1,0:T(8,128)(2,1)S(1)} %bitcast.28, f32[16,256]{1,0:T(8,128)S(1)} %fusion.12.bias_ref), custom_call_target="tpu_custom_call" | custom-call | flops 100663296 | bytes 524288 | tf_op jit(solution)/shard_map/project/pallas_call | solution.py:187
  15.6 1.9 %collective-permute-done.refs_0_ = f32[128,1024]{1,0:T(8,128)S(1)} collective-permute-done((f32[128,1024]{1,0:T(8,128)S(1)}, f32[128,1024]{1,0:T(8,128)S(1)}, u32[]{:S(2)}, u32[]{:S(2)}) %collective-permute-start) | collective-permute-done | bytes 524320 | tf_op jit(solution)/shard_map/ppermute | solution.py:950
  17.6 2.1 %collective-permute-start.2 = (f32[128,1024]{1,0:T(8,128)S(1)}, f32[128,1024]{1,0:T(8,128)}, u32[]{:S(2)}, u32[]{:S(2)}) collective-permute-start(f32[128,1024]{1,0:T(8,128)S(1)} %held.19.refs_0_.refs_1_), channel_id=1, source_target_pairs={{0,8},{8,16},{16,24},{24,28},{28,20},{20,12},{12,4},{4,0},{1,9},{9... | collective-permute-start | bytes 1572872 | tf_op jit(solution)/shard_map/ppermute | solution.py:970
  20.4 2.1 %collective-permute-start.4 = (f32[32,1024]{1,0:T(8,128)S(1)}, f32[32,1024]{1,0:T(8,128)S(1)}, u32[]{:S(2)}, u32[]{:S(2)}) collective-permute-start(f32[32,1024]{1,0:T(8,128)S(1)} %held.20.refs_2_.refs_3_.refs_0_), channel_id=1, source_target_pairs={{0,8},{8,16},{16,24},{24,28},{28,20},{20,12},{12,4},{4,0},{1,9},{9... | collective-permute-start | bytes 393224 | tf_op jit(solution)/shard_map/ppermute | solution.py:970
  23.2 7.3 %attend.1 = (f32[1216,256]{1,0:T(8,128)S(1)}, f32[8,128]{1,0:T(8,128)S(1)}) custom-call(s32[8]{0:T(128)S(1)} %bitcast.41, s32[1]{0:T(128)S(6)} %copy.92.pads_ref, bf16[1024,768]{1,0:T(8,128)(2,1)S(1)} %get-tuple-element.59.refs_1_.qkv_ref, f32[32,256]{1,0:T(8,128)S(1)} %pad_maximum_fusion.1.kv_ref, f32[16,256]{1,0:T(8,128)S(1)} %fusion.12.bias_ref, ...), custom_call_target="tpu_custom_call" | custom-call | flops 67108864 | bytes 163840 | tf_op jit(solution)/shard_map/attend/pallas_call | solution.py:257
  30.5 2.2 %collective-permute-done.4.refs_3_.refs_0_ = f32[32,1024]{1,0:T(8,128)S(1)} collective-permute-done((f32[32,1024]{1,0:T(8,128)S(1)}, f32[32,1024]{1,0:T(8,128)S(1)}, u32[]{:S(2)}, u32[]{:S(2)}) %collective-permute-start.4) | collective-permute-done | bytes 131104 | tf_op jit(solution)/shard_map/ppermute | solution.py:970
  33.9 1.6 collective-permute-start.6
  35.5 1.6 collective-permute-start.12
  37.6 1.6 collective-permute-start.7
  39.7 10.9 %collective-permute-done.7.refs_3_.refs_4_ = f32[32,1024]{1,0:T(8,128)S(1)} collective-permute-done((f32[32,1024]{1,0:T(8,128)S(1)}, f32[32,1024]{1,0:T(8,128)S(1)}, u32[]{:S(2)}, u32[]{:S(2)}) %collective-permute-start.7) | collective-permute-done | bytes 131104 | tf_op jit(solution)/shard_map/ppermute | solution.py:970
  50.6 1.6 collective-permute-start.9
  52.6 1.6 collective-permute-start.14
  54.7 2.3 %collective-permute-done.9.refs_4_.refs_5_.refs_2_ = f32[32,1024]{1,0:T(8,128)S(1)} collective-permute-done((f32[32,1024]{1,0:T(8,128)S(1)}, f32[32,1024]{1,0:T(8,128)S(1)}, u32[]{:S(2)}, u32[]{:S(2)}) %collective-permute-start.9) | collective-permute-done | bytes 131104 | tf_op jit(solution)/shard_map/ppermute | solution.py:970
  57.0 1.6 collective-permute-done.10.refs_5_.refs_6_.refs_3_
  59.9 1.6 collective-permute-start.17
  63.9 1.7 pick.6
  65.7 1.6 joined.1.refs_8_.refs_0_
  68.3 1.6 collective-permute-done.15.refs_5_.refs_1_.refs_2_
  71.4 2.9 %collective-permute-done.17.refs_2_.refs_0_ = f32[128,1024]{1,0:T(8,128)} collective-permute-done((f32[128,1024]{1,0:T(8,128)}, f32[128,1024]{1,0:T(8,128)}, u32[]{:S(2)}, u32[]{:S(2)}) %collective-permute-start.17) | collective-permute-done | bytes 524320 | tf_op jit(solution)/shard_map/ppermute | solution.py:970
  75.6 1.6 collective-permute-start.19
  81.4 5.2 %mlp.4 = (f32[512,1024]{1,0:T(8,128)S(1)}, f32[512,1024]{1,0:T(8,128)S(1)}) custom-call(s32[1]{0:T(128)} %bitcast.which_ref.core_ref, f32[512,1024]{1,0:T(8,128)S(1)} %get-tuple-element.71.n_ref.refs_1_, bf16[1024,1024]{1,0:T(8,128)(2,1)S(1)} %bitcast.36, bf16[1024,1024]{1,0:T(8,128)(2,1)S(1)} %copy-done.4, bf16[1024,1024]{1,0:T(8,128)(2,1)S(1)} %copy-done.5, ...), custom_call_target="tpu_custom_call" | custom-call | flops 85899345920 | bytes 786432 | tf_op jit(solution)/shard_map/mlp/pallas_call | solution.py:700
  87.2 1.8 %collective-permute-start.23 = (f32[128,1024]{1,0:T(8,128)}, f32[128,1024]{1,0:T(8,128)S(1)}, u32[]{:S(2)}, u32[]{:S(2)}) collective-permute-start(f32[128,1024]{1,0:T(8,128)} %get-tuple-element.75.refs_3_), channel_id=1, source_target_pairs={{0,8},{8,16},{16,24},{24,28},{28,20},{20,12},{12,4},{4,0},{1,9},{9... | collective-permute-start | bytes 1572872 | tf_op jit(solution)/shard_map/ppermute | solution.py:970
  89.3 1.8 collective-permute-start.27
  91.0 5.2 %mlp.5 = (f32[512,1024]{1,0:T(8,128)S(1)}, f32[512,1024]{1,0:T(8,128)S(1)}) custom-call(s32[1]{0:T(128)S(6)} %sub.11.which_ref, f32[512,1024]{1,0:T(8,128)S(1)} %collective-permute-done.22.n_ref.refs_2_, bf16[1024,1024]{1,0:T(8,128)(2,1)S(1)} %bitcast.37, bf16[1024,1024]{1,0:T(8,128)(2,1)S(1)} %copy-done.4, bf16[1024,1024]{1,0:T(8,128)(2,1)S(1)} %copy-done.5, ...), custom_call_target="tpu_custom_call" | custom-call | flops 268435456 | bytes 786432 | tf_op jit(solution)/shard_map/mlp/pallas_call | solution.py:700
  97.7 3.9 %collective-permute-done.25.refs_7_ = f32[128,1024]{1,0:T(8,128)S(1)} collective-permute-done((f32[128,1024]{1,0:T(8,128)S(1)}, f32[128,1024]{1,0:T(8,128)S(1)}, u32[]{:S(2)}, u32[]{:S(2)}) %collective-permute-start.25) | collective-permute-done | bytes 524320 | tf_op jit(solution)/shard_map/ppermute | solution.py:950
  102.3 1.9 %assemble.6.proj_ref = bf16[1024,1024]{1,0:T(8,128)(2,1)S(1)} custom-call(s32[1]{0:T(128)} %bitcast.2.which_ref.order_ref, f32[128,1024]{1,0:T(8,128)} %held.23.refs_0_, f32[128,1024]{1,0:T(8,128)} %get-tuple-element.67.refs_1_, f32[128,1024]{1,0:T(8,128)} %get-tuple-element.68.refs_2_, f32[128,1024]{1,0:T(8,128)} %get-tuple-element.75.refs_3_, ...), custom_call_target="tpu_custom_call" | custom-call | bytes 393216 | tf_op jit(solution)/shard_map/assemble/pallas_call | solution.py:553
  104.1 5.3 %mlp.6 = (f32[512,1024]{1,0:T(8,128)S(1)}, f32[512,1024]{1,0:T(8,128)S(1)}) custom-call(s32[1]{0:T(128)S(6)} %sub.11.which_ref, f32[512,1024]{1,0:T(8,128)S(1)} %collective-permute-done.22.n_ref.refs_2_, bf16[1024,1024]{1,0:T(8,128)(2,1)S(1)} %bitcast.38, bf16[1024,1024]{1,0:T(8,128)(2,1)S(1)} %assemble.5.refs_8_.fc_ref, ...), custom_call_target="tpu_custom_call" | custom-call | flops 4294967296 | bytes 786432 | tf_op jit(solution)/shard_map/mlp/pallas_call | solution.py:700
  109.5 1.6 collective-permute-start.28
  111.6 1.7 collective-permute-start.31
  113.3 5.2 %mlp.7 = (f32[512,1024]{1,0:T(8,128)S(1)}, f32[512,1024]{1,0:T(8,128)S(1)}) custom-call(s32[1]{0:T(128)} %bitcast.which_ref.core_ref, f32[512,1024]{1,0:T(8,128)S(1)} %get-tuple-element.71.n_ref.refs_1_, bf16[1024,1024]{1,0:T(8,128)(2,1)S(1)} %bitcast.39, bf16[1024,1024]{1,0:T(8,128)(2,1)S(1)} %assemble.5.refs_8_.fc_ref, ...), custom_call_target="tpu_custom_call" | custom-call | flops 85899345920 | bytes 786432 | tf_op jit(solution)/shard_map/mlp/pallas_call | solution.py:700
  118.5 1.7 norm_two_back.1.refs_2_.keep_ref.refs_1_.upper_ref
  122.5 1.7 result.1
  124.2 1.7 collective-permute-start.36
  125.9 1.4 collective-permute-start.34
  128.1 2.3 %heads_back.1 = (bf16[1024,256]{1,0:T(8,128)(2,1)S(1)}, bf16[1024,256]{1,0:T(8,128)(2,1)S(1)}) custom-call(s32[1]{0:T(128)} %bitcast.which_ref.core_ref, f32[512,1024]{1,0:T(8,128)S(1)} %norm_two_back.1.refs_2_.keep_ref.refs_1_.upper_ref, f32[512,1024]{1,0:T(8,128)S(1)} %collective-permute-done.33.other_ref.upper_ref, bf16[256,1024]{1,0:T(8,128)(2,1)S(1)} %copy-done.10, ...), custom_call_target="tpu_custom_call" | custom-call | flops 67108864 | bytes 327680 | tf_op jit(solution)/shard_map/heads_back/pallas_call | solution.py:331
  130.4 9.2 %attend_back.2 = (bf16[1024,768]{1,0:T(8,128)(2,1)S(1)}, f32[16,256]{1,0:T(8,128)S(1)}, f32[16,256]{1,0:T(8,128)S(1)}) custom-call(s32[8]{0:T(128)S(1)} %bitcast.42, s32[1]{0:T(128)S(6)} %copy.92.pads_ref, bf16[1024,768]{1,0:T(8,128)(2,1)S(1)} %copy-done.7, bf16[1024,256]{1,0:T(8,128)(2,1)S(1)} %get-tuple-element.91.do_ref, ...), custom_call_target="tpu_custom_call" | custom-call | flops 2684354560 | bytes 655360 | tf_op jit(solution)/shard_map/attend_back/pallas_call | solution.py:412
  141.8 1.5 place.1
  144.3 3.9 %project.3.qkv_ref.refs_1_ = bf16[1024,768]{1,0:T(8,128)(2,1)S(1)} custom-call(bf16[1024,1024]{1,0:T(8,128)(2,1)} %get-tuple-element.94.x_ref.y_ref, bf16[1024,1024]{1,0:T(8,128)(2,1)} %get-tuple-element.94.x_ref.y_ref, f32[8,1024]{1,0:T(8,128)S(1)} %copy-done.28, bf16[3,1024,256]{2,1,0:T(8,128)(2,1)S(1)} %assemble.7.w_ref.refs_3_, ...), custom_call_target="tpu_custom_call" | custom-call | flops 100663296 | bytes 524288 | tf_op jit(solution)/shard_map/project/pallas_call | solution.py:187
  148.3 3.1 %collective-permute-start.39 = (f32[16,1024]{1,0:T(8,128)S(1)}, f32[16,1024]{1,0:T(8,128)S(1)}, u32[]{:S(2)}, u32[]{:S(2)}) collective-permute-start(f32[16,1024]{1,0:T(8,128)S(1)} %held.36), channel_id=1, source_target_pairs={{0,16},{4,20},{8,24},{12,28},{16,0},{20,4},{24,8},{28,12},{1,17},{... | collective-permute-start | bytes 196616 | tf_op jit(solution)/shard_map/ppermute | solution.py:955
  151.4 9.6 %attend_back.3 = (bf16[1024,768]{1,0:T(8,128)(2,1)S(1)}, f32[16,256]{1,0:T(8,128)}, f32[16,256]{1,0:T(8,128)}) custom-call(s32[8]{0:T(128)S(1)} %bitcast.43, s32[1]{0:T(128)S(6)} %copy.92.pads_ref, bf16[1024,768]{1,0:T(8,128)(2,1)S(1)} %project.3.qkv_ref.refs_1_, bf16[1024,256]{1,0:T(8,128)(2,1)S(1)} %get-tuple-element.100.do_ref, ...), custom_call_target="tpu_custom_call" | custom-call | flops 2684354560 | bytes 655360 | tf_op jit(solution)/shard_map/attend_back/pallas_call | solution.py:412
  162.4 2.0 %unproject.2.refs_4_.a_ref = f32[512,1024]{1,0:T(8,128)S(1)} custom-call(s32[1]{0:T(128)S(6)} %sub.11.which_ref, bf16[1024,768]{1,0:T(8,128)(2,1)S(1)} %get-tuple-element.92.refs_1_.refs_0_, bf16[1024,768]{1,0:T(8,128)(2,1)S(1)} %get-tuple-element.101.refs_1_, bf16[3,1024,256]{2,1,0:T(8,128)(2,1)S(1)} %bitcast.29, ...), custom_call_target="tpu_custom_call" | custom-call | flops 100663296 | bytes 262144 | tf_op jit(solution)/shard_map/unproject/pallas_call | solution.py:619
  165.4 2.0 %unproject.3.a_ref = f32[512,1024]{1,0:T(8,128)S(1)} custom-call(s32[1]{0:T(128)} %bitcast.which_ref.core_ref, bf16[1024,768]{1,0:T(8,128)(2,1)S(1)} %get-tuple-element.92.refs_1_.refs_0_, bf16[1024,768]{1,0:T(8,128)(2,1)S(1)} %get-tuple-element.101.refs_1_, bf16[3,1024,256]{2,1,0:T(8,128)(2,1)S(1)} %bitcast.30, ...), custom_call_target="tpu_custom_call" | custom-call | flops 100663296 | bytes 262144 | tf_op jit(solution)/shard_map/unproject/pallas_call | solution.py:619
  168.8 2.8 %norm_one_back.2 = (f32[1024,1024]{1,0:T(8,128)}, f32[8,128]{1,0:T(8,128)S(1)}) custom-call(s32[1]{0:T(128)} %bitcast.which_ref.core_ref, bf16[1024,1024]{1,0:T(8,128)(2,1)S(1)} %bitcast.34, f32[512,1024]{1,0:T(8,128)S(1)} %norm_two_back.1.refs_2_.keep_ref.refs_1_.upper_ref, f32[8,1024]{1,0:T(8,128)S(1)} %copy-done.28, f32[512,1024]{1,0:T(8,128)S(1)} %unproject.3.a_ref, ...), custom_call_target="tpu_custom_call" | custom-call | flops 655360 | bytes 589824 | tf_op jit(solution)/shard_map/norm_one_back/pallas_call | solution.py:772
  172.1 2.2 %prefix_grads.1 = (f32[1024,512]{1,0:T(8,128)}, f32[512,2,256]{2,1,0:T(2,128)}, f32[1,512]{1,0:T(1,128)}, f32[2,256]{1,0:T(2,128)}, f32[16,1024]{1,0:T(8,128)}) custom-call(f32[16,1024]{1,0:T(8,128)S(1)} %add.96.refs_5_.a_ref, f32[16,1024]{1,0:T(8,128)S(1)} %collective-permute-done.43.b_ref, f32[16,512]{1,0:T(8,128)S(1)} %pad.30.trunk_ref, ...), custom_call_target="tpu_custom_call" | custom-call | bytes 262144 | tf_op jit(solution)/shard_map/prefix_grads/pallas_call | solution.py:895
  174.3 2.8 %norm_one_back.3 = (f32[1024,1024]{1,0:T(8,128)}, f32[8,128]{1,0:T(8,128)}) custom-call(s32[1]{0:T(128)S(6)} %sub.11.which_ref, bf16[1024,1024]{1,0:T(8,128)(2,1)S(1)} %bitcast.35, f32[512,1024]{1,0:T(8,128)S(1)} %collective-permute-done.33.other_ref.upper_ref, f32[8,1024]{1,0:T(8,128)S(1)} %copy-done.28, ...), custom_call_target="tpu_custom_call", output_to_operand_aliasing={{0}: (6, {})} | custom-call | flops 655360 | bytes 589824 | tf_op jit(solution)/shard_map/norm_one_back/pallas_call | solution.py:772
  (236 shorter events, 31.8 us)
Async XLA Ops:
  1.8 15.8 %collective-permute-start = (f32[128,1024]{1,0:T(8,128)S(1)}, f32[128,1024]{1,0:T(8,128)S(1)}, u32[]{:S(2)}, u32[]{:S(2)}) collective-permute-start(f32[128,1024]{1,0:T(8,128)S(1)} %pick.4.refs_1_), channel_id=1, source_target_pairs={{0,2},{1,3},{2,0},{3,1},{4,6},{5,7},{6,4},{7,5},{8,10},{9,11},{10,... | collective-permute-start | bytes 1572872 | tf_op jit(solution)/shard_map/ppermute | solution.py:950
  5.7 14.7 %collective-permute-start.1 = (f32[32,1024]{1,0:T(8,128)S(1)}, f32[32,1024]{1,0:T(8,128)S(1)}, u32[]{:S(2)}, u32[]{:S(2)}) collective-permute-start(f32[32,1024]{1,0:T(8,128)S(1)} %pick.5.refs_1_), channel_id=1, source_target_pairs={{0,2},{1,3},{2,0},{3,1},{4,6},{5,7},{6,4},{7,5},{8,10},{9,11},{10,... | collective-permute-start | bytes 393224 | tf_op jit(solution)/shard_map/ppermute | solution.py:950
  7.7 27.8 %collective-permute-start.11 = (f32[128,1024]{1,0:T(8,128)}, f32[128,1024]{1,0:T(8,128)}, u32[]{:S(2)}, u32[]{:S(2)}) collective-permute-start(f32[128,1024]{1,0:T(8,128)} %pick.7), channel_id=1, source_target_pairs={{0,2},{1,3},{2,0},{3,1},{4,6},{5,7},{6,4},{7,5},{8,10},{9,11},{10,... | collective-permute-start | bytes 1572872 | tf_op jit(solution)/shard_map/ppermute | solution.py:950
  17.6 16.3 %collective-permute-start.2 = (f32[128,1024]{1,0:T(8,128)S(1)}, f32[128,1024]{1,0:T(8,128)}, u32[]{:S(2)}, u32[]{:S(2)}) collective-permute-start(f32[128,1024]{1,0:T(8,128)S(1)} %held.19.refs_0_.refs_1_), channel_id=1, source_target_pairs={{0,8},{8,16},{16,24},{24,28},{28,20},{20,12},{12,4},{4,0},{1,9},{9... | collective-permute-start | bytes 1572872 | tf_op jit(solution)/shard_map/ppermute | solution.py:970
  19.7 14.2 %collective-permute-start.3 = (f32[128,1024]{1,0:T(8,128)S(1)}, f32[128,1024]{1,0:T(8,128)}, u32[]{:S(2)}, u32[]{:S(2)}) collective-permute-start(f32[128,1024]{1,0:T(8,128)S(1)} %held.19.refs_0_.refs_1_), channel_id=1, source_target_pairs={{0,4},{8,0},{16,8},{24,16},{28,24},{20,28},{12,20},{4,12},{1,5},{9... | collective-permute-start | bytes 1572872 | tf_op jit(solution)/shard_map/ppermute | solution.py:970
  20.3 13.6 %copy-start.8 = (bf16[256,1024]{1,0:T(8,128)(2,1)S(1)}, bf16[256,1024]{1,0:T(8,128)(2,1)}, u32[]{:S(2)}) copy-start(bf16[256,1024]{1,0:T(8,128)(2,1)} %refs_0_.9) | copy-start | bytes 1572868
  20.4 13.5 %copy-start.24 = (f32[32,1024]{1,0:T(8,128)}, f32[32,1024]{1,0:T(8,128)S(1)}, u32[]{:S(2)}) copy-start(f32[32,1024]{1,0:T(8,128)S(1)} %held.20.refs_2_.refs_3_.refs_0_) | copy-start | bytes 393220
  20.4 12.3 %collective-permute-start.4 = (f32[32,1024]{1,0:T(8,128)S(1)}, f32[32,1024]{1,0:T(8,128)S(1)}, u32[]{:S(2)}, u32[]{:S(2)}) collective-permute-start(f32[32,1024]{1,0:T(8,128)S(1)} %held.20.refs_2_.refs_3_.refs_0_), channel_id=1, source_target_pairs={{0,8},{8,16},{16,24},{24,28},{28,20},{20,12},{12,4},{4,0},{1,9},{9... | collective-permute-start | bytes 393224 | tf_op jit(solution)/shard_map/ppermute | solution.py:970
  22.5 11.4 %collective-permute-start.5 = (f32[32,1024]{1,0:T(8,128)S(1)}, f32[32,1024]{1,0:T(8,128)S(1)}, u32[]{:S(2)}, u32[]{:S(2)}) collective-permute-start(f32[32,1024]{1,0:T(8,128)S(1)} %held.20.refs_2_.refs_3_.refs_0_), channel_id=1, source_target_pairs={{0,4},{8,0},{16,8},{24,16},{28,24},{20,28},{12,20},{4,12},{1,5},{9... | collective-permute-start | bytes 393224 | tf_op jit(solution)/shard_map/ppermute | solution.py:970
  33.9 33.5 %collective-permute-start.6 = (f32[1216,256]{1,0:T(8,128)S(1)}, f32[1216,256]{1,0:T(8,128)S(1)}, u32[]{:S(2)}, u32[]{:S(2)}) collective-permute-start(f32[1216,256]{1,0:T(8,128)S(1)} %held.21.refs_2_.refs_0_.kv_ref.lse_ref), channel_id=1, source_target_pairs={{0,2},{1,3},{2,0},{3,1},{4,6},{5,7},{6,4},{7,5},{8,10},{9,11},{10,... | collective-permute-start | bytes 3735560 | tf_op jit(solution)/shard_map/ppermute | solution.py:950
  35.5 17.1 %copy-start.22 = (f32[32,1024]{1,0:T(8,128)}, f32[32,1024]{1,0:T(8,128)S(1)}, u32[]{:S(2)}) copy-start(f32[32,1024]{1,0:T(8,128)S(1)} %get-tuple-element.63.refs_2_) | copy-start | bytes 393220
  35.5 18.7 %copy-start.20 = (f32[32,1024]{1,0:T(8,128)}, f32[32,1024]{1,0:T(8,128)S(1)}, u32[]{:S(2)}) copy-start(f32[32,1024]{1,0:T(8,128)S(1)} %get-tuple-element.62.refs_1_) | copy-start | bytes 393220
  35.5 17.1 %collective-permute-start.12 = (f32[128,1024]{1,0:T(8,128)}, f32[128,1024]{1,0:T(8,128)}, u32[]{:S(2)}, u32[]{:S(2)}) collective-permute-start(f32[128,1024]{1,0:T(8,128)} %held.23.refs_0_), channel_id=1, source_target_pairs={{0,8},{8,16},{16,24},{24,28},{28,20},{20,12},{12,4},{4,0},{1,9},{9... | collective-permute-start | bytes 1572872 | tf_op jit(solution)/shard_map/ppermute | solution.py:970
  37.2 15.5 %collective-permute-start.13 = (f32[128,1024]{1,0:T(8,128)}, f32[128,1024]{1,0:T(8,128)}, u32[]{:S(2)}, u32[]{:S(2)}) collective-permute-start(f32[128,1024]{1,0:T(8,128)} %held.23.refs_0_), channel_id=1, source_target_pairs={{0,4},{8,0},{16,8},{24,16},{28,24},{20,28},{12,20},{4,12},{1,5},{9... | collective-permute-start | bytes 1572872 | tf_op jit(solution)/shard_map/ppermute | solution.py:970
  37.6 13.0 %collective-permute-start.7 = (f32[32,1024]{1,0:T(8,128)S(1)}, f32[32,1024]{1,0:T(8,128)S(1)}, u32[]{:S(2)}, u32[]{:S(2)}) collective-permute-start(f32[32,1024]{1,0:T(8,128)S(1)} %get-tuple-element.62.refs_1_), channel_id=1, source_target_pairs={{0,8},{8,16},{16,24},{24,28},{28,20},{20,12},{12,4},{4,0},{1,9},{9... | collective-permute-start | bytes 393224 | tf_op jit(solution)/shard_map/ppermute | solution.py:970
  39.2 13.0 %collective-permute-start.8 = (f32[32,1024]{1,0:T(8,128)S(1)}, f32[32,1024]{1,0:T(8,128)S(1)}, u32[]{:S(2)}, u32[]{:S(2)}) collective-permute-start(f32[32,1024]{1,0:T(8,128)S(1)} %get-tuple-element.63.refs_2_), channel_id=1, source_target_pairs={{0,4},{8,0},{16,8},{24,16},{28,24},{20,28},{12,20},{4,12},{1,5},{9... | collective-permute-start | bytes 393224 | tf_op jit(solution)/shard_map/ppermute | solution.py:970
  50.6 6.4 %collective-permute-start.9 = (f32[32,1024]{1,0:T(8,128)S(1)}, f32[32,1024]{1,0:T(8,128)S(1)}, u32[]{:S(2)}, u32[]{:S(2)}) collective-permute-start(f32[32,1024]{1,0:T(8,128)S(1)} %collective-permute-done.7.refs_3_.refs_4_), channel_id=1, source_target_pairs={{0,8},{8,16},{16,24},{24,28},{28,20},{20,12},{12,4},{4,0},{1,9},{9... | collective-permute-start | bytes 393224 | tf_op jit(solution)/shard_map/ppermute | solution.py:970
  52.2 6.4 %collective-permute-start.10 = (f32[32,1024]{1,0:T(8,128)S(1)}, f32[32,1024]{1,0:T(8,128)S(1)}, u32[]{:S(2)}, u32[]{:S(2)}) collective-permute-start(f32[32,1024]{1,0:T(8,128)S(1)} %collective-permute-done.8.refs_4_.refs_5_), channel_id=1, source_target_pairs={{0,4},{8,0},{16,8},{24,16},{28,24},{20,28},{12,20},{4,12},{1,5},{9... | collective-permute-start | bytes 393224 | tf_op jit(solution)/shard_map/ppermute | solution.py:970
  52.6 15.6 %collective-permute-start.14 = (f32[128,1024]{1,0:T(8,128)}, f32[128,1024]{1,0:T(8,128)S(1)}, u32[]{:S(2)}, u32[]{:S(2)}) collective-permute-start(f32[128,1024]{1,0:T(8,128)} %get-tuple-element.65.refs_1_), channel_id=1, source_target_pairs={{0,8},{8,16},{16,24},{24,28},{28,20},{20,12},{12,4},{4,0},{1,9},{9... | collective-permute-start | bytes 1572872 | tf_op jit(solution)/shard_map/ppermute | solution.py:970
  54.3 15.6 %collective-permute-start.15 = (f32[128,1024]{1,0:T(8,128)}, f32[128,1024]{1,0:T(8,128)S(1)}, u32[]{:S(2)}, u32[]{:S(2)}) collective-permute-start(f32[128,1024]{1,0:T(8,128)} %get-tuple-element.66.refs_2_), channel_id=1, source_target_pairs={{0,4},{8,0},{16,8},{24,16},{28,24},{20,28},{12,20},{4,12},{1,5},{9... | collective-permute-start | bytes 1572872 | tf_op jit(solution)/shard_map/ppermute | solution.py:970
  59.9 14.3 %collective-permute-start.17 = (f32[128,1024]{1,0:T(8,128)}, f32[128,1024]{1,0:T(8,128)}, u32[]{:S(2)}, u32[]{:S(2)}) collective-permute-start(f32[128,1024]{1,0:T(8,128)} %get-tuple-element.67.refs_1_), channel_id=1, source_target_pairs={{0,8},{8,16},{16,24},{24,28},{28,20},{20,12},{12,4},{4,0},{1,9},{9... | collective-permute-start | bytes 1572872 | tf_op jit(solution)/shard_map/ppermute | solution.py:970
  61.5 14.1 %collective-permute-start.18 = (f32[128,1024]{1,0:T(8,128)}, f32[128,1024]{1,0:T(8,128)}, u32[]{:S(2)}, u32[]{:S(2)}) collective-permute-start(f32[128,1024]{1,0:T(8,128)} %get-tuple-element.68.refs_2_), channel_id=1, source_target_pairs={{0,4},{8,0},{16,8},{24,16},{28,24},{20,28},{12,20},{4,12},{1,5},{9... | collective-permute-start | bytes 1572872 | tf_op jit(solution)/shard_map/ppermute | solution.py:970
  70.8 7.8 %collective-permute-start.16 = (f32[512,1024]{1,0:T(8,128)S(1)}, f32[512,1024]{1,0:T(8,128)S(1)}, u32[]{:S(2)}, u32[]{:S(2)}) collective-permute-start(f32[512,1024]{1,0:T(8,128)S(1)} %half_product.2.refs_4_), channel_id=1, source_target_pairs={{0,1},{1,0},{2,3},{3,2},{4,5},{5,4},{6,7},{7,6},{8,9},{9,8},{10,11... | collective-permute-start | bytes 6291464 | tf_op jit(solution)/shard_map/ppermute | solution.py:946
  70.8 15.8 %collective-permute-start.21 = (f32[128,1024]{1,0:T(8,128)S(1)}, f32[128,1024]{1,0:T(8,128)S(1)}, u32[]{:S(2)}, u32[]{:S(2)}) collective-permute-start(f32[128,1024]{1,0:T(8,128)S(1)} %held.27), channel_id=1, source_target_pairs={{0,2},{1,3},{2,0},{3,1},{4,6},{5,7},{6,4},{7,5},{8,10},{9,11},{10,... | collective-permute-start | bytes 1572872 | tf_op jit(solution)/shard_map/ppermute | solution.py:950
  75.6 13.7 %collective-permute-start.19 = (f32[128,1024]{1,0:T(8,128)S(1)}, f32[128,1024]{1,0:T(8,128)S(1)}, u32[]{:S(2)}, u32[]{:S(2)}) collective-permute-start(f32[128,1024]{1,0:T(8,128)S(1)} %get-tuple-element.69.refs_0_.refs_3_), channel_id=1, source_target_pairs={{0,8},{8,16},{16,24},{24,28},{28,20},{20,12},{12,4},{4,0},{1,9},{9... | collective-permute-start | bytes 1572872 | tf_op jit(solution)/shard_map/ppermute | solution.py:970
  77.2 13.9 %collective-permute-start.20 = (f32[128,1024]{1,0:T(8,128)S(1)}, f32[128,1024]{1,0:T(8,128)S(1)}, u32[]{:S(2)}, u32[]{:S(2)}) collective-permute-start(f32[128,1024]{1,0:T(8,128)S(1)} %get-tuple-element.70.refs_1_.refs_4_), channel_id=1, source_target_pairs={{0,4},{8,0},{16,8},{24,16},{28,24},{20,28},{12,20},{4,12},{1,5},{9... | collective-permute-start | bytes 1572872 | tf_op jit(solution)/shard_map/ppermute | solution.py:970
  80.0 7.2 %collective-permute-start.22 = (f32[512,1024]{1,0:T(8,128)S(1)}, f32[512,1024]{1,0:T(8,128)S(1)}, u32[]{:S(2)}, u32[]{:S(2)}) collective-permute-start(f32[512,1024]{1,0:T(8,128)S(1)} %get-tuple-element.71.n_ref.refs_1_), channel_id=1, source_target_pairs={{0,1},{1,0},{2,3},{3,2},{4,5},{5,4},{6,7},{7,6},{8,9},{9,8},{10,11... | collective-permute-start | bytes 6291464 | tf_op jit(solution)/shard_map/ppermute | solution.py:946
  86.6 14.9 %collective-permute-start.25 = (f32[128,1024]{1,0:T(8,128)S(1)}, f32[128,1024]{1,0:T(8,128)S(1)}, u32[]{:S(2)}, u32[]{:S(2)}) collective-permute-start(f32[128,1024]{1,0:T(8,128)S(1)} %held.29), channel_id=1, source_target_pairs={{0,2},{1,3},{2,0},{3,1},{4,6},{5,7},{6,4},{7,5},{8,10},{9,11},{10,... | collective-permute-start | bytes 1572872 | tf_op jit(solution)/shard_map/ppermute | solution.py:950
  87.2 14.4 %collective-permute-start.23 = (f32[128,1024]{1,0:T(8,128)}, f32[128,1024]{1,0:T(8,128)S(1)}, u32[]{:S(2)}, u32[]{:S(2)}) collective-permute-start(f32[128,1024]{1,0:T(8,128)} %get-tuple-element.75.refs_3_), channel_id=1, source_target_pairs={{0,8},{8,16},{16,24},{24,28},{28,20},{20,12},{12,4},{4,0},{1,9},{9... | collective-permute-start | bytes 1572872 | tf_op jit(solution)/shard_map/ppermute | solution.py:970
  89.0 13.3 %collective-permute-start.24 = (f32[128,1024]{1,0:T(8,128)}, f32[128,1024]{1,0:T(8,128)S(1)}, u32[]{:S(2)}, u32[]{:S(2)}) collective-permute-start(f32[128,1024]{1,0:T(8,128)} %get-tuple-element.76.refs_4_), channel_id=1, source_target_pairs={{0,4},{8,0},{16,8},{24,16},{28,24},{20,28},{12,20},{4,12},{1,5},{9... | collective-permute-start | bytes 1572872 | tf_op jit(solution)/shard_map/ppermute | solution.py:970
  89.3 20.2 %collective-permute-start.27 = (f32[3,128,256]{2,1,0:T(8,128)S(1)}, f32[3,128,256]{2,1,0:T(8,128)S(1)}, u32[]{:S(2)}, u32[]{:S(2)}) collective-permute-start(f32[3,128,256]{2,1,0:T(8,128)S(1)} %held.30), channel_id=1, source_target_pairs={{0,2},{1,3},{2,0},{3,1},{4,6},{5,7},{6,4},{7,5},{8,10},{9,11},{10,... | collective-permute-start | bytes 1179656 | tf_op jit(solution)/shard_map/ppermute | solution.py:950
  109.4 13.1 %collective-permute-start.26 = (f32[512,1024]{1,0:T(8,128)S(1)}, f32[512,1024]{1,0:T(8,128)S(1)}, u32[]{:S(2)}, u32[]{:S(2)}) collective-permute-start(f32[512,1024]{1,0:T(8,128)S(1)} %get-tuple-element.80.refs_2_), channel_id=1, source_target_pairs={{0,1},{1,0},{2,3},{3,2},{4,5},{5,4},{6,7},{7,6},{8,9},{9,8},{10,11... | collective-permute-start | bytes 6291464 | tf_op jit(solution)/shard_map/ppermute | solution.py:946
  109.5 11.5 %collective-permute-start.28 = (f32[3,128,256]{2,1,0:T(8,128)S(1)}, f32[3,128,256]{2,1,0:T(8,128)S(1)}, u32[]{:S(2)}, u32[]{:S(2)}) collective-permute-start(f32[3,128,256]{2,1,0:T(8,128)S(1)} %held.31.refs_0_), channel_id=1, source_target_pairs={{0,8},{8,16},{16,24},{24,28},{28,20},{20,12},{12,4},{4,0},{1,9},{9... | collective-permute-start | bytes 1179656 | tf_op jit(solution)/shard_map/ppermute | solution.py:970
  111.1 11.3 %collective-permute-start.29 = (f32[3,128,256]{2,1,0:T(8,128)S(1)}, f32[3,128,256]{2,1,0:T(8,128)S(1)}, u32[]{:S(2)}, u32[]{:S(2)}) collective-permute-start(f32[3,128,256]{2,1,0:T(8,128)S(1)} %held.31.refs_0_), channel_id=1, source_target_pairs={{0,4},{8,0},{16,8},{24,16},{28,24},{20,28},{12,20},{4,12},{1,5},{9... | collective-permute-start | bytes 1179656 | tf_op jit(solution)/shard_map/ppermute | solution.py:970
  111.6 10.9 %collective-permute-start.31 = (f32[3,128,256]{2,1,0:T(8,128)S(1)}, f32[3,128,256]{2,1,0:T(8,128)S(1)}, u32[]{:S(2)}, u32[]{:S(2)}) collective-permute-start(f32[3,128,256]{2,1,0:T(8,128)S(1)} %held.33), channel_id=1, source_target_pairs={{0,2},{1,3},{2,0},{3,1},{4,6},{5,7},{6,4},{7,5},{8,10},{9,11},{10,... | collective-permute-start | bytes 1179656 | tf_op jit(solution)/shard_map/ppermute | solution.py:950
  113.3 5.3 %collective-permute-start.30 = (f32[512,1024]{1,0:T(8,128)S(1)}, f32[512,1024]{1,0:T(8,128)S(1)}, u32[]{:S(2)}, u32[]{:S(2)}) collective-permute-start(f32[512,1024]{1,0:T(8,128)S(1)} %get-tuple-element.84), channel_id=1, source_target_pairs={{0,1},{1,0},{2,3},{3,2},{4,5},{5,4},{6,7},{7,6},{8,9},{9,8},{10,11... | collective-permute-start | bytes 6291464 | tf_op jit(solution)/shard_map/ppermute | solution.py:946
  120.2 7.8 %collective-permute-start.33 = (f32[512,1024]{1,0:T(8,128)S(1)}, f32[512,1024]{1,0:T(8,128)S(1)}, u32[]{:S(2)}, u32[]{:S(2)}) collective-permute-start(f32[512,1024]{1,0:T(8,128)S(1)} %norm_two_back.1.refs_2_.keep_ref.refs_1_.upper_ref), channel_id=1, source_target_pairs={{0,1},{1,0},{2,3},{3,2},{4,5},{5,4},{6,7},{7,6},{8,9},{9,8},{10,11... | collective-permute-start | bytes 6291464 | tf_op jit(solution)/shard_map/ppermute | solution.py:946
  124.2 17.6 %collective-permute-start.32 = (f32[512,1024]{1,0:T(8,128)S(1)}, f32[512,1024]{1,0:T(8,128)S(1)}, u32[]{:S(2)}, u32[]{:S(2)}) collective-permute-start(f32[512,1024]{1,0:T(8,128)S(1)} %get-tuple-element.88), channel_id=1, source_target_pairs={{0,1},{1,0},{2,3},{3,2},{4,5},{5,4},{6,7},{7,6},{8,9},{9,8},{10,11... | collective-permute-start | bytes 6291464 | tf_op jit(solution)/shard_map/ppermute | solution.py:946
  124.2 19.9 %collective-permute-start.36 = (f32[6,128,256]{2,1,0:T(8,128)S(1)}, f32[6,128,256]{2,1,0:T(8,128)S(1)}, u32[]{:S(2)}, u32[]{:S(2)}) collective-permute-start(f32[6,128,256]{2,1,0:T(8,128)S(1)} %held.34), channel_id=1, source_target_pairs={{0,2},{1,3},{2,0},{3,1},{4,6},{5,7},{6,4},{7,5},{8,10},{9,11},{10,... | collective-permute-start | bytes 2359304 | tf_op jit(solution)/shard_map/ppermute | solution.py:950
  125.9 13.7 %collective-permute-start.34 = (f32[3,128,256]{2,1,0:T(8,128)S(1)}, f32[3,128,256]{2,1,0:T(8,128)S(1)}, u32[]{:S(2)}, u32[]{:S(2)}) collective-permute-start(f32[3,128,256]{2,1,0:T(8,128)S(1)} %get-tuple-element.85.refs_0_.refs_1_), channel_id=1, source_target_pairs={{0,8},{8,16},{16,24},{24,28},{28,20},{20,12},{12,4},{4,0},{1,9},{9... | collective-permute-start | bytes 1179656 | tf_op jit(solution)/shard_map/ppermute | solution.py:970
  127.4 12.3 %collective-permute-start.35 = (f32[3,128,256]{2,1,0:T(8,128)S(1)}, f32[3,128,256]{2,1,0:T(8,128)S(1)}, u32[]{:S(2)}, u32[]{:S(2)}) collective-permute-start(f32[3,128,256]{2,1,0:T(8,128)S(1)} %get-tuple-element.86.refs_1_.refs_2_), channel_id=1, source_target_pairs={{0,4},{8,0},{16,8},{24,16},{28,24},{20,28},{12,20},{4,12},{1,5},{9... | collective-permute-start | bytes 1179656 | tf_op jit(solution)/shard_map/ppermute | solution.py:970
  140.2 1.2 collective-permute-start.37
  141.4 6.8 %collective-permute-start.38 = (f32[16,512]{1,0:T(8,128)S(1)}, f32[16,512]{1,0:T(8,128)S(1)}, u32[]{:S(2)}, u32[]{:S(2)}) collective-permute-start(f32[16,512]{1,0:T(8,128)S(1)} %add.93.refs_0_), channel_id=1, source_target_pairs={{0,2},{1,3},{2,0},{3,1},{4,6},{5,7},{6,4},{7,5},{8,10},{9,11},{10,... | collective-permute-start | bytes 98312 | tf_op jit(solution)/shard_map/ppermute | solution.py:955
  148.3 12.8 %collective-permute-start.39 = (f32[16,1024]{1,0:T(8,128)S(1)}, f32[16,1024]{1,0:T(8,128)S(1)}, u32[]{:S(2)}, u32[]{:S(2)}) collective-permute-start(f32[16,1024]{1,0:T(8,128)S(1)} %held.36), channel_id=1, source_target_pairs={{0,16},{4,20},{8,24},{12,28},{16,0},{20,4},{24,8},{28,12},{1,17},{... | collective-permute-start | bytes 196616 | tf_op jit(solution)/shard_map/ppermute | solution.py:955
  161.1 4.3 %collective-permute-start.40 = (f32[16,1024]{1,0:T(8,128)S(1)}, f32[16,1024]{1,0:T(8,128)S(1)}, u32[]{:S(2)}, u32[]{:S(2)}) collective-permute-start(f32[16,1024]{1,0:T(8,128)S(1)} %held.37.refs_4_), channel_id=1, source_target_pairs={{0,8},{4,12},{8,0},{12,4},{16,24},{20,28},{24,16},{28,20},{1,9},{5... | collective-permute-start | bytes 196616 | tf_op jit(solution)/shard_map/ppermute | solution.py:955
  164.5 4.3 %collective-permute-start.42 = (f32[512,1024]{1,0:T(8,128)S(1)}, f32[512,1024]{1,0:T(8,128)S(1)}, u32[]{:S(2)}, u32[]{:S(2)}) collective-permute-start(f32[512,1024]{1,0:T(8,128)S(1)} %unproject.2.refs_4_.a_ref), channel_id=1, source_target_pairs={{0,1},{1,0},{2,3},{3,2},{4,5},{5,4},{6,7},{7,6},{8,9},{9,8},{10,11... | collective-permute-start | bytes 6291464 | tf_op jit(solution)/shard_map/ppermute | solution.py:946
  167.5 6.8 %collective-permute-start.41 = (f32[512,1024]{1,0:T(8,128)S(1)}, f32[512,1024]{1,0:T(8,128)S(1)}, u32[]{:S(2)}, u32[]{:S(2)}) collective-permute-start(f32[512,1024]{1,0:T(8,128)S(1)} %unproject.3.a_ref), channel_id=1, source_target_pairs={{0,1},{1,0},{2,3},{3,2},{4,5},{5,4},{6,7},{7,6},{8,9},{9,8},{10,11... | collective-permute-start | bytes 6291464 | tf_op jit(solution)/shard_map/ppermute | solution.py:946
  167.6 4.5 %collective-permute-start.43 = (f32[16,1024]{1,0:T(8,128)S(1)}, f32[16,1024]{1,0:T(8,128)S(1)}, u32[]{:S(2)}, u32[]{:S(2)}) collective-permute-start(f32[16,1024]{1,0:T(8,128)S(1)} %add.96.refs_5_.a_ref), channel_id=1, source_target_pairs={{0,4},{4,0},{8,12},{12,8},{16,20},{20,16},{24,28},{28,24},{1,5},{5... | collective-permute-start | bytes 196616 | tf_op jit(solution)/shard_map/ppermute | solution.py:1210
  (55 other events, 244.8 us)

commit v3 on v2

--- a/solution.py
+++ b/solution.py
@@ -723,6 +723,91 @@
     )(which, normed, cotangent, fc, proj, bias, *sums, *after)
 
 
+def front_kernel(n_ref, fc_ref, bias_ref, *refs):
+    act_ref, slope_ref = refs[-2:]
+    normed = n_ref[...].astype(bf16)
+    units, step = fc_ref.shape[1], bias_ref.shape[1]
+    for number, at in enumerate(range(0, units, step)):
+        cols = slice(at, at + step)
+        hidden = nn(normed, fc_ref[:, cols]) + bias_ref[number : number + 1, :]
+        square = hidden * hidden
+        inner = jnp.tanh(hidden * (0.7978845608028654 + 0.7978845608028654 * 0.044715 * square))
+        gate = 0.5 + 0.5 * inner
+        act_ref[:, cols] = (hidden * gate).astype(bf16)
+        slope_ref[:, cols] = gate + (0.5 * hidden) * (1.0 - inner * inner) * (
+            0.7978845608028654 + 3.0 * 0.7978845608028654 * 0.044715 * square
+        )
+
+
+def front(normed, fc, bias, bias_spec, after=()):
+    half, width = normed.shape
+    units = fc.shape[1]
+    step = 256
+    block = pl.BlockSpec((step, units), lambda i: (i, 0))
+    return pl.pallas_call(
+        front_kernel,
+        grid=(half // step,),
+        in_specs=[
+            pl.BlockSpec((step, width), lambda i: (i, 0)),
+            once(fc.shape, (0, 0)),
+            bias_spec,
+        ]
+        + unread(after),
+        out_specs=[block] * 2,
+        out_shape=[
+            jax.ShapeDtypeStruct((half, units), bf16),
+            jax.ShapeDtypeStruct((half, units), f32),
+        ],
+        compiler_params=params(10),
+        cost_estimate=cost(2 * half * width * units, half * width * 10, half * units),
+        name="mlp_front",
+    )(normed, fc, bias, *after)
+
+
+def rest_kernel(which_ref, act_ref, slope_ref, g_ref, fc_ref, proj_ref, *refs):
+    feed_in, back_in = refs[:2]
+    feed_ref, back_ref, grad_ref = refs[-3:]
+    grad = g_ref[...]
+    units = fc_ref.shape[1]
+    step = min(units, 256)
+    for at in range(0, units, step):
+        cols = slice(at, at + step)
+        grad_ref[:, cols] = (nt(grad, proj_ref[cols, :]) * slope_ref[:, cols]).astype(bf16)
+    feed_ref[...] = nn(act_ref[...], proj_ref[...]) + feed_in[...]
+    back_ref[...] = nt(grad_ref[...], fc_ref[...]) + back_in[...]
+
+
+def rest(which, fronts, cotangent, fc, proj, sums, after=(), weight=1):
+    half, units = fronts[0].shape
+    width = fc.shape[0]
+    step = 256
+    count = half // step
+    block = pl.BlockSpec((step, width), lambda i, w: (i, 0))
+    return pl.pallas_call(
+        rest_kernel,
+        grid_spec=pltpu.PrefetchScalarGridSpec(
+            num_scalar_prefetch=1,
+            grid=(count,),
+            in_specs=[pl.BlockSpec((step, units), lambda i, w: (i, 0))] * 2
+            + [
+                pl.BlockSpec((step, width), lambda i, w: (w[0] * count + i, 0)),
+                once(fc.shape, (0, 0)),
+                once(proj.shape, (0, 0)),
+            ]
+            + [block] * 2
+            + unread(after),
+            out_specs=[block] * 2,
+            scratch_shapes=[pltpu.VMEM((step, units), bf16)],
+        ),
+        out_shape=[jax.ShapeDtypeStruct((half, width), f32)] * 2,
+        compiler_params=params(14),
+        cost_estimate=cost(
+            weight * 6 * half * width * units, half * width * 16 + 4 * width * units
+        ),
+        name="mlp_rest",
+    )(which, *fronts, cotangent, fc, proj, *sums, *after)
+
+
 def norm_two_back_kernel(which_ref, g_ref, a_ref, b_ref, middle_ref, vec_ref, *refs):
     hat, scale = normalize(middle_ref[...])
     grad = (a_ref[...] + b_ref[...]) * vector(vec_ref, GAIN_TWO)
@@ -1095,29 +1180,20 @@
         rebuilt(levels, piece, fc_spec, False, [send_sums[0]])
         for levels, piece in zip(ring_fc, facing_fc)
     ]
+    far_bias_spec = parcel.part(parcel.bias + 8, 8)
+    other_fronts, fronts = [], []
+    for fc, far in zip(far_fc, far_out_parcel):
+        other_fronts.append(front(other_normed, fc, far, far_bias_spec))
+        fronts.append(front(normed, fc, far, far_bias_spec, other_fronts[-1][:1]))
     far_proj = [
-        rebuilt(levels, piece, proj_spec, False, far_fc)
+        rebuilt(levels, piece, proj_spec, False, [ahead[1] for ahead in fronts])
         for levels, piece in zip(ring_proj, facing_proj)
     ]
-    far_bias_spec = parcel.part(parcel.bias + 8, 8)
-    for fc, proj, far in zip(far_fc, far_proj, far_out_parcel):
-        send_sums = mlp(
-            theirs, other_normed, grad_out, fc, proj, far, far_bias_spec, send_sums, (), LIGHT
-        )
+    for ahead, fc, proj in zip(other_fronts, far_fc, far_proj):
+        send_sums = rest(theirs, ahead, grad_out, fc, proj, send_sums, (), LIGHT)
     back_received = to_core(send_sums[1])
-    for fc, proj, far in zip(far_fc, far_proj, far_out_parcel):
-        keep_sums = mlp(
-            mine,
-            normed,
-            grad_out,
-            fc,
-            proj,
-            far,
-            far_bias_spec,
-            keep_sums,
-            [send_sums[0]],
-            FAR,
-        )
+    for ahead, fc, proj in zip(fronts, far_fc, far_proj):
+        keep_sums = rest(mine, ahead, grad_out, fc, proj, keep_sums, [send_sums[0]], FAR)
     facing_qkv = to_far(held([across_qkv], near_qkv + [send_sums[0]])[0])
     upper = norm_two_back(
         mine, grad_out, keep_sums[1], back_received, middle, vectors

time: 178 us -> 176 us (0.989)
  Pallas kernels: 88.7 us -> 91.8 us
  waiting for transfers between devices: 36.2 us -> 33.6 us
  local copies, waits for them, and re-layouts: 6.84 us -> 4.88 us
    pallas_call x0 -> x4, Pallas kernels: none -> 12.5 us  [the longest x2 7.51 us: rest(): pl.pallas_call(rest_kernel, grid_spec=pltpu.PrefetchScalarGridSpec(num_sc...]
    pallas_call x4 -> x2, Pallas kernels: 21 us -> 10.5 us  [mlp(): pl.pallas_call(functools.partial(mlp_kernel, bool(sums)), grid_spec=pltpu...]
    ppermute x9, waiting for transfers between devices: 6.8 us -> 3.25 us  [to_far(): lax.ppermute(values, 'tensor', [(t, (t + shift) % group) for t in range(g...]
    ppermute x8, waiting for transfers between devices: 0.02 us -> 2.94 us  [to_core(): return lax.ppermute(values, 'tensor', [(t, t ^ 1) for t in range(group)])]
    unnamed x120, local copies, waits for them, and re-layouts: 6.73 us -> 4.77 us
  transfers between devices with their start and end apart: 44 -> 44, of which waited for: 19 -> 13; matrix products, arithmetic and copies ran while one was open for 1% -> 1% of each run, Pallas kernels for 48% -> 50%
where the time goes in v3:
time: 176 us; the launch traced here: 175 us
  Pallas kernels  91.8 us (52%)
  starting transfers between devices  40.5 us (23%)
  waiting for transfers between devices  33.6 us (19%)
  local copies, waits for them, and re-layouts  4.88 us (3%)
  between operations  2.52 us (1%)
    ppermute x22, waiting for transfers between devices, along(): return lax.ppermute(values, 'dp', hop)  25.4 us
    ppermute x22, starting transfers between devices, along(): return lax.ppermute(values, 'dp', hop)  22.7 us
    pallas_call x2, Pallas kernels, attend_back(): pl.pallas_call(functools.partial(attend_back_kernel, prefix), grid=(1,),...  18.8 us
    ppermute x9, starting transfers between devices, to_far(): lax.ppermute(values, 'tensor', [(t, (t + shift) % group) for t in range(g...  11.4 us
    pallas_call x2, Pallas kernels, mlp(): pl.pallas_call(functools.partial(mlp_kernel, bool(sums)), grid_spec=pltpu...  10.5 us
    pallas_call x2, Pallas kernels, project(): pl.pallas_call(functools.partial(project_kernel, first), grid=(length //...  8.97 us
    pallas_call x2, Pallas kernels, rest(): pl.pallas_call(rest_kernel, grid_spec=pltpu.PrefetchScalarGridSpec(num_sc...  7.51 us
    pallas_call x1, Pallas kernels, attend(): pl.pallas_call(functools.partial(attend_kernel, prefix, parcel), grid=(1,...  7.26 us
  transfers between devices with their start and end apart: 44, of which 13 were waited for; matrix products, arithmetic and copies ran while one was open for 1% of the time, Pallas kernels for 50%

profile of v3, /device:TPU:0, one launch (start us, length us, event | category | flops | bytes accessed | tf_op | source)
XLA Modules:
  0.0 174.6 jit_solution(12058521332545984890)
XLA Ops:
  1.8 3.0 %collective-permute-start = (f32[128,1024]{1,0:T(8,128)S(1)}, f32[128,1024]{1,0:T(8,128)S(1)}, u32[]{:S(2)}, u32[]{:S(2)}) collective-permute-start(f32[128,1024]{1,0:T(8,128)S(1)} %pick.4.refs_1_), channel_id=1, source_target_pairs={{0,2},{1,3},{2,0},{3,1},{4,6},{5,7},{6,4},{7,5},{8,10},{9,11},{10,... | collective-permute-start | bytes 1572872 | tf_op jit(solution)/shard_map/ppermute | solution.py:1035
  5.9 1.8 %pick.7 = f32[128,1024]{1,0:T(8,128)} custom-call(s32[1]{0:T(128)} %bitcast.2.which_ref.order_ref, bf16[1024,1024]{1,0:T(8,128)(2,1)} %proj_ref.3, f32[32,1024]{1,0:T(8,128)S(1)} %pick.5.refs_1_), custom_call_target="tpu_custom_call" | custom-call | bytes 49152 | tf_op jit(solution)/shard_map/pick/pallas_call | solution.py:517
  7.7 2.0 %collective-permute-start.11 = (f32[128,1024]{1,0:T(8,128)}, f32[128,1024]{1,0:T(8,128)S(1)}, u32[]{:S(2)}, u32[]{:S(2)}) collective-permute-start(f32[128,1024]{1,0:T(8,128)} %pick.7), channel_id=1, source_target_pairs={{0,2},{1,3},{2,0},{3,1},{4,6},{5,7},{6,4},{7,5},{8,10},{9,11},{10,... | collective-permute-start | bytes 1572872 | tf_op jit(solution)/shard_map/ppermute | solution.py:1035
  9.9 5.1 %project.2 = (bf16[1024,768]{1,0:T(8,128)(2,1)S(1)}, bf16[1024,1024]{1,0:T(8,128)(2,1)}) custom-call(bf16[1024,1024]{1,0:T(8,128)(2,1)} %bitcast.31, bf16[1024,1024]{1,0:T(8,128)(2,1)} %bitcast.32, f32[8,1024]{1,0:T(8,128)S(1)} %pad_convert_fusion.vec_ref, bf16[3,1024,256]{2,1,0:T(8,128)(2,1)S(1)} %bitcast.28, f32[16,256]{1,0:T(8,128)S(1)} %fusion.12.bias_ref), custom_call_target="tpu_custom_call" | custom-call | flops 100663296 | bytes 524288 | tf_op jit(solution)/shard_map/project/pallas_call | solution.py:187
  15.1 2.5 %collective-permute-done.refs_0_ = f32[128,1024]{1,0:T(8,128)S(1)} collective-permute-done((f32[128,1024]{1,0:T(8,128)S(1)}, f32[128,1024]{1,0:T(8,128)S(1)}, u32[]{:S(2)}, u32[]{:S(2)}) %collective-permute-start) | collective-permute-done | bytes 524320 | tf_op jit(solution)/shard_map/ppermute | solution.py:1035
  17.6 2.0 %collective-permute-start.3 = (f32[128,1024]{1,0:T(8,128)S(1)}, f32[128,1024]{1,0:T(8,128)}, u32[]{:S(2)}, u32[]{:S(2)}) collective-permute-start(f32[128,1024]{1,0:T(8,128)S(1)} %held.19.refs_0_.refs_1_), channel_id=1, source_target_pairs={{0,4},{8,0},{16,8},{24,16},{28,24},{20,28},{12,20},{4,12},{1,5},{9... | collective-permute-start | bytes 1572872 | tf_op jit(solution)/shard_map/ppermute | solution.py:1055
  20.5 2.0 %collective-permute-start.5 = (f32[32,1024]{1,0:T(8,128)}, f32[32,1024]{1,0:T(8,128)S(1)}, u32[]{:S(2)}, u32[]{:S(2)}) collective-permute-start(f32[32,1024]{1,0:T(8,128)} %held.20.refs_2_.refs_3_.refs_0_), channel_id=1, source_target_pairs={{0,4},{8,0},{16,8},{24,16},{28,24},{20,28},{12,20},{4,12},{1,5},{9... | collective-permute-start | bytes 393224 | tf_op jit(solution)/shard_map/ppermute | solution.py:1055
  23.3 7.3 %attend.1 = (f32[1216,256]{1,0:T(8,128)S(1)}, f32[8,128]{1,0:T(8,128)S(1)}) custom-call(s32[8]{0:T(128)S(1)} %bitcast.41, s32[1]{0:T(128)S(6)} %copy.92.pads_ref, bf16[1024,768]{1,0:T(8,128)(2,1)S(1)} %get-tuple-element.63.refs_1_.qkv_ref, f32[32,256]{1,0:T(8,128)S(1)} %pad_maximum_fusion.1.kv_ref, f32[16,256]{1,0:T(8,128)S(1)} %fusion.12.bias_ref, ...), custom_call_target="tpu_custom_call" | custom-call | flops 67108864 | bytes 163840 | tf_op jit(solution)/shard_map/attend/pallas_call | solution.py:257
  30.6 2.1 %collective-permute-done.5.refs_4_.refs_1_ = f32[32,1024]{1,0:T(8,128)S(1)} collective-permute-done((f32[32,1024]{1,0:T(8,128)}, f32[32,1024]{1,0:T(8,128)S(1)}, u32[]{:S(2)}, u32[]{:S(2)}) %collective-permute-start.5) | collective-permute-done | bytes 131104 | tf_op jit(solution)/shard_map/ppermute | solution.py:1055
  33.8 1.6 collective-permute-start.6
  35.5 1.6 collective-permute-start.13
  38.1 1.5 collective-permute-start.8
  39.6 12.3 %collective-permute-done.7.refs_3_.refs_4_ = f32[32,1024]{1,0:T(8,128)S(1)} collective-permute-done((f32[32,1024]{1,0:T(8,128)S(1)}, f32[32,1024]{1,0:T(8,128)S(1)}, u32[]{:S(2)}, u32[]{:S(2)}) %collective-permute-start.7) | collective-permute-done | bytes 131104 | tf_op jit(solution)/shard_map/ppermute | solution.py:1055
  52.3 1.6 collective-permute-start.10
  54.4 1.6 collective-permute-start.15
  56.0 2.4 %collective-permute-done.9.refs_4_.refs_5_.refs_2_ = f32[32,1024]{1,0:T(8,128)S(1)} collective-permute-done((f32[32,1024]{1,0:T(8,128)S(1)}, f32[32,1024]{1,0:T(8,128)S(1)}, u32[]{:S(2)}, u32[]{:S(2)}) %collective-permute-start.9) | collective-permute-done | bytes 131104 | tf_op jit(solution)/shard_map/ppermute | solution.py:1055
  59.4 1.6 collective-permute-start.18
  63.0 1.7 %pick.6 = (f32[128,1024]{1,0:T(8,128)S(1)}, f32[128,1024]{1,0:T(8,128)S(1)}, f32[3,128,256]{2,1,0:T(8,128)S(1)}, f32[3,128,256]{2,1,0:T(8,128)S(1)}) custom-call(s32[4]{0:T(128)S(1)} %pad_add_fusion.1.which_ref, bf16[1024,1024]{1,0:T(8,128)(2,1)} %fc_ref.3, bf16[1024,1024]{1,0:T(8,128)(2,1)} %proj_ref.3, bf16[3,1024,256]{2,1,0:T(8,128)(2,1)} %bitcast.25, ...), custom_call_target="tpu_custom_call" | custom-call | bytes 122880 | tf_op jit(solution)/shard_map/pick/pallas_call | solution.py:517
  64.8 1.6 joined.1.refs_8_.refs_0_
  67.9 1.7 collective-permute-done.14.refs_4_.refs_0_.refs_1_
  71.1 5.3 %collective-permute-done.17.refs_2_.refs_0_ = f32[128,1024]{1,0:T(8,128)} collective-permute-done((f32[128,1024]{1,0:T(8,128)}, f32[128,1024]{1,0:T(8,128)}, u32[]{:S(2)}, u32[]{:S(2)}) %collective-permute-start.17) | collective-permute-done | bytes 524320 | tf_op jit(solution)/shard_map/ppermute | solution.py:1055
  76.9 1.6 collective-permute-start.20
  82.3 5.2 %mlp.2 = (f32[512,1024]{1,0:T(8,128)S(1)}, f32[512,1024]{1,0:T(8,128)S(1)}) custom-call(s32[1]{0:T(128)} %bitcast.which_ref.core_ref, f32[512,1024]{1,0:T(8,128)S(1)} %get-tuple-element.75.n_ref.refs_1_, bf16[1024,1024]{1,0:T(8,128)(2,1)S(1)} %bitcast.36, bf16[1024,1024]{1,0:T(8,128)(2,1)S(1)} %copy-done.4, bf16[1024,1024]{1,0:T(8,128)(2,1)S(1)} %copy-done.5, ...), custom_call_target="tpu_custom_call" | custom-call | flops 85899345920 | bytes 786432 | tf_op jit(solution)/shard_map/mlp/pallas_call | solution.py:700
  88.1 1.6 collective-permute-start.24
  89.7 1.9 %collective-permute-start.27 = (f32[3,128,256]{2,1,0:T(8,128)S(1)}, f32[3,128,256]{2,1,0:T(8,128)S(1)}, u32[]{:S(2)}, u32[]{:S(2)}) collective-permute-start(f32[3,128,256]{2,1,0:T(8,128)S(1)} %held.30), channel_id=1, source_target_pairs={{0,2},{1,3},{2,0},{3,1},{4,6},{5,7},{6,4},{7,5},{8,10},{9,11},{10,... | collective-permute-start | bytes 1179656 | tf_op jit(solution)/shard_map/ppermute | solution.py:1035
  91.7 5.2 %mlp.3 = (f32[512,1024]{1,0:T(8,128)S(1)}, f32[512,1024]{1,0:T(8,128)S(1)}) custom-call(s32[1]{0:T(128)S(6)} %sub.11.which_ref, f32[512,1024]{1,0:T(8,128)S(1)} %collective-permute-done.22.n_ref.refs_2_, bf16[1024,1024]{1,0:T(8,128)(2,1)S(1)} %bitcast.37, bf16[1024,1024]{1,0:T(8,128)(2,1)S(1)} %copy-done.4, bf16[1024,1024]{1,0:T(8,128)(2,1)S(1)} %copy-done.5, ...), custom_call_target="tpu_custom_call" | custom-call | flops 268435456 | bytes 786432 | tf_op jit(solution)/shard_map/mlp/pallas_call | solution.py:700
  98.3 2.5 %mlp_front.2 = (bf16[512,1024]{1,0:T(8,128)(2,1)S(1)}, f32[512,1024]{1,0:T(8,128)S(1)}) custom-call(f32[512,1024]{1,0:T(8,128)S(1)} %collective-permute-done.22.n_ref.refs_2_, bf16[1024,1024]{1,0:T(8,128)(2,1)S(1)} %assemble.5.fc_ref, f32[1216,256]{1,0:T(8,128)S(1)} %collective-permute-done.6.refs_7_.refs_1_.bias_ref.kv_ref.lse_ref), custom_call_target="tpu_custom_call" | custom-call | flops 67108864 | bytes 327680 | tf_op jit(solution)/shard_map/mlp_front/pallas_call | solution.py:747
  100.8 2.5 %mlp_front.3 = (bf16[512,1024]{1,0:T(8,128)(2,1)S(1)}, f32[512,1024]{1,0:T(8,128)S(1)}) custom-call(f32[512,1024]{1,0:T(8,128)S(1)} %get-tuple-element.75.n_ref.refs_1_, bf16[1024,1024]{1,0:T(8,128)(2,1)S(1)} %assemble.5.fc_ref, f32[1216,256]{1,0:T(8,128)S(1)} %collective-permute-done.6.refs_7_.refs_1_.bias_ref.kv_ref.lse_ref, ...), custom_call_target="tpu_custom_call" | custom-call | flops 67108864 | bytes 327680 | tf_op jit(solution)/shard_map/mlp_front/pallas_call | solution.py:747
  103.4 1.7 assemble.6.proj_ref
  105.1 3.8 %mlp_rest.2 = (f32[512,1024]{1,0:T(8,128)S(1)}, f32[512,1024]{1,0:T(8,128)S(1)}) custom-call(s32[1]{0:T(128)S(6)} %sub.11.which_ref, bf16[512,1024]{1,0:T(8,128)(2,1)S(1)} %get-tuple-element.79.refs_0_.act_ref, f32[512,1024]{1,0:T(8,128)S(1)} %get-tuple-element.86.slope_ref, bf16[1024,1024]{1,0:T(8,128)(2,1)S(1)} %bitcast.38, ...), custom_call_target="tpu_custom_call" | custom-call | flops 3221225472 | bytes 786432 | tf_op jit(solution)/shard_map/mlp_rest/pallas_call | solution.py:786
  108.9 1.6 collective-permute-start.29
  111.7 3.7 %mlp_rest.3 = (f32[512,1024]{1,0:T(8,128)S(1)}, f32[512,1024]{1,0:T(8,128)S(1)}) custom-call(s32[1]{0:T(128)} %bitcast.which_ref.core_ref, bf16[512,1024]{1,0:T(8,128)(2,1)S(1)} %get-tuple-element.80.act_ref, f32[512,1024]{1,0:T(8,128)S(1)} %get-tuple-element.81.refs_8_.slope_ref, bf16[1024,1024]{1,0:T(8,128)(2,1)S(1)} %bitcast.39, ...), custom_call_target="tpu_custom_call" | custom-call | flops 64424509440 | bytes 786432 | tf_op jit(solution)/shard_map/mlp_rest/pallas_call | solution.py:786
  115.5 2.9 %collective-permute-done.30.b_ref = f32[512,1024]{1,0:T(8,128)S(1)} collective-permute-done((f32[512,1024]{1,0:T(8,128)S(1)}, f32[512,1024]{1,0:T(8,128)S(1)}, u32[]{:S(2)}, u32[]{:S(2)}) %collective-permute-start.30) | collective-permute-done | bytes 2097184 | tf_op jit(solution)/shard_map/ppermute | solution.py:1031
  118.4 1.6 norm_two_back.1.refs_2_.keep_ref.refs_1_.upper_ref
  120.3 1.7 result.1
  122.4 1.8 %collective-permute-start.36 = (f32[6,128,256]{2,1,0:T(8,128)S(1)}, f32[6,128,256]{2,1,0:T(8,128)S(1)}, u32[]{:S(2)}, u32[]{:S(2)}) collective-permute-start(f32[6,128,256]{2,1,0:T(8,128)S(1)} %held.34), channel_id=1, source_target_pairs={{0,2},{1,3},{2,0},{3,1},{4,6},{5,7},{6,4},{7,5},{8,10},{9,11},{10,... | collective-permute-start | bytes 2359304 | tf_op jit(solution)/shard_map/ppermute | solution.py:1035
  124.6 1.6 collective-permute-start.35
  126.4 2.3 %heads_back.1 = (bf16[1024,256]{1,0:T(8,128)(2,1)S(1)}, bf16[1024,256]{1,0:T(8,128)(2,1)S(1)}) custom-call(s32[1]{0:T(128)} %bitcast.which_ref.core_ref, f32[512,1024]{1,0:T(8,128)S(1)} %norm_two_back.1.refs_2_.keep_ref.refs_1_.upper_ref, f32[512,1024]{1,0:T(8,128)S(1)} %collective-permute-done.33.other_ref.upper_ref, bf16[256,1024]{1,0:T(8,128)(2,1)S(1)} %copy-done.11, ...), custom_call_target="tpu_custom_call" | custom-call | flops 67108864 | bytes 327680 | tf_op jit(solution)/shard_map/heads_back/pallas_call | solution.py:331
  128.7 9.2 %attend_back.2 = (bf16[1024,768]{1,0:T(8,128)(2,1)S(1)}, f32[16,256]{1,0:T(8,128)S(1)}, f32[16,256]{1,0:T(8,128)S(1)}) custom-call(s32[8]{0:T(128)S(1)} %bitcast.42, s32[1]{0:T(128)S(6)} %copy.92.pads_ref, bf16[1024,768]{1,0:T(8,128)(2,1)S(1)} %copy-done.8, bf16[1024,256]{1,0:T(8,128)(2,1)S(1)} %get-tuple-element.99.do_ref, ...), custom_call_target="tpu_custom_call" | custom-call | flops 2684354560 | bytes 655360 | tf_op jit(solution)/shard_map/attend_back/pallas_call | solution.py:412
  139.9 1.5 place.1
  142.2 3.9 %project.3.qkv_ref.refs_1_ = bf16[1024,768]{1,0:T(8,128)(2,1)S(1)} custom-call(bf16[1024,1024]{1,0:T(8,128)(2,1)} %get-tuple-element.102.x_ref.y_ref, bf16[1024,1024]{1,0:T(8,128)(2,1)} %get-tuple-element.102.x_ref.y_ref, f32[8,1024]{1,0:T(8,128)S(1)} %copy-done.28, bf16[3,1024,256]{2,1,0:T(8,128)(2,1)S(1)} %assemble.7.w_ref.refs_3_, ...), custom_call_target="tpu_custom_call" | custom-call | flops 100663296 | bytes 524288 | tf_op jit(solution)/shard_map/project/pallas_call | solution.py:187
  147.5 9.6 %attend_back.3 = (bf16[1024,768]{1,0:T(8,128)(2,1)S(1)}, f32[16,256]{1,0:T(8,128)}, f32[16,256]{1,0:T(8,128)}) custom-call(s32[8]{0:T(128)S(1)} %bitcast.43, s32[1]{0:T(128)S(6)} %copy.92.pads_ref, bf16[1024,768]{1,0:T(8,128)(2,1)S(1)} %project.3.qkv_ref.refs_1_, bf16[1024,256]{1,0:T(8,128)(2,1)S(1)} %get-tuple-element.108.do_ref, ...), custom_call_target="tpu_custom_call" | custom-call | flops 2684354560 | bytes 655360 | tf_op jit(solution)/shard_map/attend_back/pallas_call | solution.py:412
  158.5 2.0 %unproject.2.refs_4_.a_ref = f32[512,1024]{1,0:T(8,128)S(1)} custom-call(s32[1]{0:T(128)S(6)} %sub.11.which_ref, bf16[1024,768]{1,0:T(8,128)(2,1)S(1)} %get-tuple-element.100.refs_1_.refs_0_, bf16[1024,768]{1,0:T(8,128)(2,1)S(1)} %get-tuple-element.109.refs_1_, bf16[3,1024,256]{2,1,0:T(8,128)(2,1)S(1)} %bitcast.29, ...), custom_call_target="tpu_custom_call" | custom-call | flops 100663296 | bytes 262144 | tf_op jit(solution)/shard_map/unproject/pallas_call | solution.py:619
  161.5 2.0 %unproject.3.a_ref = f32[512,1024]{1,0:T(8,128)S(1)} custom-call(s32[1]{0:T(128)} %bitcast.which_ref.core_ref, bf16[1024,768]{1,0:T(8,128)(2,1)S(1)} %get-tuple-element.100.refs_1_.refs_0_, bf16[1024,768]{1,0:T(8,128)(2,1)S(1)} %get-tuple-element.109.refs_1_, bf16[3,1024,256]{2,1,0:T(8,128)(2,1)S(1)} %bitcast.30, ...), custom_call_target="tpu_custom_call" | custom-call | flops 100663296 | bytes 262144 | tf_op jit(solution)/shard_map/unproject/pallas_call | solution.py:619
  163.7 2.3 %collective-permute-start.43 = (f32[16,1024]{1,0:T(8,128)S(1)}, f32[16,1024]{1,0:T(8,128)S(1)}, u32[]{:S(2)}, u32[]{:S(2)}) collective-permute-start(f32[16,1024]{1,0:T(8,128)S(1)} %add.96.refs_5_.a_ref), channel_id=1, source_target_pairs={{0,4},{4,0},{8,12},{12,8},{16,20},{20,16},{24,28},{28,24},{1,5},{5... | collective-permute-start | bytes 196616 | tf_op jit(solution)/shard_map/ppermute | solution.py:1286
  166.7 2.8 %norm_one_back.2 = (f32[1024,1024]{1,0:T(8,128)}, f32[8,128]{1,0:T(8,128)S(1)}) custom-call(s32[1]{0:T(128)} %bitcast.which_ref.core_ref, bf16[1024,1024]{1,0:T(8,128)(2,1)S(1)} %bitcast.34, f32[512,1024]{1,0:T(8,128)S(1)} %norm_two_back.1.refs_2_.keep_ref.refs_1_.upper_ref, f32[8,1024]{1,0:T(8,128)S(1)} %copy-done.28, f32[512,1024]{1,0:T(8,128)S(1)} %unproject.3.a_ref, ...), custom_call_target="tpu_custom_call" | custom-call | flops 655360 | bytes 589824 | tf_op jit(solution)/shard_map/norm_one_back/pallas_call | solution.py:857
  169.5 2.2 %prefix_grads.1 = (f32[1024,512]{1,0:T(8,128)}, f32[512,2,256]{2,1,0:T(2,128)}, f32[1,512]{1,0:T(1,128)}, f32[2,256]{1,0:T(2,128)}, f32[16,1024]{1,0:T(8,128)}) custom-call(f32[16,1024]{1,0:T(8,128)S(1)} %add.96.refs_5_.a_ref, f32[16,1024]{1,0:T(8,128)S(1)} %collective-permute-done.43.b_ref, f32[16,512]{1,0:T(8,128)S(1)} %pad.30.trunk_ref, ...), custom_call_target="tpu_custom_call" | custom-call | bytes 262144 | tf_op jit(solution)/shard_map/prefix_grads/pallas_call | solution.py:980
  171.7 2.8 %norm_one_back.3 = (f32[1024,1024]{1,0:T(8,128)}, f32[8,128]{1,0:T(8,128)}) custom-call(s32[1]{0:T(128)S(6)} %sub.11.which_ref, bf16[1024,1024]{1,0:T(8,128)(2,1)S(1)} %bitcast.35, f32[512,1024]{1,0:T(8,128)S(1)} %collective-permute-done.33.other_ref.upper_ref, f32[8,1024]{1,0:T(8,128)S(1)} %copy-done.28, ...), custom_call_target="tpu_custom_call", output_to_operand_aliasing={{0}: (6, {})} | custom-call | flops 655360 | bytes 589824 | tf_op jit(solution)/shard_map/norm_one_back/pallas_call | solution.py:857
  (238 shorter events, 27.9 us)
Async XLA Ops:
  1.8 15.8 %collective-permute-start = (f32[128,1024]{1,0:T(8,128)S(1)}, f32[128,1024]{1,0:T(8,128)S(1)}, u32[]{:S(2)}, u32[]{:S(2)}) collective-permute-start(f32[128,1024]{1,0:T(8,128)S(1)} %pick.4.refs_1_), channel_id=1, source_target_pairs={{0,2},{1,3},{2,0},{3,1},{4,6},{5,7},{6,4},{7,5},{8,10},{9,11},{10,... | collective-permute-start | bytes 1572872 | tf_op jit(solution)/shard_map/ppermute | solution.py:1035
  5.7 14.8 %collective-permute-start.1 = (f32[32,1024]{1,0:T(8,128)S(1)}, f32[32,1024]{1,0:T(8,128)}, u32[]{:S(2)}, u32[]{:S(2)}) collective-permute-start(f32[32,1024]{1,0:T(8,128)S(1)} %pick.5.refs_1_), channel_id=1, source_target_pairs={{0,2},{1,3},{2,0},{3,1},{4,6},{5,7},{6,4},{7,5},{8,10},{9,11},{10,... | collective-permute-start | bytes 393224 | tf_op jit(solution)/shard_map/ppermute | solution.py:1035
  7.7 27.8 %collective-permute-start.11 = (f32[128,1024]{1,0:T(8,128)}, f32[128,1024]{1,0:T(8,128)S(1)}, u32[]{:S(2)}, u32[]{:S(2)}) collective-permute-start(f32[128,1024]{1,0:T(8,128)} %pick.7), channel_id=1, source_target_pairs={{0,2},{1,3},{2,0},{3,1},{4,6},{5,7},{6,4},{7,5},{8,10},{9,11},{10,... | collective-permute-start | bytes 1572872 | tf_op jit(solution)/shard_map/ppermute | solution.py:1035
  17.6 16.2 %collective-permute-start.3 = (f32[128,1024]{1,0:T(8,128)S(1)}, f32[128,1024]{1,0:T(8,128)}, u32[]{:S(2)}, u32[]{:S(2)}) collective-permute-start(f32[128,1024]{1,0:T(8,128)S(1)} %held.19.refs_0_.refs_1_), channel_id=1, source_target_pairs={{0,4},{8,0},{16,8},{24,16},{28,24},{20,28},{12,20},{4,12},{1,5},{9... | collective-permute-start | bytes 1572872 | tf_op jit(solution)/shard_map/ppermute | solution.py:1055
  19.6 14.2 %collective-permute-start.2 = (f32[128,1024]{1,0:T(8,128)S(1)}, f32[128,1024]{1,0:T(8,128)}, u32[]{:S(2)}, u32[]{:S(2)}) collective-permute-start(f32[128,1024]{1,0:T(8,128)S(1)} %held.19.refs_0_.refs_1_), channel_id=1, source_target_pairs={{0,8},{8,16},{16,24},{24,28},{28,20},{20,12},{12,4},{4,0},{1,9},{9... | collective-permute-start | bytes 1572872 | tf_op jit(solution)/shard_map/ppermute | solution.py:1055
  20.4 13.4 %copy-start.9 = (bf16[256,1024]{1,0:T(8,128)(2,1)S(1)}, bf16[256,1024]{1,0:T(8,128)(2,1)}, u32[]{:S(2)}) copy-start(bf16[256,1024]{1,0:T(8,128)(2,1)} %refs_0_.9) | copy-start | bytes 1572868
  20.5 12.2 %collective-permute-start.5 = (f32[32,1024]{1,0:T(8,128)}, f32[32,1024]{1,0:T(8,128)S(1)}, u32[]{:S(2)}, u32[]{:S(2)}) collective-permute-start(f32[32,1024]{1,0:T(8,128)} %held.20.refs_2_.refs_3_.refs_0_), channel_id=1, source_target_pairs={{0,4},{8,0},{16,8},{24,16},{28,24},{20,28},{12,20},{4,12},{1,5},{9... | collective-permute-start | bytes 393224 | tf_op jit(solution)/shard_map/ppermute | solution.py:1055
  22.5 11.3 %collective-permute-start.4 = (f32[32,1024]{1,0:T(8,128)}, f32[32,1024]{1,0:T(8,128)S(1)}, u32[]{:S(2)}, u32[]{:S(2)}) collective-permute-start(f32[32,1024]{1,0:T(8,128)} %held.20.refs_2_.refs_3_.refs_0_), channel_id=1, source_target_pairs={{0,8},{8,16},{16,24},{24,28},{28,20},{20,12},{12,4},{4,0},{1,9},{9... | collective-permute-start | bytes 393224 | tf_op jit(solution)/shard_map/ppermute | solution.py:1055
  33.8 32.7 %collective-permute-start.6 = (f32[1216,256]{1,0:T(8,128)S(1)}, f32[1216,256]{1,0:T(8,128)S(1)}, u32[]{:S(2)}, u32[]{:S(2)}) collective-permute-start(f32[1216,256]{1,0:T(8,128)S(1)} %held.21.refs_2_.refs_0_.kv_ref.lse_ref), channel_id=1, source_target_pairs={{0,2},{1,3},{2,0},{3,1},{4,6},{5,7},{6,4},{7,5},{8,10},{9,11},{10,... | collective-permute-start | bytes 3735560 | tf_op jit(solution)/shard_map/ppermute | solution.py:1035
  35.4 23.3 %copy-start.20 = (f32[32,1024]{1,0:T(8,128)}, f32[32,1024]{1,0:T(8,128)S(1)}, u32[]{:S(2)}) copy-start(f32[32,1024]{1,0:T(8,128)S(1)} %get-tuple-element.67.refs_2_) | copy-start | bytes 393220
  35.4 23.3 %copy-start.22 = (f32[32,1024]{1,0:T(8,128)}, f32[32,1024]{1,0:T(8,128)S(1)}, u32[]{:S(2)}) copy-start(f32[32,1024]{1,0:T(8,128)S(1)} %get-tuple-element.66.refs_1_) | copy-start | bytes 393220
  35.5 18.9 %copy-start.24 = (f32[128,1024]{1,0:T(8,128)}, f32[128,1024]{1,0:T(8,128)S(1)}, u32[]{:S(2)}) copy-start(f32[128,1024]{1,0:T(8,128)S(1)} %held.23.refs_0_) | copy-start | bytes 1572868
  35.5 18.5 %collective-permute-start.13 = (f32[128,1024]{1,0:T(8,128)S(1)}, f32[128,1024]{1,0:T(8,128)}, u32[]{:S(2)}, u32[]{:S(2)}) collective-permute-start(f32[128,1024]{1,0:T(8,128)S(1)} %held.23.refs_0_), channel_id=1, source_target_pairs={{0,4},{8,0},{16,8},{24,16},{28,24},{20,28},{12,20},{4,12},{1,5},{9... | collective-permute-start | bytes 1572872 | tf_op jit(solution)/shard_map/ppermute | solution.py:1055
  37.1 16.8 %collective-permute-start.12 = (f32[128,1024]{1,0:T(8,128)S(1)}, f32[128,1024]{1,0:T(8,128)}, u32[]{:S(2)}, u32[]{:S(2)}) collective-permute-start(f32[128,1024]{1,0:T(8,128)S(1)} %held.23.refs_0_), channel_id=1, source_target_pairs={{0,8},{8,16},{16,24},{24,28},{28,20},{20,12},{12,4},{4,0},{1,9},{9... | collective-permute-start | bytes 1572872 | tf_op jit(solution)/shard_map/ppermute | solution.py:1055
  37.5 14.3 %collective-permute-start.7 = (f32[32,1024]{1,0:T(8,128)S(1)}, f32[32,1024]{1,0:T(8,128)S(1)}, u32[]{:S(2)}, u32[]{:S(2)}) collective-permute-start(f32[32,1024]{1,0:T(8,128)S(1)} %get-tuple-element.66.refs_1_), channel_id=1, source_target_pairs={{0,8},{8,16},{16,24},{24,28},{28,20},{20,12},{12,4},{4,0},{1,9},{9... | collective-permute-start | bytes 393224 | tf_op jit(solution)/shard_map/ppermute | solution.py:1055
  38.1 14.3 %collective-permute-start.8 = (f32[32,1024]{1,0:T(8,128)S(1)}, f32[32,1024]{1,0:T(8,128)S(1)}, u32[]{:S(2)}, u32[]{:S(2)}) collective-permute-start(f32[32,1024]{1,0:T(8,128)S(1)} %get-tuple-element.67.refs_2_), channel_id=1, source_target_pairs={{0,4},{8,0},{16,8},{24,16},{28,24},{20,28},{12,20},{4,12},{1,5},{9... | collective-permute-start | bytes 393224 | tf_op jit(solution)/shard_map/ppermute | solution.py:1055
  51.9 6.4 %collective-permute-start.9 = (f32[32,1024]{1,0:T(8,128)S(1)}, f32[32,1024]{1,0:T(8,128)S(1)}, u32[]{:S(2)}, u32[]{:S(2)}) collective-permute-start(f32[32,1024]{1,0:T(8,128)S(1)} %collective-permute-done.7.refs_3_.refs_4_), channel_id=1, source_target_pairs={{0,8},{8,16},{16,24},{24,28},{28,20},{20,12},{12,4},{4,0},{1,9},{9... | collective-permute-start | bytes 393224 | tf_op jit(solution)/shard_map/ppermute | solution.py:1055
  52.3 6.4 %collective-permute-start.10 = (f32[32,1024]{1,0:T(8,128)S(1)}, f32[32,1024]{1,0:T(8,128)S(1)}, u32[]{:S(2)}, u32[]{:S(2)}) collective-permute-start(f32[32,1024]{1,0:T(8,128)S(1)} %collective-permute-done.8.refs_4_.refs_5_), channel_id=1, source_target_pairs={{0,4},{8,0},{16,8},{24,16},{28,24},{20,28},{12,20},{4,12},{1,5},{9... | collective-permute-start | bytes 393224 | tf_op jit(solution)/shard_map/ppermute | solution.py:1055
  53.9 15.6 %collective-permute-start.14 = (f32[128,1024]{1,0:T(8,128)}, f32[128,1024]{1,0:T(8,128)S(1)}, u32[]{:S(2)}, u32[]{:S(2)}) collective-permute-start(f32[128,1024]{1,0:T(8,128)} %get-tuple-element.69.refs_1_), channel_id=1, source_target_pairs={{0,8},{8,16},{16,24},{24,28},{28,20},{20,12},{12,4},{4,0},{1,9},{9... | collective-permute-start | bytes 1572872 | tf_op jit(solution)/shard_map/ppermute | solution.py:1055
  54.4 15.2 %collective-permute-start.15 = (f32[128,1024]{1,0:T(8,128)}, f32[128,1024]{1,0:T(8,128)S(1)}, u32[]{:S(2)}, u32[]{:S(2)}) collective-permute-start(f32[128,1024]{1,0:T(8,128)} %get-tuple-element.70.refs_2_), channel_id=1, source_target_pairs={{0,4},{8,0},{16,8},{24,16},{28,24},{20,28},{12,20},{4,12},{1,5},{9... | collective-permute-start | bytes 1572872 | tf_op jit(solution)/shard_map/ppermute | solution.py:1055
  59.0 17.5 %collective-permute-start.17 = (f32[128,1024]{1,0:T(8,128)}, f32[128,1024]{1,0:T(8,128)}, u32[]{:S(2)}, u32[]{:S(2)}) collective-permute-start(f32[128,1024]{1,0:T(8,128)} %get-tuple-element.71.refs_1_), channel_id=1, source_target_pairs={{0,8},{8,16},{16,24},{24,28},{28,20},{20,12},{12,4},{4,0},{1,9},{9... | collective-permute-start | bytes 1572872 | tf_op jit(solution)/shard_map/ppermute | solution.py:1055
  59.4 17.0 %collective-permute-start.18 = (f32[128,1024]{1,0:T(8,128)}, f32[128,1024]{1,0:T(8,128)}, u32[]{:S(2)}, u32[]{:S(2)}) collective-permute-start(f32[128,1024]{1,0:T(8,128)} %get-tuple-element.72.refs_2_), channel_id=1, source_target_pairs={{0,4},{8,0},{16,8},{24,16},{28,24},{20,28},{12,20},{4,12},{1,5},{9... | collective-permute-start | bytes 1572872 | tf_op jit(solution)/shard_map/ppermute | solution.py:1055
  70.5 9.0 %collective-permute-start.16 = (f32[512,1024]{1,0:T(8,128)S(1)}, f32[512,1024]{1,0:T(8,128)S(1)}, u32[]{:S(2)}, u32[]{:S(2)}) collective-permute-start(f32[512,1024]{1,0:T(8,128)S(1)} %half_product.2.refs_4_), channel_id=1, source_target_pairs={{0,1},{1,0},{2,3},{3,2},{4,5},{5,4},{6,7},{7,6},{8,9},{9,8},{10,11... | collective-permute-start | bytes 6291464 | tf_op jit(solution)/shard_map/ppermute | solution.py:1031
  70.6 17.0 %collective-permute-start.21 = (f32[128,1024]{1,0:T(8,128)S(1)}, f32[128,1024]{1,0:T(8,128)S(1)}, u32[]{:S(2)}, u32[]{:S(2)}) collective-permute-start(f32[128,1024]{1,0:T(8,128)S(1)} %held.27), channel_id=1, source_target_pairs={{0,2},{1,3},{2,0},{3,1},{4,6},{5,7},{6,4},{7,5},{8,10},{9,11},{10,... | collective-permute-start | bytes 1572872 | tf_op jit(solution)/shard_map/ppermute | solution.py:1035
  76.5 13.2 %collective-permute-start.19 = (f32[128,1024]{1,0:T(8,128)S(1)}, f32[128,1024]{1,0:T(8,128)S(1)}, u32[]{:S(2)}, u32[]{:S(2)}) collective-permute-start(f32[128,1024]{1,0:T(8,128)S(1)} %get-tuple-element.73.refs_0_.refs_3_), channel_id=1, source_target_pairs={{0,8},{8,16},{16,24},{24,28},{28,20},{20,12},{12,4},{4,0},{1,9},{9... | collective-permute-start | bytes 1572872 | tf_op jit(solution)/shard_map/ppermute | solution.py:1055
  76.9 14.7 %collective-permute-start.20 = (f32[128,1024]{1,0:T(8,128)S(1)}, f32[128,1024]{1,0:T(8,128)S(1)}, u32[]{:S(2)}, u32[]{:S(2)}) collective-permute-start(f32[128,1024]{1,0:T(8,128)S(1)} %get-tuple-element.74.refs_1_.refs_4_), channel_id=1, source_target_pairs={{0,4},{8,0},{16,8},{24,16},{28,24},{20,28},{12,20},{4,12},{1,5},{9... | collective-permute-start | bytes 1572872 | tf_op jit(solution)/shard_map/ppermute | solution.py:1055
  80.7 6.9 %collective-permute-start.22 = (f32[512,1024]{1,0:T(8,128)S(1)}, f32[512,1024]{1,0:T(8,128)S(1)}, u32[]{:S(2)}, u32[]{:S(2)}) collective-permute-start(f32[512,1024]{1,0:T(8,128)S(1)} %get-tuple-element.75.n_ref.refs_1_), channel_id=1, source_target_pairs={{0,1},{1,0},{2,3},{3,2},{4,5},{5,4},{6,7},{7,6},{8,9},{9,8},{10,11... | collective-permute-start | bytes 6291464 | tf_op jit(solution)/shard_map/ppermute | solution.py:1031
  87.5 15.8 %collective-permute-start.25 = (f32[128,1024]{1,0:T(8,128)S(1)}, f32[128,1024]{1,0:T(8,128)S(1)}, u32[]{:S(2)}, u32[]{:S(2)}) collective-permute-start(f32[128,1024]{1,0:T(8,128)S(1)} %held.29), channel_id=1, source_target_pairs={{0,2},{1,3},{2,0},{3,1},{4,6},{5,7},{6,4},{7,5},{8,10},{9,11},{10,... | collective-permute-start | bytes 1572872 | tf_op jit(solution)/shard_map/ppermute | solution.py:1035
  87.6 15.7 %collective-permute-start.23 = (f32[128,1024]{1,0:T(8,128)}, f32[128,1024]{1,0:T(8,128)S(1)}, u32[]{:S(2)}, u32[]{:S(2)}) collective-permute-start(f32[128,1024]{1,0:T(8,128)} %get-tuple-element.82.refs_3_), channel_id=1, source_target_pairs={{0,8},{8,16},{16,24},{24,28},{28,20},{20,12},{12,4},{4,0},{1,9},{9... | collective-permute-start | bytes 1572872 | tf_op jit(solution)/shard_map/ppermute | solution.py:1055
  88.1 15.2 %collective-permute-start.24 = (f32[128,1024]{1,0:T(8,128)}, f32[128,1024]{1,0:T(8,128)S(1)}, u32[]{:S(2)}, u32[]{:S(2)}) collective-permute-start(f32[128,1024]{1,0:T(8,128)} %get-tuple-element.83.refs_4_), channel_id=1, source_target_pairs={{0,4},{8,0},{16,8},{24,16},{28,24},{20,28},{12,20},{4,12},{1,5},{9... | collective-permute-start | bytes 1572872 | tf_op jit(solution)/shard_map/ppermute | solution.py:1055
  89.7 19.2 %collective-permute-start.27 = (f32[3,128,256]{2,1,0:T(8,128)S(1)}, f32[3,128,256]{2,1,0:T(8,128)S(1)}, u32[]{:S(2)}, u32[]{:S(2)}) collective-permute-start(f32[3,128,256]{2,1,0:T(8,128)S(1)} %held.30), channel_id=1, source_target_pairs={{0,2},{1,3},{2,0},{3,1},{4,6},{5,7},{6,4},{7,5},{8,10},{9,11},{10,... | collective-permute-start | bytes 1179656 | tf_op jit(solution)/shard_map/ppermute | solution.py:1035
  108.9 11.3 %collective-permute-start.29 = (f32[3,128,256]{2,1,0:T(8,128)S(1)}, f32[3,128,256]{2,1,0:T(8,128)S(1)}, u32[]{:S(2)}, u32[]{:S(2)}) collective-permute-start(f32[3,128,256]{2,1,0:T(8,128)S(1)} %held.31.refs_0_), channel_id=1, source_target_pairs={{0,4},{8,0},{16,8},{24,16},{28,24},{20,28},{12,20},{4,12},{1,5},{9... | collective-permute-start | bytes 1179656 | tf_op jit(solution)/shard_map/ppermute | solution.py:1055
  110.6 9.7 %collective-permute-start.28 = (f32[3,128,256]{2,1,0:T(8,128)S(1)}, f32[3,128,256]{2,1,0:T(8,128)S(1)}, u32[]{:S(2)}, u32[]{:S(2)}) collective-permute-start(f32[3,128,256]{2,1,0:T(8,128)S(1)} %held.31.refs_0_), channel_id=1, source_target_pairs={{0,8},{8,16},{16,24},{24,28},{28,20},{20,12},{12,4},{4,0},{1,9},{9... | collective-permute-start | bytes 1179656 | tf_op jit(solution)/shard_map/ppermute | solution.py:1055
  111.0 9.2 %collective-permute-start.31 = (f32[3,128,256]{2,1,0:T(8,128)S(1)}, f32[3,128,256]{2,1,0:T(8,128)S(1)}, u32[]{:S(2)}, u32[]{:S(2)}) collective-permute-start(f32[3,128,256]{2,1,0:T(8,128)S(1)} %held.33), channel_id=1, source_target_pairs={{0,2},{1,3},{2,0},{3,1},{4,6},{5,7},{6,4},{7,5},{8,10},{9,11},{10,... | collective-permute-start | bytes 1179656 | tf_op jit(solution)/shard_map/ppermute | solution.py:1035
  111.2 9.0 %collective-permute-start.26 = (f32[512,1024]{1,0:T(8,128)S(1)}, f32[512,1024]{1,0:T(8,128)S(1)}, u32[]{:S(2)}, u32[]{:S(2)}) collective-permute-start(f32[512,1024]{1,0:T(8,128)S(1)} %get-tuple-element.88.refs_2_), channel_id=1, source_target_pairs={{0,1},{1,0},{2,3},{3,2},{4,5},{5,4},{6,7},{7,6},{8,9},{9,8},{10,11... | collective-permute-start | bytes 6291464 | tf_op jit(solution)/shard_map/ppermute | solution.py:1031
  111.2 7.2 %collective-permute-start.30 = (f32[512,1024]{1,0:T(8,128)S(1)}, f32[512,1024]{1,0:T(8,128)S(1)}, u32[]{:S(2)}, u32[]{:S(2)}) collective-permute-start(f32[512,1024]{1,0:T(8,128)S(1)} %get-tuple-element.92), channel_id=1, source_target_pairs={{0,1},{1,0},{2,3},{3,2},{4,5},{5,4},{6,7},{7,6},{8,9},{9,8},{10,11... | collective-permute-start | bytes 6291464 | tf_op jit(solution)/shard_map/ppermute | solution.py:1031
  120.0 6.3 %collective-permute-start.33 = (f32[512,1024]{1,0:T(8,128)S(1)}, f32[512,1024]{1,0:T(8,128)S(1)}, u32[]{:S(2)}, u32[]{:S(2)}) collective-permute-start(f32[512,1024]{1,0:T(8,128)S(1)} %norm_two_back.1.refs_2_.keep_ref.refs_1_.upper_ref), channel_id=1, source_target_pairs={{0,1},{1,0},{2,3},{3,2},{4,5},{5,4},{6,7},{7,6},{8,9},{9,8},{10,11... | collective-permute-start | bytes 6291464 | tf_op jit(solution)/shard_map/ppermute | solution.py:1031
  122.0 17.9 %collective-permute-start.32 = (f32[512,1024]{1,0:T(8,128)S(1)}, f32[512,1024]{1,0:T(8,128)S(1)}, u32[]{:S(2)}, u32[]{:S(2)}) collective-permute-start(f32[512,1024]{1,0:T(8,128)S(1)} %get-tuple-element.96), channel_id=1, source_target_pairs={{0,1},{1,0},{2,3},{3,2},{4,5},{5,4},{6,7},{7,6},{8,9},{9,8},{10,11... | collective-permute-start | bytes 6291464 | tf_op jit(solution)/shard_map/ppermute | solution.py:1031
  122.4 19.7 %collective-permute-start.36 = (f32[6,128,256]{2,1,0:T(8,128)S(1)}, f32[6,128,256]{2,1,0:T(8,128)S(1)}, u32[]{:S(2)}, u32[]{:S(2)}) collective-permute-start(f32[6,128,256]{2,1,0:T(8,128)S(1)} %held.34), channel_id=1, source_target_pairs={{0,2},{1,3},{2,0},{3,1},{4,6},{5,7},{6,4},{7,5},{8,10},{9,11},{10,... | collective-permute-start | bytes 2359304 | tf_op jit(solution)/shard_map/ppermute | solution.py:1035
  124.2 13.7 %collective-permute-start.34 = (f32[3,128,256]{2,1,0:T(8,128)S(1)}, f32[3,128,256]{2,1,0:T(8,128)S(1)}, u32[]{:S(2)}, u32[]{:S(2)}) collective-permute-start(f32[3,128,256]{2,1,0:T(8,128)S(1)} %get-tuple-element.93.refs_0_.refs_1_), channel_id=1, source_target_pairs={{0,8},{8,16},{16,24},{24,28},{28,20},{20,12},{12,4},{4,0},{1,9},{9... | collective-permute-start | bytes 1179656 | tf_op jit(solution)/shard_map/ppermute | solution.py:1055
  124.6 13.3 %collective-permute-start.35 = (f32[3,128,256]{2,1,0:T(8,128)S(1)}, f32[3,128,256]{2,1,0:T(8,128)S(1)}, u32[]{:S(2)}, u32[]{:S(2)}) collective-permute-start(f32[3,128,256]{2,1,0:T(8,128)S(1)} %get-tuple-element.94.refs_1_.refs_2_), channel_id=1, source_target_pairs={{0,4},{8,0},{16,8},{24,16},{28,24},{20,28},{12,20},{4,12},{1,5},{9... | collective-permute-start | bytes 1179656 | tf_op jit(solution)/shard_map/ppermute | solution.py:1055
  138.4 1.2 collective-permute-start.37
  139.7 6.4 %collective-permute-start.38 = (f32[16,512]{1,0:T(8,128)S(1)}, f32[16,512]{1,0:T(8,128)S(1)}, u32[]{:S(2)}, u32[]{:S(2)}) collective-permute-start(f32[16,512]{1,0:T(8,128)S(1)} %add.93.refs_0_), channel_id=1, source_target_pairs={{0,2},{1,3},{2,0},{3,1},{4,6},{5,7},{6,4},{7,5},{8,10},{9,11},{10,... | collective-permute-start | bytes 98312 | tf_op jit(solution)/shard_map/ppermute | solution.py:1040
  146.1 11.0 %collective-permute-start.39 = (f32[16,1024]{1,0:T(8,128)S(1)}, f32[16,1024]{1,0:T(8,128)S(1)}, u32[]{:S(2)}, u32[]{:S(2)}) collective-permute-start(f32[16,1024]{1,0:T(8,128)S(1)} %held.36), channel_id=1, source_target_pairs={{0,16},{4,20},{8,24},{12,28},{16,0},{20,4},{24,8},{28,12},{1,17},{... | collective-permute-start | bytes 196616 | tf_op jit(solution)/shard_map/ppermute | solution.py:1040
  157.1 4.3 %collective-permute-start.40 = (f32[16,1024]{1,0:T(8,128)S(1)}, f32[16,1024]{1,0:T(8,128)S(1)}, u32[]{:S(2)}, u32[]{:S(2)}) collective-permute-start(f32[16,1024]{1,0:T(8,128)S(1)} %held.37.refs_4_), channel_id=1, source_target_pairs={{0,8},{4,12},{8,0},{12,4},{16,24},{20,28},{24,16},{28,20},{1,9},{5... | collective-permute-start | bytes 196616 | tf_op jit(solution)/shard_map/ppermute | solution.py:1040
  160.6 6.1 %collective-permute-start.42 = (f32[512,1024]{1,0:T(8,128)S(1)}, f32[512,1024]{1,0:T(8,128)S(1)}, u32[]{:S(2)}, u32[]{:S(2)}) collective-permute-start(f32[512,1024]{1,0:T(8,128)S(1)} %unproject.2.refs_4_.a_ref), channel_id=1, source_target_pairs={{0,1},{1,0},{2,3},{3,2},{4,5},{5,4},{6,7},{7,6},{8,9},{9,8},{10,11... | collective-permute-start | bytes 6291464 | tf_op jit(solution)/shard_map/ppermute | solution.py:1031
  163.6 8.2 %collective-permute-start.41 = (f32[512,1024]{1,0:T(8,128)S(1)}, f32[512,1024]{1,0:T(8,128)S(1)}, u32[]{:S(2)}, u32[]{:S(2)}) collective-permute-start(f32[512,1024]{1,0:T(8,128)S(1)} %unproject.3.a_ref), channel_id=1, source_target_pairs={{0,1},{1,0},{2,3},{3,2},{4,5},{5,4},{6,7},{7,6},{8,9},{9,8},{10,11... | collective-permute-start | bytes 6291464 | tf_op jit(solution)/shard_map/ppermute | solution.py:1031
  163.7 5.9 %collective-permute-start.43 = (f32[16,1024]{1,0:T(8,128)S(1)}, f32[16,1024]{1,0:T(8,128)S(1)}, u32[]{:S(2)}, u32[]{:S(2)}) collective-permute-start(f32[16,1024]{1,0:T(8,128)S(1)} %add.96.refs_5_.a_ref), channel_id=1, source_target_pairs={{0,4},{4,0},{8,12},{12,8},{16,20},{20,16},{24,28},{28,24},{1,5},{5... | collective-permute-start | bytes 196616 | tf_op jit(solution)/shard_map/ppermute | solution.py:1286
  (55 other events, 255.8 us)

commit v4 on v3

--- a/solution.py
+++ b/solution.py
@@ -666,10 +666,34 @@
     )(which, x, *terms, vectors, *after)
 
 
-def mlp_kernel(has_sum, which_ref, n_ref, g_ref, fc_ref, proj_ref, bias_ref, *refs):
+def through_kernel(g_ref, proj_ref, *refs):
+    grad = g_ref[...]
+    units = proj_ref.shape[0]
+    step = min(units, 256)
+    for at in range(0, units, step):
+        refs[-1][:, at : at + step] = nt(grad, proj_ref[at : at + step, :])
+
+
+def through(cotangent, proj, after=()):
+    length, width = cotangent.shape
+    units = proj.shape[0]
+    step = 256
+    return pl.pallas_call(
+        through_kernel,
+        grid=(length // step,),
+        in_specs=[pl.BlockSpec((step, width), lambda i: (i, 0)), once(proj.shape, (0, 0))]
+        + unread(after),
+        out_specs=pl.BlockSpec((step, units), lambda i: (i, 0)),
+        out_shape=jax.ShapeDtypeStruct((length, units), f32),
+        compiler_params=params(8),
+        cost_estimate=cost(2 * length * width * units, length * width * 6),
+        name="through",
+    )(cotangent, proj, *after)
+
+
+def mlp_kernel(which_ref, n_ref, through_ref, fc_ref, proj_ref, bias_ref, *refs):
     feed_ref, back_ref, act_ref, grad_ref = refs[-4:]
     normed = n_ref[...].astype(bf16)
-    grad = g_ref[...]
     units, step = fc_ref.shape[1], bias_ref.shape[1]
     for number, at in enumerate(range(0, units, step)):
         cols = slice(at, at + step)
@@ -681,35 +705,29 @@
         slope = gate + (0.5 * hidden) * (1.0 - inner * inner) * (
             0.7978845608028654 + 3.0 * 0.7978845608028654 * 0.044715 * square
         )
-        grad_ref[:, cols] = (nt(grad, proj_ref[cols, :]) * slope).astype(bf16)
-    feed = nn(act_ref[...], proj_ref[...])
-    back = nt(grad_ref[...], fc_ref[...])
-    if has_sum:
-        feed = feed + refs[0][...]
-        back = back + refs[1][...]
-    feed_ref[...] = feed
-    back_ref[...] = back
-
-
-def mlp(which, normed, cotangent, fc, proj, bias, bias_spec, sums=(), after=(), weight=1):
+        grad_ref[:, cols] = (through_ref[:, cols] * slope).astype(bf16)
+    feed_ref[...] = nn(act_ref[...], proj_ref[...])
+    back_ref[...] = nt(grad_ref[...], fc_ref[...])
+
+
+def mlp(which, normed, grads, fc, proj, bias, bias_spec, after=(), weight=1):
     half, width = normed.shape
     units = fc.shape[1]
     step = 256
     count = half // step
     block = pl.BlockSpec((step, width), lambda i, w: (i, 0))
     return pl.pallas_call(
-        functools.partial(mlp_kernel, bool(sums)),
+        mlp_kernel,
         grid_spec=pltpu.PrefetchScalarGridSpec(
             num_scalar_prefetch=1,
             grid=(count,),
             in_specs=[
                 block,
-                pl.BlockSpec((step, width), lambda i, w: (w[0] * count + i, 0)),
+                pl.BlockSpec((step, units), lambda i, w: (w[0] * count + i, 0)),
                 once(fc.shape, (0, 0)),
                 once(proj.shape, (0, 0)),
                 bias_spec,
             ]
-            + [block] * len(sums)
             + unread(after),
             out_specs=[block] * 2,
             scratch_shapes=[pltpu.VMEM((step, units), bf16)] * 2,
@@ -720,7 +738,7 @@
             weight * 8 * half * width * units, half * width * 16 + 4 * width * units, half * units
         ),
         name="mlp",
-    )(which, normed, cotangent, fc, proj, bias, *sums, *after)
+    )(which, normed, grads, fc, proj, bias, *after)
 
 
 def front_kernel(n_ref, fc_ref, bias_ref, *refs):
@@ -1148,8 +1166,10 @@
     pieces_qkv = joined(
         [(here + place + RING) % RING for place in far_places], qkv_w, [piece_qkv]
     )
+    own_grads = through(grad_out, proj_weight, [piece_qkv])
+    own_token = own_grads
     far_out = [
-        rebuilt(levels, far, parcel.part(length, parcel.piece), True, [pieces_qkv])
+        rebuilt(levels, far, parcel.part(length, parcel.piece), True, [pieces_qkv, own_token])
         for levels, far in zip(ring_out, far_out_parcel)
     ]
     lefts = [out] + far_out_parcel
@@ -1164,14 +1184,14 @@
     middle, normed = norm_two(mine, x, [keep, received], vectors, fc_held)
     other_normed = to_core(normed)
     own = (fc_weight, proj_weight, biases, fc_bias_spec)
-    keep_sums = mlp(mine, normed, grad_out, *own, (), (), OWN)
+    keep_sums = mlp(mine, normed, own_grads, *own, (), OWN)
     hold(ring_proj, [other_normed])
     hop(ring_proj)
     near_qkv = to_far(held([piece_qkv], [normed])[0])
     facing_proj = to_far(held([across_proj], facing_fc + [keep_sums[0]])[0])
     fc_spec, proj_spec = once(piece_fc.shape, (0, 0)), once(piece_proj.shape, (0, 0))
     send_sums = mlp(
-        theirs, other_normed, grad_out, *own, (), [keep_sums[0]] + last(ring_fc)
+        theirs, other_normed, own_grads, *own, [keep_sums[0]] + last(ring_fc)
     )
     ring_qkv = starting(near_qkv)
     hold(ring_qkv, [send_sums[0]] + last(ring_fc))

time: 176 us -> 176 us (level)
  Pallas kernels: 91.8 us -> 94.6 us
  waiting for transfers between devices: 33.6 us -> 31.8 us
    ppermute x22, waiting for transfers between devices: 25.4 us -> 20.8 us  [along(): return lax.ppermute(values, 'dp', hop)]
    ppermute x9, waiting for transfers between devices: 3.25 us -> 6.11 us  [to_far(): lax.ppermute(values, 'tensor', [(t, (t + shift) % group) for t in range(g...]
    pallas_call x2, Pallas kernels: 18.8 us -> 20.7 us  [attend_back(): pl.pallas_call(functools.partial(attend_back_kernel, prefix), grid=(1,),...]
    pallas_call x2 -> x3, Pallas kernels: 10.5 us -> 11.4 us  [the longest x2 8.42 us: mlp(): pl.pallas_call(mlp_kernel, grid_spec=pltpu.PrefetchScalarGridSpec(num_sca...]
  transfers between devices with their start and end apart: 44 -> 44, of which waited for: 13 -> 13; matrix products, arithmetic and copies ran while one was open for 1% -> 1% of each run, Pallas kernels for 50% -> 52%
where the time goes in v4:
time: 176 us; the launch traced here: 175 us
  Pallas kernels  94.6 us (54%)
  starting transfers between devices  39.8 us (23%)
  waiting for transfers between devices  31.8 us (18%)
  local copies, waits for them, and re-layouts  4.47 us (3%)
  between operations  2.5 us (1%)
    ppermute x22, starting transfers between devices, along(): return lax.ppermute(values, 'dp', hop)  22.6 us
    ppermute x22, waiting for transfers between devices, along(): return lax.ppermute(values, 'dp', hop)  20.8 us
    pallas_call x2, Pallas kernels, attend_back(): pl.pallas_call(functools.partial(attend_back_kernel, prefix), grid=(1,),...  20.7 us
    ppermute x9, starting transfers between devices, to_far(): lax.ppermute(values, 'tensor', [(t, (t + shift) % group) for t in range(g...  11.4 us
    pallas_call x2, Pallas kernels, project(): pl.pallas_call(functools.partial(project_kernel, first), grid=(length //...  8.97 us
    pallas_call x2, Pallas kernels, mlp(): pl.pallas_call(mlp_kernel, grid_spec=pltpu.PrefetchScalarGridSpec(num_sca...  8.42 us
    pallas_call x1, Pallas kernels, attend(): pl.pallas_call(functools.partial(attend_kernel, prefix, parcel), grid=(1,...  8.06 us
    pallas_call x2, Pallas kernels, rest(): pl.pallas_call(rest_kernel, grid_spec=pltpu.PrefetchScalarGridSpec(num_sc...  7.58 us
  transfers between devices with their start and end apart: 44, of which 13 were waited for; matrix products, arithmetic and copies ran while one was open for 1% of the time, Pallas kernels for 52%

profile of v4, /device:TPU:0, one launch (start us, length us, event | category | flops | bytes accessed | tf_op | source)
XLA Modules:
  0.0 174.5 jit_solution(8743363275964797884)
XLA Ops:
  1.8 3.0 %collective-permute-start = (f32[128,1024]{1,0:T(8,128)S(1)}, f32[128,1024]{1,0:T(8,128)S(1)}, u32[]{:S(2)}, u32[]{:S(2)}) collective-permute-start(f32[128,1024]{1,0:T(8,128)S(1)} %pick.4.refs_1_), channel_id=1, source_target_pairs={{0,2},{1,3},{2,0},{3,1},{4,6},{5,7},{6,4},{7,5},{8,10},{9,11},{10,... | collective-permute-start | bytes 1572872 | tf_op jit(solution)/shard_map/ppermute | solution.py:1053
  5.9 1.8 %pick.7 = f32[128,1024]{1,0:T(8,128)} custom-call(s32[1]{0:T(128)} %bitcast.2.which_ref.order_ref, bf16[1024,1024]{1,0:T(8,128)(2,1)} %proj_ref.5, f32[32,1024]{1,0:T(8,128)S(1)} %pick.5.refs_1_), custom_call_target="tpu_custom_call" | custom-call | bytes 49152 | tf_op jit(solution)/shard_map/pick/pallas_call | solution.py:517
  7.7 2.0 %collective-permute-start.11 = (f32[128,1024]{1,0:T(8,128)}, f32[128,1024]{1,0:T(8,128)}, u32[]{:S(2)}, u32[]{:S(2)}) collective-permute-start(f32[128,1024]{1,0:T(8,128)} %pick.7), channel_id=1, source_target_pairs={{0,2},{1,3},{2,0},{3,1},{4,6},{5,7},{6,4},{7,5},{8,10},{9,11},{10,... | collective-permute-start | bytes 1572872 | tf_op jit(solution)/shard_map/ppermute | solution.py:1053
  9.9 5.1 %project.2 = (bf16[1024,768]{1,0:T(8,128)(2,1)S(1)}, bf16[1024,1024]{1,0:T(8,128)(2,1)}) custom-call(bf16[1024,1024]{1,0:T(8,128)(2,1)} %bitcast.31, bf16[1024,1024]{1,0:T(8,128)(2,1)} %bitcast.32, f32[8,1024]{1,0:T(8,128)S(1)} %pad_convert_fusion.vec_ref, bf16[3,1024,256]{2,1,0:T(8,128)(2,1)S(1)} %bitcast.28, f32[16,256]{1,0:T(8,128)S(1)} %fusion.12.bias_ref), custom_call_target="tpu_custom_call" | custom-call | flops 100663296 | bytes 524288 | tf_op jit(solution)/shard_map/project/pallas_call | solution.py:187
  15.1 2.5 %collective-permute-done.refs_0_ = f32[128,1024]{1,0:T(8,128)S(1)} collective-permute-done((f32[128,1024]{1,0:T(8,128)S(1)}, f32[128,1024]{1,0:T(8,128)S(1)}, u32[]{:S(2)}, u32[]{:S(2)}) %collective-permute-start) | collective-permute-done | bytes 524320 | tf_op jit(solution)/shard_map/ppermute | solution.py:1053
  17.6 2.0 %collective-permute-start.3 = (f32[128,1024]{1,0:T(8,128)S(1)}, f32[128,1024]{1,0:T(8,128)}, u32[]{:S(2)}, u32[]{:S(2)}) collective-permute-start(f32[128,1024]{1,0:T(8,128)S(1)} %held.19.refs_0_.refs_1_), channel_id=1, source_target_pairs={{0,4},{8,0},{16,8},{24,16},{28,24},{20,28},{12,20},{4,12},{1,5},{9... | collective-permute-start | bytes 1572872 | tf_op jit(solution)/shard_map/ppermute | solution.py:1073
  20.4 2.0 %collective-permute-start.5 = (f32[32,1024]{1,0:T(8,128)S(1)}, f32[32,1024]{1,0:T(8,128)S(1)}, u32[]{:S(2)}, u32[]{:S(2)}) collective-permute-start(f32[32,1024]{1,0:T(8,128)S(1)} %held.20.refs_2_.refs_3_.refs_0_), channel_id=1, source_target_pairs={{0,4},{8,0},{16,8},{24,16},{28,24},{20,28},{12,20},{4,12},{1,5},{9... | collective-permute-start | bytes 393224 | tf_op jit(solution)/shard_map/ppermute | solution.py:1073
  23.3 8.1 %attend.1 = (f32[1216,256]{1,0:T(8,128)S(1)}, f32[8,128]{1,0:T(8,128)S(1)}) custom-call(s32[8]{0:T(128)S(1)} %bitcast.40, s32[1]{0:T(128)S(6)} %copy.92.pads_ref, bf16[1024,768]{1,0:T(8,128)(2,1)S(1)} %get-tuple-element.63.refs_1_.qkv_ref, f32[32,256]{1,0:T(8,128)S(1)} %pad_maximum_fusion.1.kv_ref, f32[16,256]{1,0:T(8,128)S(1)} %fusion.12.bias_ref, ...), custom_call_target="tpu_custom_call" | custom-call | flops 67108864 | bytes 163840 | tf_op jit(solution)/shard_map/attend/pallas_call | solution.py:257
  33.9 1.6 collective-permute-start.6
  35.5 1.6 collective-permute-start.13
  38.1 1.5 collective-permute-start.8
  39.6 12.5 %collective-permute-done.7.refs_3_.refs_4_ = f32[32,1024]{1,0:T(8,128)S(1)} collective-permute-done((f32[32,1024]{1,0:T(8,128)S(1)}, f32[32,1024]{1,0:T(8,128)S(1)}, u32[]{:S(2)}, u32[]{:S(2)}) %collective-permute-start.7) | collective-permute-done | bytes 131104 | tf_op jit(solution)/shard_map/ppermute | solution.py:1073
  52.5 1.6 collective-permute-start.10
  54.6 1.6 collective-permute-start.15
  56.2 2.4 %collective-permute-done.9.refs_4_.refs_5_.refs_2_ = f32[32,1024]{1,0:T(8,128)S(1)} collective-permute-done((f32[32,1024]{1,0:T(8,128)S(1)}, f32[32,1024]{1,0:T(8,128)S(1)}, u32[]{:S(2)}, u32[]{:S(2)}) %collective-permute-start.9) | collective-permute-done | bytes 131104 | tf_op jit(solution)/shard_map/ppermute | solution.py:1073
  59.6 1.6 collective-permute-start.18
  63.2 1.8 %pick.6 = (f32[128,1024]{1,0:T(8,128)S(1)}, f32[128,1024]{1,0:T(8,128)S(1)}, f32[3,128,256]{2,1,0:T(8,128)S(1)}, f32[3,128,256]{2,1,0:T(8,128)S(1)}) custom-call(s32[4]{0:T(128)S(1)} %pad_add_fusion.1.which_ref, bf16[1024,1024]{1,0:T(8,128)(2,1)} %fc_ref.3, bf16[1024,1024]{1,0:T(8,128)(2,1)} %proj_ref.5, bf16[3,1024,256]{2,1,0:T(8,128)(2,1)} %bitcast.25, ...), custom_call_target="tpu_custom_call" | custom-call | bytes 122880 | tf_op jit(solution)/shard_map/pick/pallas_call | solution.py:517
  65.1 1.7 joined.1.refs_8_.refs_0_
  66.9 3.0 %through.1.refs_9_.through_ref = f32[1024,1024]{1,0:T(8,128)S(1)} custom-call(bf16[1024,1024]{1,0:T(8,128)(2,1)S(1)} %bitcast.36, bf16[1024,1024]{1,0:T(8,128)(2,1)S(1)} %copy-done.4, f32[3,128,256]{2,1,0:T(8,128)S(1)} %get-tuple-element.68.refs_0_), custom_call_target="tpu_custom_call" | custom-call | flops 134217728 | bytes 393216 | tf_op jit(solution)/shard_map/through/pallas_call | solution.py:681
  72.5 2.9 %collective-permute-done.17.refs_2_.refs_0_ = f32[128,1024]{1,0:T(8,128)} collective-permute-done((f32[128,1024]{1,0:T(8,128)}, f32[128,1024]{1,0:T(8,128)}, u32[]{:S(2)}, u32[]{:S(2)}) %collective-permute-start.17) | collective-permute-done | bytes 524320 | tf_op jit(solution)/shard_map/ppermute | solution.py:1073
  75.9 1.6 collective-permute-start.20
  80.0 4.2 %mlp.2 = (f32[512,1024]{1,0:T(8,128)S(1)}, f32[512,1024]{1,0:T(8,128)S(1)}) custom-call(s32[1]{0:T(128)} %bitcast.which_ref.core_ref, f32[512,1024]{1,0:T(8,128)S(1)} %get-tuple-element.75.n_ref.refs_1_, f32[1024,1024]{1,0:T(8,128)S(1)} %through.1.refs_9_.through_ref, bf16[1024,1024]{1,0:T(8,128)(2,1)S(1)} %copy-done.5, bf16[1024,1024]{1,0:T(8,128)(2,1)S(1)} %copy-done.4, ...), custom_call_target="tpu_custom_call" | custom-call | flops 85899345920 | bytes 786432 | tf_op jit(solution)/shard_map/mlp/pallas_call | solution.py:719
  84.2 2.1 %collective-permute-done.21.refs_7_.refs_1_ = f32[128,1024]{1,0:T(8,128)S(1)} collective-permute-done((f32[128,1024]{1,0:T(8,128)S(1)}, f32[128,1024]{1,0:T(8,128)S(1)}, u32[]{:S(2)}, u32[]{:S(2)}) %collective-permute-start.21) | collective-permute-done | bytes 524320 | tf_op jit(solution)/shard_map/ppermute | solution.py:1053
  87.3 1.5 collective-permute-start.24
  88.9 1.5 collective-permute-start.27
  90.4 4.2 %mlp.3 = (f32[512,1024]{1,0:T(8,128)S(1)}, f32[512,1024]{1,0:T(8,128)S(1)}) custom-call(s32[1]{0:T(128)S(6)} %sub.11.which_ref, f32[512,1024]{1,0:T(8,128)S(1)} %collective-permute-done.22.n_ref.refs_2_, f32[1024,1024]{1,0:T(8,128)S(1)} %through.1.refs_9_.through_ref, bf16[1024,1024]{1,0:T(8,128)(2,1)S(1)} %copy-done.5, bf16[1024,1024]{1,0:T(8,128)(2,1)S(1)} %copy-done.4, ...), custom_call_target="tpu_custom_call" | custom-call | flops 268435456 | bytes 786432 | tf_op jit(solution)/shard_map/mlp/pallas_call | solution.py:719
  96.0 2.5 %mlp_front.2 = (bf16[512,1024]{1,0:T(8,128)(2,1)S(1)}, f32[512,1024]{1,0:T(8,128)S(1)}) custom-call(f32[512,1024]{1,0:T(8,128)S(1)} %collective-permute-done.22.n_ref.refs_2_, bf16[1024,1024]{1,0:T(8,128)(2,1)S(1)} %assemble.5.fc_ref, f32[1216,256]{1,0:T(8,128)S(1)} %collective-permute-done.6.refs_7_.refs_1_.bias_ref.kv_ref.lse_ref), custom_call_target="tpu_custom_call" | custom-call | flops 67108864 | bytes 327680 | tf_op jit(solution)/shard_map/mlp_front/pallas_call | solution.py:765
  98.5 2.5 %mlp_front.3 = (bf16[512,1024]{1,0:T(8,128)(2,1)S(1)}, f32[512,1024]{1,0:T(8,128)S(1)}) custom-call(f32[512,1024]{1,0:T(8,128)S(1)} %get-tuple-element.75.n_ref.refs_1_, bf16[1024,1024]{1,0:T(8,128)(2,1)S(1)} %assemble.5.fc_ref, f32[1216,256]{1,0:T(8,128)S(1)} %collective-permute-done.6.refs_7_.refs_1_.bias_ref.kv_ref.lse_ref, ...), custom_call_target="tpu_custom_call" | custom-call | flops 67108864 | bytes 327680 | tf_op jit(solution)/shard_map/mlp_front/pallas_call | solution.py:765
  101.1 1.9 %assemble.6.proj_ref = bf16[1024,1024]{1,0:T(8,128)(2,1)S(1)} custom-call(s32[1]{0:T(128)} %bitcast.2.which_ref.order_ref, f32[128,1024]{1,0:T(8,128)} %held.23.refs_0_, f32[128,1024]{1,0:T(8,128)} %get-tuple-element.71.refs_1_, f32[128,1024]{1,0:T(8,128)} %get-tuple-element.72.refs_2_, f32[128,1024]{1,0:T(8,128)} %get-tuple-element.82.refs_3_, ...), custom_call_target="tpu_custom_call" | custom-call | bytes 393216 | tf_op jit(solution)/shard_map/assemble/pallas_call | solution.py:553
  103.0 3.8 %mlp_rest.2 = (f32[512,1024]{1,0:T(8,128)S(1)}, f32[512,1024]{1,0:T(8,128)S(1)}) custom-call(s32[1]{0:T(128)S(6)} %sub.11.which_ref, bf16[512,1024]{1,0:T(8,128)(2,1)S(1)} %get-tuple-element.79.refs_0_.act_ref, f32[512,1024]{1,0:T(8,128)S(1)} %get-tuple-element.86.slope_ref, bf16[1024,1024]{1,0:T(8,128)(2,1)S(1)} %bitcast.37, ...), custom_call_target="tpu_custom_call" | custom-call | flops 3221225472 | bytes 786432 | tf_op jit(solution)/shard_map/mlp_rest/pallas_call | solution.py:804
  108.2 1.6 collective-permute-start.29
  111.3 3.8 %mlp_rest.3 = (f32[512,1024]{1,0:T(8,128)S(1)}, f32[512,1024]{1,0:T(8,128)S(1)}) custom-call(s32[1]{0:T(128)} %bitcast.which_ref.core_ref, bf16[512,1024]{1,0:T(8,128)(2,1)S(1)} %get-tuple-element.80.act_ref, f32[512,1024]{1,0:T(8,128)S(1)} %get-tuple-element.81.refs_8_.slope_ref, bf16[1024,1024]{1,0:T(8,128)(2,1)S(1)} %bitcast.38, ...), custom_call_target="tpu_custom_call" | custom-call | flops 64424509440 | bytes 786432 | tf_op jit(solution)/shard_map/mlp_rest/pallas_call | solution.py:804
  115.0 2.9 %collective-permute-done.30.b_ref = f32[512,1024]{1,0:T(8,128)S(1)} collective-permute-done((f32[512,1024]{1,0:T(8,128)S(1)}, f32[512,1024]{1,0:T(8,128)S(1)}, u32[]{:S(2)}, u32[]{:S(2)}) %collective-permute-start.30) | collective-permute-done | bytes 2097184 | tf_op jit(solution)/shard_map/ppermute | solution.py:1049
  117.9 1.6 norm_two_back.1.refs_2_.keep_ref.refs_1_.upper_ref
  119.8 1.7 result.1
  121.9 1.5 collective-permute-start.36
  123.9 1.6 collective-permute-start.35
  125.6 2.3 %heads_back.1 = (bf16[1024,256]{1,0:T(8,128)(2,1)S(1)}, bf16[1024,256]{1,0:T(8,128)(2,1)S(1)}) custom-call(s32[1]{0:T(128)} %bitcast.which_ref.core_ref, f32[512,1024]{1,0:T(8,128)S(1)} %norm_two_back.1.refs_2_.keep_ref.refs_1_.upper_ref, f32[512,1024]{1,0:T(8,128)S(1)} %collective-permute-done.33.other_ref.upper_ref, bf16[256,1024]{1,0:T(8,128)(2,1)S(1)} %copy-done.11, ...), custom_call_target="tpu_custom_call" | custom-call | flops 67108864 | bytes 327680 | tf_op jit(solution)/shard_map/heads_back/pallas_call | solution.py:331
  127.9 10.2 %attend_back.2 = (bf16[1024,768]{1,0:T(8,128)(2,1)S(1)}, f32[16,256]{1,0:T(8,128)S(1)}, f32[16,256]{1,0:T(8,128)S(1)}) custom-call(s32[8]{0:T(128)S(1)} %bitcast.41, s32[1]{0:T(128)S(6)} %copy.92.pads_ref, bf16[1024,768]{1,0:T(8,128)(2,1)S(1)} %copy-done.8, bf16[1024,256]{1,0:T(8,128)(2,1)S(1)} %get-tuple-element.99.do_ref, ...), custom_call_target="tpu_custom_call" | custom-call | flops 2684354560 | bytes 655360 | tf_op jit(solution)/shard_map/attend_back/pallas_call | solution.py:412
  140.3 1.5 place.1
  142.0 3.9 %project.3.qkv_ref.refs_1_ = bf16[1024,768]{1,0:T(8,128)(2,1)S(1)} custom-call(bf16[1024,1024]{1,0:T(8,128)(2,1)} %get-tuple-element.102.x_ref.y_ref, bf16[1024,1024]{1,0:T(8,128)(2,1)} %get-tuple-element.102.x_ref.y_ref, f32[8,1024]{1,0:T(8,128)S(1)} %copy-done.28, bf16[3,1024,256]{2,1,0:T(8,128)(2,1)S(1)} %assemble.7.w_ref.refs_3_, ...), custom_call_target="tpu_custom_call" | custom-call | flops 100663296 | bytes 524288 | tf_op jit(solution)/shard_map/project/pallas_call | solution.py:187
  147.1 10.6 %attend_back.3 = (bf16[1024,768]{1,0:T(8,128)(2,1)S(1)}, f32[16,256]{1,0:T(8,128)}, f32[16,256]{1,0:T(8,128)}) custom-call(s32[8]{0:T(128)S(1)} %bitcast.42, s32[1]{0:T(128)S(6)} %copy.92.pads_ref, bf16[1024,768]{1,0:T(8,128)(2,1)S(1)} %project.3.qkv_ref.refs_1_, bf16[1024,256]{1,0:T(8,128)(2,1)S(1)} %get-tuple-element.108.do_ref, ...), custom_call_target="tpu_custom_call" | custom-call | flops 2684354560 | bytes 655360 | tf_op jit(solution)/shard_map/attend_back/pallas_call | solution.py:412
  159.1 2.0 %unproject.2.refs_4_.a_ref = f32[512,1024]{1,0:T(8,128)S(1)} custom-call(s32[1]{0:T(128)S(6)} %sub.11.which_ref, bf16[1024,768]{1,0:T(8,128)(2,1)S(1)} %get-tuple-element.100.refs_1_.refs_0_, bf16[1024,768]{1,0:T(8,128)(2,1)S(1)} %get-tuple-element.109.refs_1_, bf16[3,1024,256]{2,1,0:T(8,128)(2,1)S(1)} %bitcast.29, ...), custom_call_target="tpu_custom_call" | custom-call | flops 100663296 | bytes 262144 | tf_op jit(solution)/shard_map/unproject/pallas_call | solution.py:619
  162.1 2.0 %unproject.3.a_ref = f32[512,1024]{1,0:T(8,128)S(1)} custom-call(s32[1]{0:T(128)} %bitcast.which_ref.core_ref, bf16[1024,768]{1,0:T(8,128)(2,1)S(1)} %get-tuple-element.100.refs_1_.refs_0_, bf16[1024,768]{1,0:T(8,128)(2,1)S(1)} %get-tuple-element.109.refs_1_, bf16[3,1024,256]{2,1,0:T(8,128)(2,1)S(1)} %bitcast.30, ...), custom_call_target="tpu_custom_call" | custom-call | flops 100663296 | bytes 262144 | tf_op jit(solution)/shard_map/unproject/pallas_call | solution.py:619
  164.3 1.6 collective-permute-start.43
  166.6 2.8 %norm_one_back.2 = (f32[1024,1024]{1,0:T(8,128)}, f32[8,128]{1,0:T(8,128)S(1)}) custom-call(s32[1]{0:T(128)} %bitcast.which_ref.core_ref, bf16[1024,1024]{1,0:T(8,128)(2,1)S(1)} %bitcast.34, f32[512,1024]{1,0:T(8,128)S(1)} %norm_two_back.1.refs_2_.keep_ref.refs_1_.upper_ref, f32[8,1024]{1,0:T(8,128)S(1)} %copy-done.28, f32[512,1024]{1,0:T(8,128)S(1)} %unproject.3.a_ref, ...), custom_call_target="tpu_custom_call" | custom-call | flops 655360 | bytes 589824 | tf_op jit(solution)/shard_map/norm_one_back/pallas_call | solution.py:875
  169.5 2.2 %prefix_grads.1 = (f32[1024,512]{1,0:T(8,128)}, f32[512,2,256]{2,1,0:T(2,128)}, f32[1,512]{1,0:T(1,128)}, f32[2,256]{1,0:T(2,128)}, f32[16,1024]{1,0:T(8,128)}) custom-call(f32[16,1024]{1,0:T(8,128)S(1)} %add.96.refs_5_.a_ref, f32[16,1024]{1,0:T(8,128)S(1)} %collective-permute-done.43.b_ref, f32[16,512]{1,0:T(8,128)S(1)} %pad.30.trunk_ref, ...), custom_call_target="tpu_custom_call" | custom-call | bytes 262144 | tf_op jit(solution)/shard_map/prefix_grads/pallas_call | solution.py:998
  171.7 2.8 %norm_one_back.3 = (f32[1024,1024]{1,0:T(8,128)}, f32[8,128]{1,0:T(8,128)}) custom-call(s32[1]{0:T(128)S(6)} %sub.11.which_ref, bf16[1024,1024]{1,0:T(8,128)(2,1)S(1)} %bitcast.35, f32[512,1024]{1,0:T(8,128)S(1)} %collective-permute-done.33.other_ref.upper_ref, f32[8,1024]{1,0:T(8,128)S(1)} %copy-done.28, ...), custom_call_target="tpu_custom_call", output_to_operand_aliasing={{0}: (6, {})} | custom-call | flops 655360 | bytes 589824 | tf_op jit(solution)/shard_map/norm_one_back/pallas_call | solution.py:875
  (239 shorter events, 29.2 us)
Async XLA Ops:
  1.8 15.8 %collective-permute-start = (f32[128,1024]{1,0:T(8,128)S(1)}, f32[128,1024]{1,0:T(8,128)S(1)}, u32[]{:S(2)}, u32[]{:S(2)}) collective-permute-start(f32[128,1024]{1,0:T(8,128)S(1)} %pick.4.refs_1_), channel_id=1, source_target_pairs={{0,2},{1,3},{2,0},{3,1},{4,6},{5,7},{6,4},{7,5},{8,10},{9,11},{10,... | collective-permute-start | bytes 1572872 | tf_op jit(solution)/shard_map/ppermute | solution.py:1053
  5.7 14.7 %collective-permute-start.1 = (f32[32,1024]{1,0:T(8,128)S(1)}, f32[32,1024]{1,0:T(8,128)S(1)}, u32[]{:S(2)}, u32[]{:S(2)}) collective-permute-start(f32[32,1024]{1,0:T(8,128)S(1)} %pick.5.refs_1_), channel_id=1, source_target_pairs={{0,2},{1,3},{2,0},{3,1},{4,6},{5,7},{6,4},{7,5},{8,10},{9,11},{10,... | collective-permute-start | bytes 393224 | tf_op jit(solution)/shard_map/ppermute | solution.py:1053
  7.7 27.8 %collective-permute-start.11 = (f32[128,1024]{1,0:T(8,128)}, f32[128,1024]{1,0:T(8,128)}, u32[]{:S(2)}, u32[]{:S(2)}) collective-permute-start(f32[128,1024]{1,0:T(8,128)} %pick.7), channel_id=1, source_target_pairs={{0,2},{1,3},{2,0},{3,1},{4,6},{5,7},{6,4},{7,5},{8,10},{9,11},{10,... | collective-permute-start | bytes 1572872 | tf_op jit(solution)/shard_map/ppermute | solution.py:1053
  17.6 13.7 %copy-start.12 = (f32[128,1024]{1,0:T(8,128)}, f32[128,1024]{1,0:T(8,128)S(1)}, u32[]{:S(2)}) copy-start(f32[128,1024]{1,0:T(8,128)S(1)} %held.19.refs_0_.refs_1_) | copy-start | bytes 1572868
  17.6 16.2 %collective-permute-start.3 = (f32[128,1024]{1,0:T(8,128)S(1)}, f32[128,1024]{1,0:T(8,128)}, u32[]{:S(2)}, u32[]{:S(2)}) collective-permute-start(f32[128,1024]{1,0:T(8,128)S(1)} %held.19.refs_0_.refs_1_), channel_id=1, source_target_pairs={{0,4},{8,0},{16,8},{24,16},{28,24},{20,28},{12,20},{4,12},{1,5},{9... | collective-permute-start | bytes 1572872 | tf_op jit(solution)/shard_map/ppermute | solution.py:1073
  19.6 14.2 %collective-permute-start.2 = (f32[128,1024]{1,0:T(8,128)S(1)}, f32[128,1024]{1,0:T(8,128)}, u32[]{:S(2)}, u32[]{:S(2)}) collective-permute-start(f32[128,1024]{1,0:T(8,128)S(1)} %held.19.refs_0_.refs_1_), channel_id=1, source_target_pairs={{0,8},{8,16},{16,24},{24,28},{28,20},{20,12},{12,4},{4,0},{1,9},{9... | collective-permute-start | bytes 1572872 | tf_op jit(solution)/shard_map/ppermute | solution.py:1073
  20.4 13.4 %copy-start.9 = (bf16[256,1024]{1,0:T(8,128)(2,1)S(1)}, bf16[256,1024]{1,0:T(8,128)(2,1)}, u32[]{:S(2)}) copy-start(bf16[256,1024]{1,0:T(8,128)(2,1)} %refs_0_.9) | copy-start | bytes 1572868
  20.4 12.2 %collective-permute-start.5 = (f32[32,1024]{1,0:T(8,128)S(1)}, f32[32,1024]{1,0:T(8,128)S(1)}, u32[]{:S(2)}, u32[]{:S(2)}) collective-permute-start(f32[32,1024]{1,0:T(8,128)S(1)} %held.20.refs_2_.refs_3_.refs_0_), channel_id=1, source_target_pairs={{0,4},{8,0},{16,8},{24,16},{28,24},{20,28},{12,20},{4,12},{1,5},{9... | collective-permute-start | bytes 393224 | tf_op jit(solution)/shard_map/ppermute | solution.py:1073
  22.4 11.4 %collective-permute-start.4 = (f32[32,1024]{1,0:T(8,128)S(1)}, f32[32,1024]{1,0:T(8,128)S(1)}, u32[]{:S(2)}, u32[]{:S(2)}) collective-permute-start(f32[32,1024]{1,0:T(8,128)S(1)} %held.20.refs_2_.refs_3_.refs_0_), channel_id=1, source_target_pairs={{0,8},{8,16},{16,24},{24,28},{28,20},{20,12},{12,4},{4,0},{1,9},{9... | collective-permute-start | bytes 393224 | tf_op jit(solution)/shard_map/ppermute | solution.py:1073
  33.9 36.1 %collective-permute-start.6 = (f32[1216,256]{1,0:T(8,128)S(1)}, f32[1216,256]{1,0:T(8,128)S(1)}, u32[]{:S(2)}, u32[]{:S(2)}) collective-permute-start(f32[1216,256]{1,0:T(8,128)S(1)} %held.21.refs_2_.refs_0_.kv_ref.lse_ref), channel_id=1, source_target_pairs={{0,2},{1,3},{2,0},{3,1},{4,6},{5,7},{6,4},{7,5},{8,10},{9,11},{10,... | collective-permute-start | bytes 3735560 | tf_op jit(solution)/shard_map/ppermute | solution.py:1053
  35.4 23.5 %copy-start.20 = (f32[32,1024]{1,0:T(8,128)}, f32[32,1024]{1,0:T(8,128)S(1)}, u32[]{:S(2)}) copy-start(f32[32,1024]{1,0:T(8,128)S(1)} %get-tuple-element.67.refs_2_) | copy-start | bytes 393220
  35.4 23.5 %copy-start.22 = (f32[32,1024]{1,0:T(8,128)}, f32[32,1024]{1,0:T(8,128)S(1)}, u32[]{:S(2)}) copy-start(f32[32,1024]{1,0:T(8,128)S(1)} %get-tuple-element.66.refs_1_) | copy-start | bytes 393220
  35.5 18.7 %collective-permute-start.13 = (f32[128,1024]{1,0:T(8,128)}, f32[128,1024]{1,0:T(8,128)}, u32[]{:S(2)}, u32[]{:S(2)}) collective-permute-start(f32[128,1024]{1,0:T(8,128)} %held.23.refs_0_), channel_id=1, source_target_pairs={{0,4},{8,0},{16,8},{24,16},{28,24},{20,28},{12,20},{4,12},{1,5},{9... | collective-permute-start | bytes 1572872 | tf_op jit(solution)/shard_map/ppermute | solution.py:1073
  37.1 17.0 %collective-permute-start.12 = (f32[128,1024]{1,0:T(8,128)}, f32[128,1024]{1,0:T(8,128)}, u32[]{:S(2)}, u32[]{:S(2)}) collective-permute-start(f32[128,1024]{1,0:T(8,128)} %held.23.refs_0_), channel_id=1, source_target_pairs={{0,8},{8,16},{16,24},{24,28},{28,20},{20,12},{12,4},{4,0},{1,9},{9... | collective-permute-start | bytes 1572872 | tf_op jit(solution)/shard_map/ppermute | solution.py:1073
  37.5 14.5 %collective-permute-start.7 = (f32[32,1024]{1,0:T(8,128)S(1)}, f32[32,1024]{1,0:T(8,128)S(1)}, u32[]{:S(2)}, u32[]{:S(2)}) collective-permute-start(f32[32,1024]{1,0:T(8,128)S(1)} %get-tuple-element.66.refs_1_), channel_id=1, source_target_pairs={{0,8},{8,16},{16,24},{24,28},{28,20},{20,12},{12,4},{4,0},{1,9},{9... | collective-permute-start | bytes 393224 | tf_op jit(solution)/shard_map/ppermute | solution.py:1073
  38.1 14.5 %collective-permute-start.8 = (f32[32,1024]{1,0:T(8,128)S(1)}, f32[32,1024]{1,0:T(8,128)S(1)}, u32[]{:S(2)}, u32[]{:S(2)}) collective-permute-start(f32[32,1024]{1,0:T(8,128)S(1)} %get-tuple-element.67.refs_2_), channel_id=1, source_target_pairs={{0,4},{8,0},{16,8},{24,16},{28,24},{20,28},{12,20},{4,12},{1,5},{9... | collective-permute-start | bytes 393224 | tf_op jit(solution)/shard_map/ppermute | solution.py:1073
  52.1 6.4 %collective-permute-start.9 = (f32[32,1024]{1,0:T(8,128)S(1)}, f32[32,1024]{1,0:T(8,128)S(1)}, u32[]{:S(2)}, u32[]{:S(2)}) collective-permute-start(f32[32,1024]{1,0:T(8,128)S(1)} %collective-permute-done.7.refs_3_.refs_4_), channel_id=1, source_target_pairs={{0,8},{8,16},{16,24},{24,28},{28,20},{20,12},{12,4},{4,0},{1,9},{9... | collective-permute-start | bytes 393224 | tf_op jit(solution)/shard_map/ppermute | solution.py:1073
  52.5 6.4 %collective-permute-start.10 = (f32[32,1024]{1,0:T(8,128)S(1)}, f32[32,1024]{1,0:T(8,128)S(1)}, u32[]{:S(2)}, u32[]{:S(2)}) collective-permute-start(f32[32,1024]{1,0:T(8,128)S(1)} %collective-permute-done.8.refs_4_.refs_5_), channel_id=1, source_target_pairs={{0,4},{8,0},{16,8},{24,16},{28,24},{20,28},{12,20},{4,12},{1,5},{9... | collective-permute-start | bytes 393224 | tf_op jit(solution)/shard_map/ppermute | solution.py:1073
  54.1 16.0 %collective-permute-start.14 = (f32[128,1024]{1,0:T(8,128)}, f32[128,1024]{1,0:T(8,128)S(1)}, u32[]{:S(2)}, u32[]{:S(2)}) collective-permute-start(f32[128,1024]{1,0:T(8,128)} %get-tuple-element.69.refs_1_), channel_id=1, source_target_pairs={{0,8},{8,16},{16,24},{24,28},{28,20},{20,12},{12,4},{4,0},{1,9},{9... | collective-permute-start | bytes 1572872 | tf_op jit(solution)/shard_map/ppermute | solution.py:1073
  54.6 15.6 %collective-permute-start.15 = (f32[128,1024]{1,0:T(8,128)}, f32[128,1024]{1,0:T(8,128)S(1)}, u32[]{:S(2)}, u32[]{:S(2)}) collective-permute-start(f32[128,1024]{1,0:T(8,128)} %get-tuple-element.70.refs_2_), channel_id=1, source_target_pairs={{0,4},{8,0},{16,8},{24,16},{28,24},{20,28},{12,20},{4,12},{1,5},{9... | collective-permute-start | bytes 1572872 | tf_op jit(solution)/shard_map/ppermute | solution.py:1073
  59.2 16.3 %collective-permute-start.17 = (f32[128,1024]{1,0:T(8,128)}, f32[128,1024]{1,0:T(8,128)}, u32[]{:S(2)}, u32[]{:S(2)}) collective-permute-start(f32[128,1024]{1,0:T(8,128)} %get-tuple-element.71.refs_1_), channel_id=1, source_target_pairs={{0,8},{8,16},{16,24},{24,28},{28,20},{20,12},{12,4},{4,0},{1,9},{9... | collective-permute-start | bytes 1572872 | tf_op jit(solution)/shard_map/ppermute | solution.py:1073
  59.6 15.8 %collective-permute-start.18 = (f32[128,1024]{1,0:T(8,128)}, f32[128,1024]{1,0:T(8,128)}, u32[]{:S(2)}, u32[]{:S(2)}) collective-permute-start(f32[128,1024]{1,0:T(8,128)} %get-tuple-element.72.refs_2_), channel_id=1, source_target_pairs={{0,4},{8,0},{16,8},{24,16},{28,24},{20,28},{12,20},{4,12},{1,5},{9... | collective-permute-start | bytes 1572872 | tf_op jit(solution)/shard_map/ppermute | solution.py:1073
  71.9 6.6 %collective-permute-start.16 = (f32[512,1024]{1,0:T(8,128)S(1)}, f32[512,1024]{1,0:T(8,128)S(1)}, u32[]{:S(2)}, u32[]{:S(2)}) collective-permute-start(f32[512,1024]{1,0:T(8,128)S(1)} %half_product.2.refs_4_), channel_id=1, source_target_pairs={{0,1},{1,0},{2,3},{3,2},{4,5},{5,4},{6,7},{7,6},{8,9},{9,8},{10,11... | collective-permute-start | bytes 6291464 | tf_op jit(solution)/shard_map/ppermute | solution.py:1049
  72.0 14.3 %collective-permute-start.21 = (f32[128,1024]{1,0:T(8,128)S(1)}, f32[128,1024]{1,0:T(8,128)S(1)}, u32[]{:S(2)}, u32[]{:S(2)}) collective-permute-start(f32[128,1024]{1,0:T(8,128)S(1)} %held.27), channel_id=1, source_target_pairs={{0,2},{1,3},{2,0},{3,1},{4,6},{5,7},{6,4},{7,5},{8,10},{9,11},{10,... | collective-permute-start | bytes 1572872 | tf_op jit(solution)/shard_map/ppermute | solution.py:1053
  75.5 13.4 %collective-permute-start.19 = (f32[128,1024]{1,0:T(8,128)S(1)}, f32[128,1024]{1,0:T(8,128)S(1)}, u32[]{:S(2)}, u32[]{:S(2)}) collective-permute-start(f32[128,1024]{1,0:T(8,128)S(1)} %get-tuple-element.73.refs_0_.refs_3_), channel_id=1, source_target_pairs={{0,8},{8,16},{16,24},{24,28},{28,20},{20,12},{12,4},{4,0},{1,9},{9... | collective-permute-start | bytes 1572872 | tf_op jit(solution)/shard_map/ppermute | solution.py:1073
  75.9 14.4 %collective-permute-start.20 = (f32[128,1024]{1,0:T(8,128)S(1)}, f32[128,1024]{1,0:T(8,128)S(1)}, u32[]{:S(2)}, u32[]{:S(2)}) collective-permute-start(f32[128,1024]{1,0:T(8,128)S(1)} %get-tuple-element.74.refs_1_.refs_4_), channel_id=1, source_target_pairs={{0,4},{8,0},{16,8},{24,16},{28,24},{20,28},{12,20},{4,12},{1,5},{9... | collective-permute-start | bytes 1572872 | tf_op jit(solution)/shard_map/ppermute | solution.py:1073
  79.7 7.1 %collective-permute-start.22 = (f32[512,1024]{1,0:T(8,128)S(1)}, f32[512,1024]{1,0:T(8,128)S(1)}, u32[]{:S(2)}, u32[]{:S(2)}) collective-permute-start(f32[512,1024]{1,0:T(8,128)S(1)} %get-tuple-element.75.n_ref.refs_1_), channel_id=1, source_target_pairs={{0,1},{1,0},{2,3},{3,2},{4,5},{5,4},{6,7},{7,6},{8,9},{9,8},{10,11... | collective-permute-start | bytes 6291464 | tf_op jit(solution)/shard_map/ppermute | solution.py:1049
  86.3 14.8 %collective-permute-start.25 = (f32[128,1024]{1,0:T(8,128)S(1)}, f32[128,1024]{1,0:T(8,128)S(1)}, u32[]{:S(2)}, u32[]{:S(2)}) collective-permute-start(f32[128,1024]{1,0:T(8,128)S(1)} %held.29), channel_id=1, source_target_pairs={{0,2},{1,3},{2,0},{3,1},{4,6},{5,7},{6,4},{7,5},{8,10},{9,11},{10,... | collective-permute-start | bytes 1572872 | tf_op jit(solution)/shard_map/ppermute | solution.py:1053
  86.8 14.3 %collective-permute-start.23 = (f32[128,1024]{1,0:T(8,128)}, f32[128,1024]{1,0:T(8,128)S(1)}, u32[]{:S(2)}, u32[]{:S(2)}) collective-permute-start(f32[128,1024]{1,0:T(8,128)} %get-tuple-element.82.refs_3_), channel_id=1, source_target_pairs={{0,8},{8,16},{16,24},{24,28},{28,20},{20,12},{12,4},{4,0},{1,9},{9... | collective-permute-start | bytes 1572872 | tf_op jit(solution)/shard_map/ppermute | solution.py:1073
  87.3 13.8 %collective-permute-start.24 = (f32[128,1024]{1,0:T(8,128)}, f32[128,1024]{1,0:T(8,128)S(1)}, u32[]{:S(2)}, u32[]{:S(2)}) collective-permute-start(f32[128,1024]{1,0:T(8,128)} %get-tuple-element.83.refs_4_), channel_id=1, source_target_pairs={{0,4},{8,0},{16,8},{24,16},{28,24},{20,28},{12,20},{4,12},{1,5},{9... | collective-permute-start | bytes 1572872 | tf_op jit(solution)/shard_map/ppermute | solution.py:1073
  88.9 19.4 %collective-permute-start.27 = (f32[3,128,256]{2,1,0:T(8,128)S(1)}, f32[3,128,256]{2,1,0:T(8,128)S(1)}, u32[]{:S(2)}, u32[]{:S(2)}) collective-permute-start(f32[3,128,256]{2,1,0:T(8,128)S(1)} %held.30), channel_id=1, source_target_pairs={{0,2},{1,3},{2,0},{3,1},{4,6},{5,7},{6,4},{7,5},{8,10},{9,11},{10,... | collective-permute-start | bytes 1179656 | tf_op jit(solution)/shard_map/ppermute | solution.py:1053
  108.2 11.6 %collective-permute-start.29 = (f32[3,128,256]{2,1,0:T(8,128)S(1)}, f32[3,128,256]{2,1,0:T(8,128)S(1)}, u32[]{:S(2)}, u32[]{:S(2)}) collective-permute-start(f32[3,128,256]{2,1,0:T(8,128)S(1)} %held.31.refs_0_), channel_id=1, source_target_pairs={{0,4},{8,0},{16,8},{24,16},{28,24},{20,28},{12,20},{4,12},{1,5},{9... | collective-permute-start | bytes 1179656 | tf_op jit(solution)/shard_map/ppermute | solution.py:1073
  109.8 10.0 %collective-permute-start.28 = (f32[3,128,256]{2,1,0:T(8,128)S(1)}, f32[3,128,256]{2,1,0:T(8,128)S(1)}, u32[]{:S(2)}, u32[]{:S(2)}) collective-permute-start(f32[3,128,256]{2,1,0:T(8,128)S(1)} %held.31.refs_0_), channel_id=1, source_target_pairs={{0,8},{8,16},{16,24},{24,28},{28,20},{20,12},{12,4},{4,0},{1,9},{9... | collective-permute-start | bytes 1179656 | tf_op jit(solution)/shard_map/ppermute | solution.py:1073
  110.2 9.5 %collective-permute-start.31 = (f32[3,128,256]{2,1,0:T(8,128)S(1)}, f32[3,128,256]{2,1,0:T(8,128)S(1)}, u32[]{:S(2)}, u32[]{:S(2)}) collective-permute-start(f32[3,128,256]{2,1,0:T(8,128)S(1)} %held.33), channel_id=1, source_target_pairs={{0,2},{1,3},{2,0},{3,1},{4,6},{5,7},{6,4},{7,5},{8,10},{9,11},{10,... | collective-permute-start | bytes 1179656 | tf_op jit(solution)/shard_map/ppermute | solution.py:1053
  110.7 9.0 %collective-permute-start.26 = (f32[512,1024]{1,0:T(8,128)S(1)}, f32[512,1024]{1,0:T(8,128)S(1)}, u32[]{:S(2)}, u32[]{:S(2)}) collective-permute-start(f32[512,1024]{1,0:T(8,128)S(1)} %get-tuple-element.88.refs_2_), channel_id=1, source_target_pairs={{0,1},{1,0},{2,3},{3,2},{4,5},{5,4},{6,7},{7,6},{8,9},{9,8},{10,11... | collective-permute-start | bytes 6291464 | tf_op jit(solution)/shard_map/ppermute | solution.py:1049
  110.7 7.2 %collective-permute-start.30 = (f32[512,1024]{1,0:T(8,128)S(1)}, f32[512,1024]{1,0:T(8,128)S(1)}, u32[]{:S(2)}, u32[]{:S(2)}) collective-permute-start(f32[512,1024]{1,0:T(8,128)S(1)} %get-tuple-element.92), channel_id=1, source_target_pairs={{0,1},{1,0},{2,3},{3,2},{4,5},{5,4},{6,7},{7,6},{8,9},{9,8},{10,11... | collective-permute-start | bytes 6291464 | tf_op jit(solution)/shard_map/ppermute | solution.py:1049
  119.6 6.0 %collective-permute-start.33 = (f32[512,1024]{1,0:T(8,128)S(1)}, f32[512,1024]{1,0:T(8,128)S(1)}, u32[]{:S(2)}, u32[]{:S(2)}) collective-permute-start(f32[512,1024]{1,0:T(8,128)S(1)} %norm_two_back.1.refs_2_.keep_ref.refs_1_.upper_ref), channel_id=1, source_target_pairs={{0,1},{1,0},{2,3},{3,2},{4,5},{5,4},{6,7},{7,6},{8,9},{9,8},{10,11... | collective-permute-start | bytes 6291464 | tf_op jit(solution)/shard_map/ppermute | solution.py:1049
  121.5 18.8 %collective-permute-start.32 = (f32[512,1024]{1,0:T(8,128)S(1)}, f32[512,1024]{1,0:T(8,128)S(1)}, u32[]{:S(2)}, u32[]{:S(2)}) collective-permute-start(f32[512,1024]{1,0:T(8,128)S(1)} %get-tuple-element.96), channel_id=1, source_target_pairs={{0,1},{1,0},{2,3},{3,2},{4,5},{5,4},{6,7},{7,6},{8,9},{9,8},{10,11... | collective-permute-start | bytes 6291464 | tf_op jit(solution)/shard_map/ppermute | solution.py:1049
  121.9 20.0 %collective-permute-start.36 = (f32[6,128,256]{2,1,0:T(8,128)S(1)}, f32[6,128,256]{2,1,0:T(8,128)S(1)}, u32[]{:S(2)}, u32[]{:S(2)}) collective-permute-start(f32[6,128,256]{2,1,0:T(8,128)S(1)} %held.34), channel_id=1, source_target_pairs={{0,2},{1,3},{2,0},{3,1},{4,6},{5,7},{6,4},{7,5},{8,10},{9,11},{10,... | collective-permute-start | bytes 2359304 | tf_op jit(solution)/shard_map/ppermute | solution.py:1053
  123.4 14.6 %collective-permute-start.34 = (f32[3,128,256]{2,1,0:T(8,128)S(1)}, f32[3,128,256]{2,1,0:T(8,128)S(1)}, u32[]{:S(2)}, u32[]{:S(2)}) collective-permute-start(f32[3,128,256]{2,1,0:T(8,128)S(1)} %get-tuple-element.93.refs_0_.refs_1_), channel_id=1, source_target_pairs={{0,8},{8,16},{16,24},{24,28},{28,20},{20,12},{12,4},{4,0},{1,9},{9... | collective-permute-start | bytes 1179656 | tf_op jit(solution)/shard_map/ppermute | solution.py:1073
  123.9 14.2 %collective-permute-start.35 = (f32[3,128,256]{2,1,0:T(8,128)S(1)}, f32[3,128,256]{2,1,0:T(8,128)S(1)}, u32[]{:S(2)}, u32[]{:S(2)}) collective-permute-start(f32[3,128,256]{2,1,0:T(8,128)S(1)} %get-tuple-element.94.refs_1_.refs_2_), channel_id=1, source_target_pairs={{0,4},{8,0},{16,8},{24,16},{28,24},{20,28},{12,20},{4,12},{1,5},{9... | collective-permute-start | bytes 1179656 | tf_op jit(solution)/shard_map/ppermute | solution.py:1073
  138.6 1.2 collective-permute-start.37
  139.8 6.1 %collective-permute-start.38 = (f32[16,512]{1,0:T(8,128)S(1)}, f32[16,512]{1,0:T(8,128)S(1)}, u32[]{:S(2)}, u32[]{:S(2)}) collective-permute-start(f32[16,512]{1,0:T(8,128)S(1)} %add.93.refs_0_), channel_id=1, source_target_pairs={{0,2},{1,3},{2,0},{3,1},{4,6},{5,7},{6,4},{7,5},{8,10},{9,11},{10,... | collective-permute-start | bytes 98312 | tf_op jit(solution)/shard_map/ppermute | solution.py:1058
  146.0 11.7 %collective-permute-start.39 = (f32[16,1024]{1,0:T(8,128)S(1)}, f32[16,1024]{1,0:T(8,128)S(1)}, u32[]{:S(2)}, u32[]{:S(2)}) collective-permute-start(f32[16,1024]{1,0:T(8,128)S(1)} %held.36), channel_id=1, source_target_pairs={{0,16},{4,20},{8,24},{12,28},{16,0},{20,4},{24,8},{28,12},{1,17},{... | collective-permute-start | bytes 196616 | tf_op jit(solution)/shard_map/ppermute | solution.py:1058
  157.8 4.3 %collective-permute-start.40 = (f32[16,1024]{1,0:T(8,128)S(1)}, f32[16,1024]{1,0:T(8,128)S(1)}, u32[]{:S(2)}, u32[]{:S(2)}) collective-permute-start(f32[16,1024]{1,0:T(8,128)S(1)} %held.37.refs_4_), channel_id=1, source_target_pairs={{0,8},{4,12},{8,0},{12,4},{16,24},{20,28},{24,16},{28,20},{1,9},{5... | collective-permute-start | bytes 196616 | tf_op jit(solution)/shard_map/ppermute | solution.py:1058
  161.2 5.4 %collective-permute-start.42 = (f32[512,1024]{1,0:T(8,128)S(1)}, f32[512,1024]{1,0:T(8,128)S(1)}, u32[]{:S(2)}, u32[]{:S(2)}) collective-permute-start(f32[512,1024]{1,0:T(8,128)S(1)} %unproject.2.refs_4_.a_ref), channel_id=1, source_target_pairs={{0,1},{1,0},{2,3},{3,2},{4,5},{5,4},{6,7},{7,6},{8,9},{9,8},{10,11... | collective-permute-start | bytes 6291464 | tf_op jit(solution)/shard_map/ppermute | solution.py:1049
  164.2 7.5 %collective-permute-start.41 = (f32[512,1024]{1,0:T(8,128)S(1)}, f32[512,1024]{1,0:T(8,128)S(1)}, u32[]{:S(2)}, u32[]{:S(2)}) collective-permute-start(f32[512,1024]{1,0:T(8,128)S(1)} %unproject.3.a_ref), channel_id=1, source_target_pairs={{0,1},{1,0},{2,3},{3,2},{4,5},{5,4},{6,7},{7,6},{8,9},{9,8},{10,11... | collective-permute-start | bytes 6291464 | tf_op jit(solution)/shard_map/ppermute | solution.py:1049
  164.3 5.2 %collective-permute-start.43 = (f32[16,1024]{1,0:T(8,128)S(1)}, f32[16,1024]{1,0:T(8,128)S(1)}, u32[]{:S(2)}, u32[]{:S(2)}) collective-permute-start(f32[16,1024]{1,0:T(8,128)S(1)} %add.96.refs_5_.a_ref), channel_id=1, source_target_pairs={{0,4},{4,0},{8,12},{12,8},{16,20},{20,16},{24,28},{28,24},{1,5},{5... | collective-permute-start | bytes 196616 | tf_op jit(solution)/shard_map/ppermute | solution.py:1306
  (55 other events, 253.9 us)
